TPU v7x, 256 devices: a whole 4x4x8 slice. The times are simulated.
256 devices in a mesh: dp: 16 (over z, core), expert: 16 (over x, y).
Axes of the slice: x: 4, y: 4, z: 8, core: 2. Of those that a mesh axis runs over, the one named last changes fastest.
Arguments:
- tokens_in: bfloat16 [16, 4096, 2048], P('expert', 'dp'), may hold values from -6 to 6
- out_grads: bfloat16 [16, 4096, 768], P('expert', 'dp'), may hold values from -6 to 6
- counts: int32 [16, 16, 2], P('expert', 'dp'), may hold values from 32 to 128, as said below
- copy_list: int32 [16], replicated, may hold values from 0 to 15, as said below
- weights: bfloat16 [16, 2048, 768], P('expert', 'dp'), may hold values from -0.125 to 0.125
- momentum: float32 [16, 2048, 768], P('expert', 'dp'), may hold values from -1920 to 1920
Outputs:
- new_momentum: float32 [16, 2048, 768], P('expert', 'dp')
- home_update: float32 [16, 2048, 768], P('expert', 'dp')
- replica_weight: bfloat16 [16, 2048, 768], P('expert')
Inputs may be any that keep to these rules, and one draw needn't show every extreme that they name: Each count lies between 32 and 128; both ends are taken by some device in every draw; slots past the two counts are padding. copy_list[j] is never j; an expert may sit in several copy slots.
All inputs are finite; a program needn't handle non-finite values.
Results may differ from a plain program's by a relative error of at most 0.011.
Values may be sent and summed in bfloat16 or wider, within the bound.
No kernel may reach another device: no remote copies, remote signals or barrier semaphores. Data moves between devices by JAX's collectives and lax.ppermute only.
A program may use at most 64 MiB of HBM per device.

v0:
```python
import functools
import math

import jax
import jax.numpy as jnp
from jax import lax
from jax.experimental import pallas as pl
from jax.experimental.pallas import tpu as pltpu
from jax.sharding import Mesh, PartitionSpec as P

coef_a = 3.4445
coef_b = -4.775
coef_c = 2.0315
beta_mom = 0.95
learn_rate = 0.02
norm_eps = 1e-07

NZ, NC, NX, NY = 8, 2, 4, 4
BF = jnp.bfloat16
F32 = jnp.float32


def swap(value):
    return lax.ppermute(value, "core", [(0, 1), (1, 0)])


def up(value):
    return lax.ppermute(value, "z", [(i, (i + 1) % NZ) for i in range(NZ)])


def down(value):
    return lax.ppermute(value, "z", [((i + 1) % NZ, i) for i in range(NZ)])


def shift(value, axis, offset):
    return lax.ppermute(value, axis, [(i, (i + offset) % 4) for i in range(4)])


def add_bf(left, right):
    return (left.astype(F32) + right.astype(F32)).astype(BF)


SMEM = pl.BlockSpec(memory_space=pltpu.SMEM)
VMEM = pl.BlockSpec(memory_space=pltpu.VMEM)
ANY = pl.BlockSpec(memory_space=pl.ANY)
HBM = pl.BlockSpec(memory_space=pltpu.HBM)


def small(limit=8):
    return pltpu.CompilerParams(vmem_limit_bytes=limit * 1024 * 1024)


def place_kernel(side, here_ref, blocks_ref, *refs):
    out_ref, sems = refs[-2:]
    rows = blocks_ref.shape[0] // NZ
    z, core = here_ref[0], here_ref[1]
    parity = 1 - core if side else core
    copies = []
    for index in range(NZ):
        there = NC * lax.rem(z + index + NZ // 2, NZ) + parity
        copies.append(
            pltpu.make_async_copy(
                blocks_ref.at[pl.ds(index * rows, rows), :],
                out_ref.at[pl.ds(pl.multiple_of(there * rows, rows), rows), :],
                sems.at[index],
            )
        )
    for copy in copies:
        copy.start()
    for copy in copies:
        copy.wait()


def place(side, here, blocks, before=None):
    return pl.pallas_call(
        functools.partial(place_kernel, side),
        out_shape=jax.ShapeDtypeStruct((NC * blocks.shape[0], blocks.shape[1]), blocks.dtype),
        in_specs=[SMEM, VMEM] + ([] if before is None else [ANY]),
        out_specs=ANY,
        scratch_shapes=[pltpu.SemaphoreType.DMA((NZ,))],
        input_output_aliases={} if before is None else {2: 0},
        compiler_params=small(),
        name="place",
    )(here, blocks, *([] if before is None else [before]))


def bucket_kernel(here_ref, list_ref, *refs):
    pieces, outs = refs[:NY], refs[NY:]
    x, y = here_ref[2], here_ref[3]
    totals = [jnp.zeros(outs[0].shape, F32) for _ in range(NX)]
    for offset, piece in enumerate(pieces):
        target = list_ref[x * NY + lax.rem(y + NY - offset, NY)]
        value = piece[...].astype(F32)
        for ahead in range(NX):
            fits = target == lax.rem(x + ahead, NX) * NY + y
            totals[ahead] = totals[ahead] + jnp.where(fits, value, 0.0)
    for out, total in zip(outs, totals, strict=True):
        out[...] = total.astype(out.dtype)


def buckets(here, copy_list, pieces):
    shape = pieces[0].shape
    return pl.pallas_call(
        bucket_kernel,
        out_shape=tuple(jax.ShapeDtypeStruct(shape, BF if k else F32) for k in range(NX)),
        in_specs=[SMEM, SMEM] + [VMEM] * NY,
        out_specs=(VMEM,) * NX,
        compiler_params=small(),
        name="buckets",
    )(here, copy_list, *pieces)


def wanted_kernel(here_ref, list_ref, *refs):
    pieces, outs = refs[:NX], refs[NX:]
    x, y = here_ref[2], here_ref[3]
    for offset, out in enumerate(outs):
        source = list_ref[x * NY + lax.rem(y + offset, NY)]
        behind = lax.rem(x + NX - lax.div(source, NY), NX)
        for k, piece in enumerate(pieces):

            @pl.when(behind == k)
            def _():
                out[...] = piece[...]


def wanted(here, copy_list, pieces):
    shape = pieces[0].shape
    return pl.pallas_call(
        wanted_kernel,
        out_shape=(jax.ShapeDtypeStruct(shape, BF),) * NY,
        in_specs=[SMEM, SMEM] + [VMEM] * NX,
        out_specs=(VMEM,) * NY,
        compiler_params=small(),
        name="wanted",
    )(here, copy_list, *pieces)


def pick_kernel(here_ref, list_ref, *refs):
    pieces, out = refs[:NY], refs[NY]
    x, y = here_ref[2], here_ref[3]
    behind = lax.rem(y + NY - lax.rem(list_ref[x * NY + y], NY), NY)
    for k, piece in enumerate(pieces):

        @pl.when(behind == k)
        def _():
            out[...] = piece[...]


def pick(here, copy_list, pieces):
    return pl.pallas_call(
        pick_kernel,
        out_shape=jax.ShapeDtypeStruct(pieces[0].shape, BF),
        in_specs=[SMEM, SMEM] + [VMEM] * NY,
        out_specs=VMEM,
        compiler_params=small(),
        name="pick",
    )(here, copy_list, *pieces)


CHUNK = 64


def terms_kernel(
    offsets, here_ref, counts_ref, got_counts_ref, acts_ref, got_ref, grads_ref, got_grads_ref, *out_refs
):
    tok_rows, width = grads_ref.shape
    rows = acts_ref.shape[1] // (NZ * NC)
    z, core = here_ref[0], here_ref[1]
    starts = [
        pl.multiple_of((NC * lax.rem(z + NZ + offset, NZ) + core) * rows, rows) for offset in offsets
    ]
    slot = lax.broadcasted_iota(jnp.int32, (tok_rows, width), 0)
    totals = [None, None]
    for acts, grads, counts in (
        (acts_ref, grads_ref, counts_ref),
        (got_ref, got_grads_ref, got_counts_ref),
    ):
        home, copy = counts[0, 0], counts[0, 1]
        left = jnp.concatenate([acts[:, pl.ds(start, rows)] for start in starts], axis=1)
        value = grads[...].astype(F32)
        for which, (low, high) in enumerate(((home, home + copy), (0, home))):
            right = jnp.where((slot >= low) & (slot < high), value, 0.0).astype(BF)
            part = lax.dot_general(
                left, right, (((0,), (0,)), ((), ())), preferred_element_type=F32
            )
            totals[which] = part if totals[which] is None else totals[which] + part
    for index, out_ref in enumerate(out_refs):
        span = slice(index * rows, (index + 1) * rows)
        out_ref[:rows] = totals[0][span].astype(BF)
        out_ref[rows:] = totals[1][span].astype(BF)


def terms(here, counts, got_counts, acts, got, grads, got_grads, offsets):
    tok_rows, width = grads.shape
    rows = acts.shape[1] // (NZ * NC)
    return pl.pallas_call(
        functools.partial(terms_kernel, offsets),
        out_shape=(jax.ShapeDtypeStruct((2 * rows, width), BF),) * len(offsets),
        in_specs=[SMEM] * 3 + [VMEM] * 4,
        out_specs=(VMEM,) * len(offsets),
        compiler_params=small(20),
        cost_estimate=pl.CostEstimate(
            flops=8 * tok_rows * rows * len(offsets) * width,
            bytes_accessed=4 * tok_rows * rows * NZ,
            transcendentals=0,
        ),
        name="terms",
    )(here, counts, got_counts, acts, got, grads, got_grads)


def halves(value):
    high = value.astype(BF)
    return high, (value - high.astype(F32)).astype(BF)


def dot(left, right):
    return jnp.dot(left, right, preferred_element_type=F32)


def newton_kernel(
    factor,
    gram_ref,
    other_ref,
    mom_ref,
    weight_ref,
    update_ref,
    fresh_ref,
    s_hi,
    s_lo,
    k_hi,
    k_lo,
    t_hi,
    t_lo,
    iterate_ref,
    full_ref,
):
    width = gram_ref.shape[0]
    tile = width // 3
    spans = [slice(i * tile, (i + 1) * tile) for i in range(3)]
    pairs = [(i, j) for i in range(3) for j in range(i, 3)]

    def store(hi, lo, i, j, value):
        hi[spans[i], spans[j]], lo[spans[i], spans[j]] = halves(value)
        if i != j:
            hi[spans[j], spans[i]], lo[spans[j], spans[i]] = halves(value.T)

    def load(hi, lo, i, j):
        return hi[spans[i], spans[j]].astype(F32) + lo[spans[i], spans[j]].astype(F32)

    def product(left, right, i, j):
        (l_hi, l_lo), (r_hi, r_lo) = left, right
        rows, cols = spans[i], spans[j]
        out = dot(l_hi[rows, :], r_lo[:, cols]) + dot(l_lo[rows, :], r_hi[:, cols])
        return out + dot(l_hi[rows, :], r_hi[:, cols])

    def times(value, right):
        hi, lo = halves(value)
        r_hi, r_lo = right
        both = dot(jnp.concatenate([hi, lo], axis=0), r_hi[...])
        rows = value.shape[0]
        return both[:rows] + (both[rows:] + dot(hi, r_lo[...]))

    same = lax.broadcasted_iota(jnp.int32, (tile, tile), 0) == lax.broadcasted_iota(
        jnp.int32, (tile, tile), 1
    )
    total = jnp.zeros((1, 1), F32)
    for span in spans:
        value = gram_ref[span, :] + lax.dot_general(
            other_ref[:, span],
            other_ref[...],
            (((0,), (0,)), ((), ())),
            preferred_element_type=F32,
        )
        full_ref[span, :] = value
        on = jnp.where(same, value[:, span], 0.0)
        total = total + jnp.sum(jnp.sum(on, axis=1, keepdims=True), axis=0, keepdims=True)
    scale = 1.0 / (jnp.sqrt(total) + norm_eps)

    @pl.loop(0, width // CHUNK)
    def _(index):
        chunk = pl.ds(pl.multiple_of(index * CHUNK, CHUNK), CHUNK)
        s_hi[chunk, :], s_lo[chunk, :] = halves(full_ref[chunk, :] * scale * scale)

    iterate_ref[...] = mom_ref[...] * scale
    s, k, t = (s_hi, s_lo), (k_hi, k_lo), (t_hi, t_lo)

    @pl.loop(0, 2)
    def _(step):
        for i, j in pairs:
            store(*k, i, j, coef_b * load(*s, i, j) + coef_c * product(s, s, i, j))
        iterate_ref[...] = coef_a * iterate_ref[...] + times(iterate_ref[...], k)
        for i, j in pairs:
            store(*t, i, j, coef_a * load(*s, i, j) + product(s, k, i, j))
        for i, j in pairs:
            store(*s, i, j, coef_a * load(*t, i, j) + product(t, k, i, j))

    iterate = iterate_ref[...]
    side = times(iterate, s)
    iterate = coef_a * iterate + (coef_b * side + coef_c * times(side, s))
    update = factor * iterate
    update_ref[...] = update
    fresh_ref[...] = (weight_ref[...].astype(F32) - learn_rate * update).astype(BF)


def newton_schulz(gram, other, mom, weight, longest):
    rows, width = mom.shape
    vmem = pl.BlockSpec(memory_space=pltpu.VMEM)
    return pl.pallas_call(
        functools.partial(newton_kernel, 0.2 * math.sqrt(longest)),
        out_shape=(
            jax.ShapeDtypeStruct((rows, width), F32),
            jax.ShapeDtypeStruct((rows, width), BF),
        ),
        in_specs=[vmem] * 4,
        out_specs=(vmem, vmem),
        scratch_shapes=[pltpu.VMEM((width, width), BF)] * 6
        + [pltpu.VMEM((rows, width), F32), pltpu.VMEM((width, width), F32)],
        compiler_params=small(20),
        cost_estimate=pl.CostEstimate(
            flops=28 * width**3, bytes_accessed=8 * width * width, transcendentals=0
        ),
        name="newton_schulz",
    )(gram, other, mom, weight)


def after(value, *others):
    return lax.optimization_barrier((value, *others))


def ring_sum(far, near):
    rows = far.shape[0] // 2
    up3, up2, up1, mine, down1, down2, down3 = near
    copies, homes = up(far[:rows]), down(far[rows:])
    below = jnp.concatenate([add_bf(up3[:rows], copies), up3[rows:]], axis=0)
    above = jnp.concatenate([down3[:rows], add_bf(down3[rows:], homes)], axis=0)
    on_up = jnp.stack([up2, up1, mine])
    on_down = jnp.stack([down2, down1, jnp.zeros_like(mine)])

    def one(step, carry):
        below, above = carry
        below, above = up(below), down(above)
        return add_bf(below, on_up[step]), add_bf(above, on_down[step])

    return lax.fori_loop(0, 3, one, (below, above))


def ring(block):
    rows, width = block.shape

    def one(step, carry):
        below, above, got = carry
        got = lax.dynamic_update_slice(got, below, ((4 - step) * rows, 0))
        got = lax.dynamic_update_slice(got, above, ((4 + step) * rows, 0))
        return up(below), down(above), got

    got = jnp.zeros((NZ * rows, width), block.dtype)
    far, _, got = lax.fori_loop(0, 4, one, (block, block, got))
    return lax.dynamic_update_slice(got, far, (0, 0))


def body(tokens_in, out_grads, counts, copy_list, weights, momentum):
    acts = tokens_in[0]
    grads = out_grads[0]
    model_width = acts.shape[1]
    width = grads.shape[1]
    here = jnp.stack([lax.axis_index(name) for name in ("z", "core", "x", "y")]).astype(jnp.int32)

    tokens = (counts[0], swap(counts[0]), acts, swap(acts), grads, swap(grads))
    (far,) = terms(here, *tokens, (4,))
    near = terms(here, *tokens, (3, 2, 1, 0, -1, -2, -3))
    below, above = ring_sum(far, near)
    rows = below.shape[0] // 2
    total = below.astype(F32) + above.astype(F32)
    copy_sum, home_sum = total[:rows].astype(BF), total[rows:]

    pieces = {offset: shift(copy_sum, "y", offset) for offset in (2, 1, 3)}
    pieces = [copy_sum] + [pieces[offset] for offset in range(1, NY)]
    copies, *sent = buckets(here, copy_list, pieces)
    for ahead in (2, 1, 3):
        copies = copies + shift(sent[ahead - 1], "x", ahead).astype(F32)
    fresh_mom = beta_mom * momentum[0] + (home_sum + copies)

    own = ring(fresh_mom.astype(BF))
    gram = lax.dot_general(own, own, (((0,), (0,)), ((), ())), preferred_element_type=F32)
    update, fresh = newton_schulz(
        gram, swap(own), fresh_mom, weights[0], max(model_width, width)
    )

    pieces = {offset: shift(fresh, "x", offset) for offset in (2, 1, 3)}
    pieces = [fresh] + [pieces[offset] for offset in range(1, NX)]
    kept, *sent = wanted(here, copy_list, pieces)
    pieces = {offset: shift(sent[offset - 1], "y", offset) for offset in (2, 1, 3)}
    pieces = [kept] + [pieces[offset] for offset in range(1, NY)]
    replica = pick(here, copy_list, pieces)

    own = ring(replica)
    full = place(1, here, swap(own), place(0, here, own))
    return (fresh_mom[None], update[None], full[None])


def solution(mesh):
    grid = Mesh(mesh.devices.reshape(NZ, NC, NX, NY), ("z", "core", "x", "y"))
    split = P(("x", "y"), ("z", "core"), None)
    return jax.shard_map(
        body,
        mesh=grid,
        in_specs=(split, split, split, P(), split, split),
        out_specs=(split, split, P(("x", "y"), None, None)),
        check_vma=False,
    )
```

profile of v0, /device:TPU:1, one launch (start us, length us, event | category | flops | bytes accessed | tf_op | source)
XLA Modules:
  0.0 198.7 jit_solution(11698964220335340912)
XLA Ops:
  0.6 3.3 %collective-permute-start.7 = (bf16[256,2048]{1,0:T(8,128)(2,1)}, bf16[256,2048]{1,0:T(8,128)(2,1)S(1)}, u32[]{:S(2)}, u32[]{:S(2)}) collective-permute-start(bf16[256,2048]{1,0:T(8,128)(2,1)} %bitcast.32), channel_id=1, source_target_pairs={{0,16},{16,0},{1,17},{17,1},{2,18},{18,2},{3,19},{19,3},{4,20},{20... | collective-permute-start | bytes 3145736 | tf_op jit(solution)/shard_map/ppermute | solution.py:24
  4.6 2.4 %collective-permute-done.6.got_counts_ref = s32[1,2]{1,0:T(1,128)S(1)} collective-permute-done((s32[1,2]{1,0:T(1,128)}, s32[1,2]{1,0:T(1,128)S(1)}, u32[]{:S(2)}, u32[]{:S(2)}) %collective-permute-start.6) | collective-permute-done | bytes 40 | tf_op jit(solution)/shard_map/ppermute | solution.py:24
  10.9 3.9 %collective-permute-start.10 = (bf16[128,768]{1,0:T(8,128)(2,1)S(1)}, bf16[128,768]{1,0:T(8,128)(2,1)S(1)}, u32[]{:S(2)}, u32[]{:S(2)}) collective-permute-start(bf16[128,768]{1,0:T(8,128)(2,1)S(1)} %get-tuple-element.326), channel_id=1, source_target_pairs={{32,0},{64,32},{96,64},{128,96},{160,128},{192,160},{224,192},{0,2... | collective-permute-start | bytes 589832 | tf_op jit(solution)/shard_map/ppermute | solution.py:32
  17.4 4.5 %collective-permute-done.9 = bf16[128,768]{1,0:T(8,128)(2,1)S(1)} collective-permute-done((bf16[128,768]{1,0:T(8,128)(2,1)S(1)}, bf16[128,768]{1,0:T(8,128)(2,1)S(1)}, u32[]{:S(2)}, u32[]{:S(2)}) %collective-permute-start.9) | collective-permute-done | bytes 196640 | tf_op jit(solution)/shard_map/ppermute | solution.py:28
  22.8 31.7 %while.49 = (s32[]{:T(128)}, bf16[256,768]{1,0:T(8,128)(2,1)S(1)}, bf16[256,768]{1,0:T(8,128)(2,1)}, bf16[3,256,768]{2,1,0:T(8,128)(2,1)S(1)}, bf16[3,256,768]{2,1,0:T(8,128)(2,1)S(1)}, /*index=5*/s32[]{:T(128)}) while((s32[]{:T(128)}, bf16[256,768]{1,0:T(8,128)(2,1)S(1)}, bf16[256,768]{1,0:T(8,128)(2,1)}, bf16[3,256,768]{2,1,0:T(8,128)(2,1)S(1)}, ...), condition=%wide.region_1.0_spmd, body=%wide.region_0.0_spmd.sunk | while | flops 1572866 | bytes 5505189 | solution.py:344
  24.3 7.8 %collective-permute-done.1 = bf16[256,768]{1,0:T(8,128)(2,1)S(1)} collective-permute-done((bf16[256,768]{1,0:T(8,128)(2,1)}, bf16[256,768]{1,0:T(8,128)(2,1)S(1)}, u32[]{:S(2)}, u32[]{:S(2)}) %collective-permute-start.1) | collective-permute-done | bytes 393248 | tf_op jit(solution)/shard_map/while/body/eval_jaxpr/ppermute | solution.py:32
  35.0 7.0 %collective-permute-done.1 = bf16[256,768]{1,0:T(8,128)(2,1)S(1)} collective-permute-done((bf16[256,768]{1,0:T(8,128)(2,1)}, bf16[256,768]{1,0:T(8,128)(2,1)S(1)}, u32[]{:S(2)}, u32[]{:S(2)}) %collective-permute-start.1) | collective-permute-done | bytes 393248 | tf_op jit(solution)/shard_map/while/body/eval_jaxpr/ppermute | solution.py:32
  46.0 6.0 %collective-permute-done.1 = bf16[256,768]{1,0:T(8,128)(2,1)S(1)} collective-permute-done((bf16[256,768]{1,0:T(8,128)(2,1)}, bf16[256,768]{1,0:T(8,128)(2,1)S(1)}, u32[]{:S(2)}, u32[]{:S(2)}) %collective-permute-start.1) | collective-permute-done | bytes 393248 | tf_op jit(solution)/shard_map/while/body/eval_jaxpr/ppermute | solution.py:32
  55.7 2.7 %collective-permute-start.13 = (bf16[128,768]{1,0:T(8,128)(2,1)S(1)}, bf16[128,768]{1,0:T(8,128)(2,1)S(1)}, u32[]{:S(2)}, u32[]{:S(2)}) collective-permute-start(bf16[128,768]{1,0:T(8,128)(2,1)S(1)} %slice.43.refs_0_), channel_id=1, source_target_pairs={{0,3},{1,0},{2,1},{3,2},{4,7},{5,4},{6,5},{7,6},{8,11},{9,8},{10,9... | collective-permute-start | bytes 589832 | tf_op jit(solution)/shard_map/ppermute | solution.py:36
  59.5 3.7 %collective-permute-done.13.refs_3_ = bf16[128,768]{1,0:T(8,128)(2,1)S(1)} collective-permute-done((bf16[128,768]{1,0:T(8,128)(2,1)S(1)}, bf16[128,768]{1,0:T(8,128)(2,1)S(1)}, u32[]{:S(2)}, u32[]{:S(2)}) %collective-permute-start.13) | collective-permute-done | bytes 196640 | tf_op jit(solution)/shard_map/ppermute | solution.py:36
  67.5 2.8 %collective-permute-start.14 = (bf16[128,768]{1,0:T(8,128)(2,1)S(1)}, bf16[128,768]{1,0:T(8,128)(2,1)S(1)}, u32[]{:S(2)}, u32[]{:S(2)}) collective-permute-start(bf16[128,768]{1,0:T(8,128)(2,1)S(1)} %get-tuple-element.285), channel_id=1, source_target_pairs={{0,8},{4,12},{8,0},{12,4},{1,9},{5,13},{9,1},{13,5},{2,10},{6,14},... | collective-permute-start | bytes 589832 | tf_op jit(solution)/shard_map/ppermute | solution.py:36
  73.7 2.4 %collective-permute-done.15 = bf16[128,768]{1,0:T(8,128)(2,1)S(1)} collective-permute-done((bf16[128,768]{1,0:T(8,128)(2,1)S(1)}, bf16[128,768]{1,0:T(8,128)(2,1)S(1)}, u32[]{:S(2)}, u32[]{:S(2)}) %collective-permute-start.15) | collective-permute-done | bytes 196640 | tf_op jit(solution)/shard_map/ppermute | solution.py:36
  76.4 27.1 %while.50 = (s32[]{:T(128)}, bf16[128,768]{1,0:T(8,128)(2,1)S(1)}, bf16[128,768]{1,0:T(8,128)(2,1)S(1)}, bf16[1024,768]{1,0:T(8,128)(2,1)S(1)}, s32[]{:T(128)}, ...) while((s32[]{:T(128)}, bf16[128,768]{1,0:T(8,128)(2,1)S(1)}, bf16[128,768]{1,0:T(8,128)(2,1)S(1)}, ...), condition=%wide.region_3.0_spmd, body=%wide.region_2.0_spmd.sunk | while | flops 12 | bytes 3146025 | solution.py:357
  76.5 2.7 %collective-permute-start.3 = (bf16[128,768]{1,0:T(8,128)(2,1)S(1)}, bf16[128,768]{1,0:T(8,128)(2,1)S(1)}, u32[]{:S(2)}, u32[]{:S(2)}) collective-permute-start(bf16[128,768]{1,0:T(8,128)(2,1)S(1)} %copy.29), channel_id=1, source_target_pairs={{32,0},{64,32},{96,64},{128,96},{160,128},{192,160},{224,192},{0,2... | collective-permute-start | bytes 589832 | tf_op jit(solution)/shard_map/while/body/eval_jaxpr/ppermute | solution.py:32
  79.3 3.2 %collective-permute-done.2 = bf16[128,768]{1,0:T(8,128)(2,1)S(1)} collective-permute-done((bf16[128,768]{1,0:T(8,128)(2,1)S(1)}, bf16[128,768]{1,0:T(8,128)(2,1)S(1)}, u32[]{:S(2)}, u32[]{:S(2)}) %collective-permute-start.2) | collective-permute-done | bytes 196640 | tf_op jit(solution)/shard_map/while/body/eval_jaxpr/ppermute | solution.py:28
  82.7 2.7 %collective-permute-start.3 = (bf16[128,768]{1,0:T(8,128)(2,1)S(1)}, bf16[128,768]{1,0:T(8,128)(2,1)S(1)}, u32[]{:S(2)}, u32[]{:S(2)}) collective-permute-start(bf16[128,768]{1,0:T(8,128)(2,1)S(1)} %copy.29), channel_id=1, source_target_pairs={{32,0},{64,32},{96,64},{128,96},{160,128},{192,160},{224,192},{0,2... | collective-permute-start | bytes 589832 | tf_op jit(solution)/shard_map/while/body/eval_jaxpr/ppermute | solution.py:32
  85.4 3.8 %collective-permute-done.2 = bf16[128,768]{1,0:T(8,128)(2,1)S(1)} collective-permute-done((bf16[128,768]{1,0:T(8,128)(2,1)S(1)}, bf16[128,768]{1,0:T(8,128)(2,1)S(1)}, u32[]{:S(2)}, u32[]{:S(2)}) %collective-permute-start.2) | collective-permute-done | bytes 196640 | tf_op jit(solution)/shard_map/while/body/eval_jaxpr/ppermute | solution.py:28
  92.2 2.9 %collective-permute-done.2 = bf16[128,768]{1,0:T(8,128)(2,1)S(1)} collective-permute-done((bf16[128,768]{1,0:T(8,128)(2,1)S(1)}, bf16[128,768]{1,0:T(8,128)(2,1)S(1)}, u32[]{:S(2)}, u32[]{:S(2)}) %collective-permute-start.2) | collective-permute-done | bytes 196640 | tf_op jit(solution)/shard_map/while/body/eval_jaxpr/ppermute | solution.py:28
  100.0 3.5 %collective-permute-done.2 = bf16[128,768]{1,0:T(8,128)(2,1)S(1)} collective-permute-done((bf16[128,768]{1,0:T(8,128)(2,1)S(1)}, bf16[128,768]{1,0:T(8,128)(2,1)S(1)}, u32[]{:S(2)}, u32[]{:S(2)}) %collective-permute-start.2) | collective-permute-done | bytes 196640 | tf_op jit(solution)/shard_map/while/body/eval_jaxpr/ppermute | solution.py:28
  103.5 9.6 %collective-permute-start.17 = (bf16[1024,768]{1,0:T(8,128)(2,1)S(1)}, bf16[1024,768]{1,0:T(8,128)(2,1)S(1)}, u32[]{:S(2)}, u32[]{:S(2)}) collective-permute-start(bf16[1024,768]{1,0:T(8,128)(2,1)S(1)} %constant_dynamic-update-slice_fusion.5), channel_id=1, source_target_pairs={{0,16},{16,0},{1,17},{17,1},{2,18},{18,2},{3,19},{19,3},{4,20},{20... | collective-permute-start | bytes 4718600 | tf_op jit(solution)/shard_map/ppermute | solution.py:24
  116.2 16.7 %newton_schulz.1 = (f32[128,768]{1,0:T(8,128)}, bf16[128,768]{1,0:T(8,128)(2,1)S(1)}) custom-call(f32[768,768]{1,0:T(8,128)S(1)} %fusion.6.gram_ref, bf16[1024,768]{1,0:T(8,128)(2,1)S(1)} %collective-permute-done.17.other_ref, f32[128,768]{1,0:T(8,128)S(1)} %get-tuple-element.325.mom_ref, bf16[128,768]{1,0:T(8,128)(2,1)S(1)} %bitcast.47), custom_call_target="tpu_custom_call" | custom-call | flops 12683575296 | bytes 4718592 | tf_op jit(solution)/shard_map/newton_schulz/pallas_call | solution.py:308
  132.9 2.5 %collective-permute-start.20 = (bf16[128,768]{1,0:T(8,128)(2,1)S(1)}, bf16[128,768]{1,0:T(8,128)(2,1)S(1)}, u32[]{:S(2)}, u32[]{:S(2)}) collective-permute-start(bf16[128,768]{1,0:T(8,128)(2,1)S(1)} %get-tuple-element.291.refs_0_), channel_id=1, source_target_pairs={{0,12},{4,0},{8,4},{12,8},{1,13},{5,1},{9,5},{13,9},{2,14},{6,2},{... | collective-permute-start | bytes 589832 | tf_op jit(solution)/shard_map/ppermute | solution.py:36
  136.0 7.4 %collective-permute-done.20.refs_3_ = bf16[128,768]{1,0:T(8,128)(2,1)S(1)} collective-permute-done((bf16[128,768]{1,0:T(8,128)(2,1)S(1)}, bf16[128,768]{1,0:T(8,128)(2,1)S(1)}, u32[]{:S(2)}, u32[]{:S(2)}) %collective-permute-start.20) | collective-permute-done | bytes 196640 | tf_op jit(solution)/shard_map/ppermute | solution.py:36
  143.4 3.9 %collective-permute-done.18.refs_1_ = bf16[128,768]{1,0:T(8,128)(2,1)S(1)} collective-permute-done((bf16[128,768]{1,0:T(8,128)(2,1)S(1)}, bf16[128,768]{1,0:T(8,128)(2,1)S(1)}, u32[]{:S(2)}, u32[]{:S(2)}) %collective-permute-start.18) | collective-permute-done | bytes 196640 | tf_op jit(solution)/shard_map/ppermute | solution.py:36
  151.0 4.5 %collective-permute-done.21.refs_1_ = bf16[128,768]{1,0:T(8,128)(2,1)S(1)} collective-permute-done((bf16[128,768]{1,0:T(8,128)(2,1)S(1)}, bf16[128,768]{1,0:T(8,128)(2,1)S(1)}, u32[]{:S(2)}, u32[]{:S(2)}) %collective-permute-start.21) | collective-permute-done | bytes 196640 | tf_op jit(solution)/shard_map/ppermute | solution.py:36
  155.5 3.1 %collective-permute-done.22.refs_2_ = bf16[128,768]{1,0:T(8,128)(2,1)S(1)} collective-permute-done((bf16[128,768]{1,0:T(8,128)(2,1)S(1)}, bf16[128,768]{1,0:T(8,128)(2,1)S(1)}, u32[]{:S(2)}, u32[]{:S(2)}) %collective-permute-start.22) | collective-permute-done | bytes 196640 | tf_op jit(solution)/shard_map/ppermute | solution.py:36
  160.5 26.3 %while.51 = (s32[]{:T(128)}, bf16[128,768]{1,0:T(8,128)(2,1)S(1)}, bf16[128,768]{1,0:T(8,128)(2,1)S(1)}, bf16[1024,768]{1,0:T(8,128)(2,1)S(1)}, s32[]{:T(128)}, ...) while((s32[]{:T(128)}, bf16[128,768]{1,0:T(8,128)(2,1)S(1)}, bf16[128,768]{1,0:T(8,128)(2,1)S(1)}, ...), condition=%wide.region_5.0_spmd, body=%wide.region_4.0_spmd.sunk | while | flops 12 | bytes 3146025 | solution.py:357
  163.8 3.4 %collective-permute-done.4 = bf16[128,768]{1,0:T(8,128)(2,1)S(1)} collective-permute-done((bf16[128,768]{1,0:T(8,128)(2,1)S(1)}, bf16[128,768]{1,0:T(8,128)(2,1)S(1)}, u32[]{:S(2)}, u32[]{:S(2)}) %collective-permute-start.4) | collective-permute-done | bytes 196640 | tf_op jit(solution)/shard_map/while/body/eval_jaxpr/ppermute | solution.py:28
  170.6 2.9 %collective-permute-done.4 = bf16[128,768]{1,0:T(8,128)(2,1)S(1)} collective-permute-done((bf16[128,768]{1,0:T(8,128)(2,1)S(1)}, bf16[128,768]{1,0:T(8,128)(2,1)S(1)}, u32[]{:S(2)}, u32[]{:S(2)}) %collective-permute-start.4) | collective-permute-done | bytes 196640 | tf_op jit(solution)/shard_map/while/body/eval_jaxpr/ppermute | solution.py:28
  176.7 2.9 %collective-permute-done.4 = bf16[128,768]{1,0:T(8,128)(2,1)S(1)} collective-permute-done((bf16[128,768]{1,0:T(8,128)(2,1)S(1)}, bf16[128,768]{1,0:T(8,128)(2,1)S(1)}, u32[]{:S(2)}, u32[]{:S(2)}) %collective-permute-start.4) | collective-permute-done | bytes 196640 | tf_op jit(solution)/shard_map/while/body/eval_jaxpr/ppermute | solution.py:28
  183.0 3.4 %collective-permute-done.4 = bf16[128,768]{1,0:T(8,128)(2,1)S(1)} collective-permute-done((bf16[128,768]{1,0:T(8,128)(2,1)S(1)}, bf16[128,768]{1,0:T(8,128)(2,1)S(1)}, u32[]{:S(2)}, u32[]{:S(2)}) %collective-permute-start.4) | collective-permute-done | bytes 196640 | tf_op jit(solution)/shard_map/while/body/eval_jaxpr/ppermute | solution.py:28
  186.8 6.9 %collective-permute-start.24 = (bf16[1024,768]{1,0:T(8,128)(2,1)S(1)}, bf16[1024,768]{1,0:T(8,128)(2,1)S(1)}, u32[]{:S(2)}, u32[]{:S(2)}) collective-permute-start(bf16[1024,768]{1,0:T(8,128)(2,1)S(1)} %constant_dynamic-update-slice_fusion.4.blocks_ref), channel_id=1, source_target_pairs={{0,16},{16,0},{1,17},{17,1},{2,18},{18,2},{3,19},{19,3},{4,20},{20... | collective-permute-start | bytes 4718600 | tf_op jit(solution)/shard_map/ppermute | solution.py:24
  (133 shorter events, 64.6 us)
Async XLA Ops:
  0.6 6.4 %collective-permute-start.7 = (bf16[256,2048]{1,0:T(8,128)(2,1)}, bf16[256,2048]{1,0:T(8,128)(2,1)S(1)}, u32[]{:S(2)}, u32[]{:S(2)}) collective-permute-start(bf16[256,2048]{1,0:T(8,128)(2,1)} %bitcast.32), channel_id=1, source_target_pairs={{0,16},{16,0},{1,17},{17,1},{2,18},{18,2},{3,19},{19,3},{4,20},{20... | collective-permute-start | bytes 3145736 | tf_op jit(solution)/shard_map/ppermute | solution.py:24
  10.9 11.0 %collective-permute-start.10 = (bf16[128,768]{1,0:T(8,128)(2,1)S(1)}, bf16[128,768]{1,0:T(8,128)(2,1)S(1)}, u32[]{:S(2)}, u32[]{:S(2)}) collective-permute-start(bf16[128,768]{1,0:T(8,128)(2,1)S(1)} %get-tuple-element.326), channel_id=1, source_target_pairs={{32,0},{64,32},{96,64},{128,96},{160,128},{192,160},{224,192},{0,2... | collective-permute-start | bytes 589832 | tf_op jit(solution)/shard_map/ppermute | solution.py:32
  14.8 7.0 %collective-permute-start.9 = (bf16[128,768]{1,0:T(8,128)(2,1)S(1)}, bf16[128,768]{1,0:T(8,128)(2,1)S(1)}, u32[]{:S(2)}, u32[]{:S(2)}) collective-permute-start(bf16[128,768]{1,0:T(8,128)(2,1)S(1)} %get-tuple-element.327), channel_id=1, source_target_pairs={{0,32},{32,64},{64,96},{96,128},{128,160},{160,192},{192,224},{224... | collective-permute-start | bytes 589832 | tf_op jit(solution)/shard_map/ppermute | solution.py:28
  22.8 9.3 %collective-permute-start.1 = (bf16[256,768]{1,0:T(8,128)(2,1)}, bf16[256,768]{1,0:T(8,128)(2,1)S(1)}, u32[]{:S(2)}, u32[]{:S(2)}) collective-permute-start(bf16[256,768]{1,0:T(8,128)(2,1)} %get-tuple-element.419), channel_id=1, source_target_pairs={{32,0},{64,32},{96,64},{128,96},{160,128},{192,160},{224,192},{0,2... | collective-permute-start | bytes 1179656 | tf_op jit(solution)/shard_map/while/body/eval_jaxpr/ppermute | solution.py:32
  23.0 10.3 %collective-permute-start = (bf16[256,768]{1,0:T(8,128)(2,1)S(1)}, bf16[256,768]{1,0:T(8,128)(2,1)S(1)}, u32[]{:S(2)}, u32[]{:S(2)}) collective-permute-start(bf16[256,768]{1,0:T(8,128)(2,1)S(1)} %get-tuple-element.418), channel_id=1, source_target_pairs={{0,32},{32,64},{64,96},{96,128},{128,160},{160,192},{192,224},{224... | collective-permute-start | bytes 1179656 | tf_op jit(solution)/shard_map/while/body/eval_jaxpr/ppermute | solution.py:28
  33.5 8.5 %collective-permute-start.1 = (bf16[256,768]{1,0:T(8,128)(2,1)}, bf16[256,768]{1,0:T(8,128)(2,1)S(1)}, u32[]{:S(2)}, u32[]{:S(2)}) collective-permute-start(bf16[256,768]{1,0:T(8,128)(2,1)} %get-tuple-element.419), channel_id=1, source_target_pairs={{32,0},{64,32},{96,64},{128,96},{160,128},{192,160},{224,192},{0,2... | collective-permute-start | bytes 1179656 | tf_op jit(solution)/shard_map/while/body/eval_jaxpr/ppermute | solution.py:32
  34.9 9.4 %collective-permute-start = (bf16[256,768]{1,0:T(8,128)(2,1)S(1)}, bf16[256,768]{1,0:T(8,128)(2,1)S(1)}, u32[]{:S(2)}, u32[]{:S(2)}) collective-permute-start(bf16[256,768]{1,0:T(8,128)(2,1)S(1)} %get-tuple-element.418), channel_id=1, source_target_pairs={{0,32},{32,64},{64,96},{96,128},{128,160},{160,192},{192,224},{224... | collective-permute-start | bytes 1179656 | tf_op jit(solution)/shard_map/while/body/eval_jaxpr/ppermute | solution.py:28
  44.4 7.6 %collective-permute-start.1 = (bf16[256,768]{1,0:T(8,128)(2,1)}, bf16[256,768]{1,0:T(8,128)(2,1)S(1)}, u32[]{:S(2)}, u32[]{:S(2)}) collective-permute-start(bf16[256,768]{1,0:T(8,128)(2,1)} %get-tuple-element.419), channel_id=1, source_target_pairs={{32,0},{64,32},{96,64},{128,96},{160,128},{192,160},{224,192},{0,2... | collective-permute-start | bytes 1179656 | tf_op jit(solution)/shard_map/while/body/eval_jaxpr/ppermute | solution.py:32
  45.8 8.5 %collective-permute-start = (bf16[256,768]{1,0:T(8,128)(2,1)S(1)}, bf16[256,768]{1,0:T(8,128)(2,1)S(1)}, u32[]{:S(2)}, u32[]{:S(2)}) collective-permute-start(bf16[256,768]{1,0:T(8,128)(2,1)S(1)} %get-tuple-element.418), channel_id=1, source_target_pairs={{0,32},{32,64},{64,96},{96,128},{128,160},{160,192},{192,224},{224... | collective-permute-start | bytes 1179656 | tf_op jit(solution)/shard_map/while/body/eval_jaxpr/ppermute | solution.py:28
  55.7 7.5 %collective-permute-start.13 = (bf16[128,768]{1,0:T(8,128)(2,1)S(1)}, bf16[128,768]{1,0:T(8,128)(2,1)S(1)}, u32[]{:S(2)}, u32[]{:S(2)}) collective-permute-start(bf16[128,768]{1,0:T(8,128)(2,1)S(1)} %slice.43.refs_0_), channel_id=1, source_target_pairs={{0,3},{1,0},{2,1},{3,2},{4,7},{5,4},{6,5},{7,6},{8,11},{9,8},{10,9... | collective-permute-start | bytes 589832 | tf_op jit(solution)/shard_map/ppermute | solution.py:36
  58.4 6.1 %collective-permute-start.12 = (bf16[128,768]{1,0:T(8,128)(2,1)S(1)}, bf16[128,768]{1,0:T(8,128)(2,1)S(1)}, u32[]{:S(2)}, u32[]{:S(2)}) collective-permute-start(bf16[128,768]{1,0:T(8,128)(2,1)S(1)} %slice.43.refs_0_), channel_id=1, source_target_pairs={{0,2},{1,3},{2,0},{3,1},{4,6},{5,7},{6,4},{7,5},{8,10},{9,11},{10,... | collective-permute-start | bytes 589832 | tf_op jit(solution)/shard_map/ppermute | solution.py:36
  58.8 7.8 %collective-permute-start.11 = (bf16[128,768]{1,0:T(8,128)(2,1)S(1)}, bf16[128,768]{1,0:T(8,128)(2,1)S(1)}, u32[]{:S(2)}, u32[]{:S(2)}) collective-permute-start(bf16[128,768]{1,0:T(8,128)(2,1)S(1)} %slice.43.refs_0_), channel_id=1, source_target_pairs={{0,1},{1,2},{2,3},{3,0},{4,5},{5,6},{6,7},{7,4},{8,9},{9,10},{10,1... | collective-permute-start | bytes 589832 | tf_op jit(solution)/shard_map/ppermute | solution.py:36
  67.5 6.1 %collective-permute-start.14 = (bf16[128,768]{1,0:T(8,128)(2,1)S(1)}, bf16[128,768]{1,0:T(8,128)(2,1)S(1)}, u32[]{:S(2)}, u32[]{:S(2)}) collective-permute-start(bf16[128,768]{1,0:T(8,128)(2,1)S(1)} %get-tuple-element.285), channel_id=1, source_target_pairs={{0,8},{4,12},{8,0},{12,4},{1,9},{5,13},{9,1},{13,5},{2,10},{6,14},... | collective-permute-start | bytes 589832 | tf_op jit(solution)/shard_map/ppermute | solution.py:36
  76.4 6.1 %collective-permute-start.2 = (bf16[128,768]{1,0:T(8,128)(2,1)S(1)}, bf16[128,768]{1,0:T(8,128)(2,1)S(1)}, u32[]{:S(2)}, u32[]{:S(2)}) collective-permute-start(bf16[128,768]{1,0:T(8,128)(2,1)S(1)} %copy.28), channel_id=1, source_target_pairs={{0,32},{32,64},{64,96},{96,128},{128,160},{160,192},{192,224},{224... | collective-permute-start | bytes 589832 | tf_op jit(solution)/shard_map/while/body/eval_jaxpr/ppermute | solution.py:28
  76.5 6.0 %collective-permute-start.3 = (bf16[128,768]{1,0:T(8,128)(2,1)S(1)}, bf16[128,768]{1,0:T(8,128)(2,1)S(1)}, u32[]{:S(2)}, u32[]{:S(2)}) collective-permute-start(bf16[128,768]{1,0:T(8,128)(2,1)S(1)} %copy.29), channel_id=1, source_target_pairs={{32,0},{64,32},{96,64},{128,96},{160,128},{192,160},{224,192},{0,2... | collective-permute-start | bytes 589832 | tf_op jit(solution)/shard_map/while/body/eval_jaxpr/ppermute | solution.py:32
  82.5 6.7 %collective-permute-start.2 = (bf16[128,768]{1,0:T(8,128)(2,1)S(1)}, bf16[128,768]{1,0:T(8,128)(2,1)S(1)}, u32[]{:S(2)}, u32[]{:S(2)}) collective-permute-start(bf16[128,768]{1,0:T(8,128)(2,1)S(1)} %copy.28), channel_id=1, source_target_pairs={{0,32},{32,64},{64,96},{96,128},{128,160},{160,192},{192,224},{224... | collective-permute-start | bytes 589832 | tf_op jit(solution)/shard_map/while/body/eval_jaxpr/ppermute | solution.py:28
  82.7 6.6 %collective-permute-start.3 = (bf16[128,768]{1,0:T(8,128)(2,1)S(1)}, bf16[128,768]{1,0:T(8,128)(2,1)S(1)}, u32[]{:S(2)}, u32[]{:S(2)}) collective-permute-start(bf16[128,768]{1,0:T(8,128)(2,1)S(1)} %copy.29), channel_id=1, source_target_pairs={{32,0},{64,32},{96,64},{128,96},{160,128},{192,160},{224,192},{0,2... | collective-permute-start | bytes 589832 | tf_op jit(solution)/shard_map/while/body/eval_jaxpr/ppermute | solution.py:32
  89.3 5.9 %collective-permute-start.2 = (bf16[128,768]{1,0:T(8,128)(2,1)S(1)}, bf16[128,768]{1,0:T(8,128)(2,1)S(1)}, u32[]{:S(2)}, u32[]{:S(2)}) collective-permute-start(bf16[128,768]{1,0:T(8,128)(2,1)S(1)} %copy.28), channel_id=1, source_target_pairs={{0,32},{32,64},{64,96},{96,128},{128,160},{160,192},{192,224},{224... | collective-permute-start | bytes 589832 | tf_op jit(solution)/shard_map/while/body/eval_jaxpr/ppermute | solution.py:28
  90.8 6.3 %collective-permute-start.3 = (bf16[128,768]{1,0:T(8,128)(2,1)S(1)}, bf16[128,768]{1,0:T(8,128)(2,1)S(1)}, u32[]{:S(2)}, u32[]{:S(2)}) collective-permute-start(bf16[128,768]{1,0:T(8,128)(2,1)S(1)} %copy.29), channel_id=1, source_target_pairs={{32,0},{64,32},{96,64},{128,96},{160,128},{192,160},{224,192},{0,2... | collective-permute-start | bytes 589832 | tf_op jit(solution)/shard_map/while/body/eval_jaxpr/ppermute | solution.py:32
  97.1 6.4 %collective-permute-start.2 = (bf16[128,768]{1,0:T(8,128)(2,1)S(1)}, bf16[128,768]{1,0:T(8,128)(2,1)S(1)}, u32[]{:S(2)}, u32[]{:S(2)}) collective-permute-start(bf16[128,768]{1,0:T(8,128)(2,1)S(1)} %copy.28), channel_id=1, source_target_pairs={{0,32},{32,64},{64,96},{96,128},{128,160},{160,192},{192,224},{224... | collective-permute-start | bytes 589832 | tf_op jit(solution)/shard_map/while/body/eval_jaxpr/ppermute | solution.py:28
  103.5 12.7 %collective-permute-start.17 = (bf16[1024,768]{1,0:T(8,128)(2,1)S(1)}, bf16[1024,768]{1,0:T(8,128)(2,1)S(1)}, u32[]{:S(2)}, u32[]{:S(2)}) collective-permute-start(bf16[1024,768]{1,0:T(8,128)(2,1)S(1)} %constant_dynamic-update-slice_fusion.5), channel_id=1, source_target_pairs={{0,16},{16,0},{1,17},{17,1},{2,18},{18,2},{3,19},{19,3},{4,20},{20... | collective-permute-start | bytes 4718600 | tf_op jit(solution)/shard_map/ppermute | solution.py:24
  132.9 10.5 %collective-permute-start.20 = (bf16[128,768]{1,0:T(8,128)(2,1)S(1)}, bf16[128,768]{1,0:T(8,128)(2,1)S(1)}, u32[]{:S(2)}, u32[]{:S(2)}) collective-permute-start(bf16[128,768]{1,0:T(8,128)(2,1)S(1)} %get-tuple-element.291.refs_0_), channel_id=1, source_target_pairs={{0,12},{4,0},{8,4},{12,8},{1,13},{5,1},{9,5},{13,9},{2,14},{6,2},{... | collective-permute-start | bytes 589832 | tf_op jit(solution)/shard_map/ppermute | solution.py:36
  135.4 8.0 %collective-permute-start.19 = (bf16[128,768]{1,0:T(8,128)(2,1)S(1)}, bf16[128,768]{1,0:T(8,128)(2,1)S(1)}, u32[]{:S(2)}, u32[]{:S(2)}) collective-permute-start(bf16[128,768]{1,0:T(8,128)(2,1)S(1)} %get-tuple-element.291.refs_0_), channel_id=1, source_target_pairs={{0,8},{4,12},{8,0},{12,4},{1,9},{5,13},{9,1},{13,5},{2,10},{6,14},... | collective-permute-start | bytes 589832 | tf_op jit(solution)/shard_map/ppermute | solution.py:36
  135.4 11.9 %collective-permute-start.18 = (bf16[128,768]{1,0:T(8,128)(2,1)S(1)}, bf16[128,768]{1,0:T(8,128)(2,1)S(1)}, u32[]{:S(2)}, u32[]{:S(2)}) collective-permute-start(bf16[128,768]{1,0:T(8,128)(2,1)S(1)} %get-tuple-element.291.refs_0_), channel_id=1, source_target_pairs={{0,4},{4,8},{8,12},{12,0},{1,5},{5,9},{9,13},{13,1},{2,6},{6,10},{... | collective-permute-start | bytes 589832 | tf_op jit(solution)/shard_map/ppermute | solution.py:36
  148.0 7.5 %collective-permute-start.21 = (bf16[128,768]{1,0:T(8,128)(2,1)S(1)}, bf16[128,768]{1,0:T(8,128)(2,1)S(1)}, u32[]{:S(2)}, u32[]{:S(2)}) collective-permute-start(bf16[128,768]{1,0:T(8,128)(2,1)S(1)} %get-tuple-element.293), channel_id=1, source_target_pairs={{0,1},{1,2},{2,3},{3,0},{4,5},{5,6},{6,7},{7,4},{8,9},{9,10},{10,1... | collective-permute-start | bytes 589832 | tf_op jit(solution)/shard_map/ppermute | solution.py:36
  148.1 10.5 %collective-permute-start.22 = (bf16[128,768]{1,0:T(8,128)(2,1)S(1)}, bf16[128,768]{1,0:T(8,128)(2,1)S(1)}, u32[]{:S(2)}, u32[]{:S(2)}) collective-permute-start(bf16[128,768]{1,0:T(8,128)(2,1)S(1)} %get-tuple-element.294), channel_id=1, source_target_pairs={{0,2},{1,3},{2,0},{3,1},{4,6},{5,7},{6,4},{7,5},{8,10},{9,11},{10,... | collective-permute-start | bytes 589832 | tf_op jit(solution)/shard_map/ppermute | solution.py:36
  150.1 9.6 %collective-permute-start.23 = (bf16[128,768]{1,0:T(8,128)(2,1)S(1)}, bf16[128,768]{1,0:T(8,128)(2,1)S(1)}, u32[]{:S(2)}, u32[]{:S(2)}) collective-permute-start(bf16[128,768]{1,0:T(8,128)(2,1)S(1)} %get-tuple-element.295), channel_id=1, source_target_pairs={{0,3},{1,0},{2,1},{3,2},{4,7},{5,4},{6,5},{7,6},{8,11},{9,8},{10,9... | collective-permute-start | bytes 589832 | tf_op jit(solution)/shard_map/ppermute | solution.py:36
  160.5 6.7 %collective-permute-start.4 = (bf16[128,768]{1,0:T(8,128)(2,1)S(1)}, bf16[128,768]{1,0:T(8,128)(2,1)S(1)}, u32[]{:S(2)}, u32[]{:S(2)}) collective-permute-start(bf16[128,768]{1,0:T(8,128)(2,1)S(1)} %copy.41), channel_id=1, source_target_pairs={{0,32},{32,64},{64,96},{96,128},{128,160},{160,192},{192,224},{224... | collective-permute-start | bytes 589832 | tf_op jit(solution)/shard_map/while/body/eval_jaxpr/ppermute | solution.py:28
  173.8 5.8 %collective-permute-start.4 = (bf16[128,768]{1,0:T(8,128)(2,1)S(1)}, bf16[128,768]{1,0:T(8,128)(2,1)S(1)}, u32[]{:S(2)}, u32[]{:S(2)}) collective-permute-start(bf16[128,768]{1,0:T(8,128)(2,1)S(1)} %copy.41), channel_id=1, source_target_pairs={{0,32},{32,64},{64,96},{96,128},{128,160},{160,192},{192,224},{224... | collective-permute-start | bytes 589832 | tf_op jit(solution)/shard_map/while/body/eval_jaxpr/ppermute | solution.py:28
  180.1 6.3 %collective-permute-start.4 = (bf16[128,768]{1,0:T(8,128)(2,1)S(1)}, bf16[128,768]{1,0:T(8,128)(2,1)S(1)}, u32[]{:S(2)}, u32[]{:S(2)}) collective-permute-start(bf16[128,768]{1,0:T(8,128)(2,1)S(1)} %copy.41), channel_id=1, source_target_pairs={{0,32},{32,64},{64,96},{96,128},{128,160},{160,192},{192,224},{224... | collective-permute-start | bytes 589832 | tf_op jit(solution)/shard_map/while/body/eval_jaxpr/ppermute | solution.py:28
  180.9 5.9 %collective-permute-start.5 = (bf16[128,768]{1,0:T(8,128)(2,1)S(1)}, bf16[128,768]{1,0:T(8,128)(2,1)S(1)}, u32[]{:S(2)}, u32[]{:S(2)}) collective-permute-start(bf16[128,768]{1,0:T(8,128)(2,1)S(1)} %copy.42), channel_id=1, source_target_pairs={{32,0},{64,32},{96,64},{128,96},{160,128},{192,160},{224,192},{0,2... | collective-permute-start | bytes 589832 | tf_op jit(solution)/shard_map/while/body/eval_jaxpr/ppermute | solution.py:32
  186.8 10.0 %collective-permute-start.24 = (bf16[1024,768]{1,0:T(8,128)(2,1)S(1)}, bf16[1024,768]{1,0:T(8,128)(2,1)S(1)}, u32[]{:S(2)}, u32[]{:S(2)}) collective-permute-start(bf16[1024,768]{1,0:T(8,128)(2,1)S(1)} %constant_dynamic-update-slice_fusion.4.blocks_ref), channel_id=1, source_target_pairs={{0,16},{16,0},{1,17},{17,1},{2,18},{18,2},{3,19},{19,3},{4,20},{20... | collective-permute-start | bytes 4718600 | tf_op jit(solution)/shard_map/ppermute | solution.py:24
  (16 other events, 131.6 us)
where the time goes:
time: 199 us
  waiting for transfers between devices  93.7 us (47%)
  starting transfers between devices  67.3 us (34%)
  Pallas kernels  25.7 us (13%)
  other arithmetic  5.34 us (3%)
  local copies, waits for them, and re-layouts  3.85 us (2%)
    ppermute x12, waiting for transfers between devices, up(): return lax.ppermute(value, 'z', [(i, (i + 1) % NZ) for i in range(NZ)])  33.9 us
    ppermute x12, waiting for transfers between devices, shift(): return lax.ppermute(value, axis, [(i, (i + offset) % 4) for i in range(4)])  30.2 us
    ppermute x12, waiting for transfers between devices, down(): return lax.ppermute(value, 'z', [((i + 1) % NZ, i) for i in range(NZ)])  24.4 us
    ppermute x12, starting transfers between devices, down(): return lax.ppermute(value, 'z', [((i + 1) % NZ, i) for i in range(NZ)])  21.3 us
    ppermute x5, starting transfers between devices, swap(): return lax.ppermute(value, 'core', [(0, 1), (1, 0)])  20.4 us
    pallas_call x1, Pallas kernels, newton_schulz(): pl.pallas_call(functools.partial(newton_kernel, 0.2 * math.sqrt(longest))...  16.7 us
    ppermute x12, starting transfers between devices, shift(): return lax.ppermute(value, axis, [(i, (i + offset) % 4) for i in range(4)])  15.3 us
    ppermute x12, starting transfers between devices, up(): return lax.ppermute(value, 'z', [(i, (i + 1) % NZ) for i in range(NZ)])  10.3 us
  transfers between devices with their start and end apart: 41, of which 33 were waited for; matrix products, arithmetic and copies ran while one was open for 2% of the time, Pallas kernels for 2%

commit v1 on v0

--- a/solution.py
+++ b/solution.py
@@ -198,7 +198,7 @@
         out_shape=(jax.ShapeDtypeStruct((2 * rows, width), BF),) * len(offsets),
         in_specs=[SMEM] * 3 + [VMEM] * 4,
         out_specs=(VMEM,) * len(offsets),
-        compiler_params=small(20),
+        compiler_params=small(56 if len(offsets) == 1 else 20),
         cost_estimate=pl.CostEstimate(
             flops=8 * tok_rows * rows * len(offsets) * width,
             bytes_accessed=4 * tok_rows * rows * NZ,
@@ -333,15 +333,9 @@
     copies, homes = up(far[:rows]), down(far[rows:])
     below = jnp.concatenate([add_bf(up3[:rows], copies), up3[rows:]], axis=0)
     above = jnp.concatenate([down3[:rows], add_bf(down3[rows:], homes)], axis=0)
-    on_up = jnp.stack([up2, up1, mine])
-    on_down = jnp.stack([down2, down1, jnp.zeros_like(mine)])
-
-    def one(step, carry):
-        below, above = carry
-        below, above = up(below), down(above)
-        return add_bf(below, on_up[step]), add_bf(above, on_down[step])
-
-    return lax.fori_loop(0, 3, one, (below, above))
+    for near_up, near_down in ((up2, down2), (up1, down1)):
+        below, above = add_bf(near_up, up(below)), add_bf(near_down, down(above))
+    return mine.astype(F32) + up(below).astype(F32) + down(above).astype(F32)
 
 
 def ring(block):
@@ -368,12 +362,11 @@
     tokens = (counts[0], swap(counts[0]), acts, swap(acts), grads, swap(grads))
     (far,) = terms(here, *tokens, (4,))
     near = terms(here, *tokens, (3, 2, 1, 0, -1, -2, -3))
-    below, above = ring_sum(far, near)
-    rows = below.shape[0] // 2
-    total = below.astype(F32) + above.astype(F32)
+    total = ring_sum(far, near)
+    rows = total.shape[0] // 2
     copy_sum, home_sum = total[:rows].astype(BF), total[rows:]
 
-    pieces = {offset: shift(copy_sum, "y", offset) for offset in (2, 1, 3)}
+    pieces = {offset: shift(copy_sum, "y", offset) for offset in (3, 1, 2)}
     pieces = [copy_sum] + [pieces[offset] for offset in range(1, NY)]
     copies, *sent = buckets(here, copy_list, pieces)
     for ahead in (2, 1, 3):
@@ -386,7 +379,7 @@
         gram, swap(own), fresh_mom, weights[0], max(model_width, width)
     )
 
-    pieces = {offset: shift(fresh, "x", offset) for offset in (2, 1, 3)}
+    pieces = {offset: shift(fresh, "x", offset) for offset in (3, 1, 2)}
     pieces = [fresh] + [pieces[offset] for offset in range(1, NX)]
     kept, *sent = wanted(here, copy_list, pieces)
     pieces = {offset: shift(sent[offset - 1], "y", offset) for offset in (2, 1, 3)}

time: 199 us -> 199 us (level)
  waiting for transfers between devices: 93.7 us -> 86.1 us
  starting transfers between devices: 67.3 us -> 74.6 us
  other arithmetic: 5.34 us -> 1.49 us
  local copies, waits for them, and re-layouts: 3.85 us -> 6.48 us
    ppermute x12, starting transfers between devices: 21.3 us -> 29.1 us  [down(): return lax.ppermute(value, 'z', [((i + 1) % NZ, i) for i in range(NZ)])]
    ppermute x12, waiting for transfers between devices: 33.9 us -> 29.1 us  [up(): return lax.ppermute(value, 'z', [(i, (i + 1) % NZ) for i in range(NZ)])]
    ppermute x12, starting transfers between devices: 10.3 us -> 7.42 us  [up(): return lax.ppermute(value, 'z', [(i, (i + 1) % NZ) for i in range(NZ)])]
    convert_element_type x8 -> x6, other arithmetic: 2.92 us -> 0.48 us  [add_bf(): return (left.astype(F32) + right.astype(F32)).astype(BF)]
    ppermute x12, waiting for transfers between devices: 24.4 us -> 22 us  [down(): return lax.ppermute(value, 'z', [((i + 1) % NZ, i) for i in range(NZ)])]
    unnamed x16 -> x30, local copies, waits for them, and re-layouts: 2.93 us -> 4.61 us
  transfers between devices with their start and end apart: 41 -> 41, of which waited for: 33 -> 31; matrix products, arithmetic and copies ran while one was open for 2% -> 2% of each run, Pallas kernels for 2% -> 2%
where the time goes in v1:
time: 199 us
  waiting for transfers between devices  86.1 us (43%)
  starting transfers between devices  74.6 us (37%)
  Pallas kernels  27.6 us (14%)
  local copies, waits for them, and re-layouts  6.48 us (3%)
    ppermute x12, waiting for transfers between devices, shift(): return lax.ppermute(value, axis, [(i, (i + offset) % 4) for i in range(4)])  30.3 us
    ppermute x12, waiting for transfers between devices, up(): return lax.ppermute(value, 'z', [(i, (i + 1) % NZ) for i in range(NZ)])  29.1 us
    ppermute x12, starting transfers between devices, down(): return lax.ppermute(value, 'z', [((i + 1) % NZ, i) for i in range(NZ)])  29.1 us
    ppermute x12, waiting for transfers between devices, down(): return lax.ppermute(value, 'z', [((i + 1) % NZ, i) for i in range(NZ)])  22 us
    ppermute x5, starting transfers between devices, swap(): return lax.ppermute(value, 'core', [(0, 1), (1, 0)])  21.8 us
    pallas_call x1, Pallas kernels, newton_schulz(): pl.pallas_call(functools.partial(newton_kernel, 0.2 * math.sqrt(longest))...  16.7 us
    ppermute x12, starting transfers between devices, shift(): return lax.ppermute(value, axis, [(i, (i + offset) % 4) for i in range(4)])  16.3 us
    ppermute x12, starting transfers between devices, up(): return lax.ppermute(value, 'z', [(i, (i + 1) % NZ) for i in range(NZ)])  7.42 us
  transfers between devices with their start and end apart: 41, of which 31 were waited for; matrix products, arithmetic and copies ran while one was open for 2% of the time, Pallas kernels for 2%

profile of v1, /device:TPU:1, one launch (start us, length us, event | category | flops | bytes accessed | tf_op | source)
XLA Modules:
  0.0 199.1 jit_solution(7493896996906601795)
XLA Ops:
  0.6 3.3 %collective-permute-start.5 = (bf16[256,2048]{1,0:T(8,128)(2,1)}, bf16[256,2048]{1,0:T(8,128)(2,1)S(1)}, u32[]{:S(2)}, u32[]{:S(2)}) collective-permute-start(bf16[256,2048]{1,0:T(8,128)(2,1)} %bitcast.16), channel_id=1, source_target_pairs={{0,16},{16,0},{1,17},{17,1},{2,18},{18,2},{3,19},{19,3},{4,20},{20... | collective-permute-start | bytes 3145736 | tf_op jit(solution)/shard_map/ppermute | solution.py:24
  8.7 2.9 %terms.3 = bf16[256,768]{1,0:T(8,128)(2,1)} custom-call(s32[4]{0:T(128)} %pad_add_fusion.here_ref, s32[1,2]{1,0:T(1,128)} %bitcast.24, s32[1,2]{1,0:T(1,128)} %copy-done.10, bf16[256,2048]{1,0:T(8,128)(2,1)} %bitcast.17, bf16[256,2048]{1,0:T(8,128)(2,1)} %copy-done.1, bf16[256,768]{1,0:T(8,128)(2,1)} %bitcast.20, bf16[256,768]{1,0:T(8,128)(2,1)} %copy-done.5), custom_call_target="tpu_custom_call" | custom-call | flops 201326592 | bytes 1048576 | tf_op jit(solution)/shard_map/terms/pallas_call | solution.py:196
  12.7 3.9 %collective-permute-start.11 = (bf16[128,768]{1,0:T(8,128)(2,1)S(1)}, bf16[128,768]{1,0:T(8,128)(2,1)S(1)}, u32[]{:S(2)}, u32[]{:S(2)}) collective-permute-start(bf16[128,768]{1,0:T(8,128)(2,1)S(1)} %get-tuple-element.220), channel_id=1, source_target_pairs={{32,0},{64,32},{96,64},{128,96},{160,128},{192,160},{224,192},{0,2... | collective-permute-start | bytes 589832 | tf_op jit(solution)/shard_map/ppermute | solution.py:32
  24.8 7.3 %collective-permute-done.12 = bf16[256,768]{1,0:T(8,128)(2,1)S(1)} collective-permute-done((bf16[256,768]{1,0:T(8,128)(2,1)S(1)}, bf16[256,768]{1,0:T(8,128)(2,1)S(1)}, u32[]{:S(2)}, u32[]{:S(2)}) %collective-permute-start.12) | collective-permute-done | bytes 393248 | tf_op jit(solution)/shard_map/ppermute | solution.py:32
  32.2 3.5 %collective-permute-start.13 = (bf16[256,768]{1,0:T(8,128)(2,1)S(1)}, bf16[256,768]{1,0:T(8,128)(2,1)S(1)}, u32[]{:S(2)}, u32[]{:S(2)}) collective-permute-start(bf16[256,768]{1,0:T(8,128)(2,1)S(1)} %add_convert_fusion.1), channel_id=1, source_target_pairs={{32,0},{64,32},{96,64},{128,96},{160,128},{192,160},{224,192},{0,2... | collective-permute-start | bytes 1179656 | tf_op jit(solution)/shard_map/ppermute | solution.py:32
  35.9 6.4 %collective-permute-done.13 = bf16[256,768]{1,0:T(8,128)(2,1)S(1)} collective-permute-done((bf16[256,768]{1,0:T(8,128)(2,1)S(1)}, bf16[256,768]{1,0:T(8,128)(2,1)S(1)}, u32[]{:S(2)}, u32[]{:S(2)}) %collective-permute-start.13) | collective-permute-done | bytes 393248 | tf_op jit(solution)/shard_map/ppermute | solution.py:32
  42.4 3.5 %collective-permute-start.14 = (bf16[256,768]{1,0:T(8,128)(2,1)S(1)}, bf16[256,768]{1,0:T(8,128)(2,1)S(1)}, u32[]{:S(2)}, u32[]{:S(2)}) collective-permute-start(bf16[256,768]{1,0:T(8,128)(2,1)S(1)} %add_convert_fusion), channel_id=1, source_target_pairs={{32,0},{64,32},{96,64},{128,96},{160,128},{192,160},{224,192},{0,2... | collective-permute-start | bytes 1179656 | tf_op jit(solution)/shard_map/ppermute | solution.py:32
  46.0 5.5 %collective-permute-done.14 = bf16[256,768]{1,0:T(8,128)(2,1)S(1)} collective-permute-done((bf16[256,768]{1,0:T(8,128)(2,1)S(1)}, bf16[256,768]{1,0:T(8,128)(2,1)S(1)}, u32[]{:S(2)}, u32[]{:S(2)}) %collective-permute-start.14) | collective-permute-done | bytes 393248 | tf_op jit(solution)/shard_map/ppermute | solution.py:32
  51.5 3.3 %collective-permute-done.10 = bf16[256,768]{1,0:T(8,128)(2,1)S(1)} collective-permute-done((bf16[256,768]{1,0:T(8,128)(2,1)S(1)}, bf16[256,768]{1,0:T(8,128)(2,1)S(1)}, u32[]{:S(2)}, u32[]{:S(2)}) %collective-permute-start.10) | collective-permute-done | bytes 393248 | tf_op jit(solution)/shard_map/ppermute | solution.py:28
  55.0 2.8 %collective-permute-start.17 = (bf16[128,768]{1,0:T(8,128)(2,1)S(1)}, bf16[128,768]{1,0:T(8,128)(2,1)S(1)}, u32[]{:S(2)}, u32[]{:S(2)}) collective-permute-start(bf16[128,768]{1,0:T(8,128)(2,1)S(1)} %slice.43.refs_0_), channel_id=1, source_target_pairs={{0,3},{1,0},{2,1},{3,2},{4,7},{5,4},{6,5},{7,6},{8,11},{9,8},{10,9... | collective-permute-start | bytes 589832 | tf_op jit(solution)/shard_map/ppermute | solution.py:36
  58.9 3.7 %collective-permute-done.17.refs_3_ = bf16[128,768]{1,0:T(8,128)(2,1)S(1)} collective-permute-done((bf16[128,768]{1,0:T(8,128)(2,1)S(1)}, bf16[128,768]{1,0:T(8,128)(2,1)S(1)}, u32[]{:S(2)}, u32[]{:S(2)}) %collective-permute-start.17) | collective-permute-done | bytes 196640 | tf_op jit(solution)/shard_map/ppermute | solution.py:36
  67.0 2.8 %collective-permute-start.18 = (bf16[128,768]{1,0:T(8,128)(2,1)S(1)}, bf16[128,768]{1,0:T(8,128)(2,1)S(1)}, u32[]{:S(2)}, u32[]{:S(2)}) collective-permute-start(bf16[128,768]{1,0:T(8,128)(2,1)S(1)} %get-tuple-element.188), channel_id=1, source_target_pairs={{0,8},{4,12},{8,0},{12,4},{1,9},{5,13},{9,1},{13,5},{2,10},{6,14},... | collective-permute-start | bytes 589832 | tf_op jit(solution)/shard_map/ppermute | solution.py:36
  75.8 26.0 %while.34 = (s32[]{:T(128)}, bf16[128,768]{1,0:T(8,128)(2,1)S(1)}, bf16[128,768]{1,0:T(8,128)(2,1)S(1)}, bf16[1024,768]{1,0:T(8,128)(2,1)S(1)}, s32[]{:T(128)}, ...) while((s32[]{:T(128)}, bf16[128,768]{1,0:T(8,128)(2,1)S(1)}, bf16[128,768]{1,0:T(8,128)(2,1)S(1)}, ...), condition=%wide.region_1.0_spmd, body=%wide.region_0.0_spmd.sunk | while | flops 12 | bytes 3146025 | solution.py:351
  76.0 2.7 %collective-permute-start.1 = (bf16[128,768]{1,0:T(8,128)(2,1)S(1)}, bf16[128,768]{1,0:T(8,128)(2,1)S(1)}, u32[]{:S(2)}, u32[]{:S(2)}) collective-permute-start(bf16[128,768]{1,0:T(8,128)(2,1)S(1)} %copy.20), channel_id=1, source_target_pairs={{32,0},{64,32},{96,64},{128,96},{160,128},{192,160},{224,192},{0,2... | collective-permute-start | bytes 589832 | tf_op jit(solution)/shard_map/while/body/eval_jaxpr/ppermute | solution.py:32
  78.8 3.2 %collective-permute-done = bf16[128,768]{1,0:T(8,128)(2,1)S(1)} collective-permute-done((bf16[128,768]{1,0:T(8,128)(2,1)S(1)}, bf16[128,768]{1,0:T(8,128)(2,1)S(1)}, u32[]{:S(2)}, u32[]{:S(2)}) %collective-permute-start) | collective-permute-done | bytes 196640 | tf_op jit(solution)/shard_map/while/body/eval_jaxpr/ppermute | solution.py:28
  82.1 2.7 %collective-permute-start.1 = (bf16[128,768]{1,0:T(8,128)(2,1)S(1)}, bf16[128,768]{1,0:T(8,128)(2,1)S(1)}, u32[]{:S(2)}, u32[]{:S(2)}) collective-permute-start(bf16[128,768]{1,0:T(8,128)(2,1)S(1)} %copy.20), channel_id=1, source_target_pairs={{32,0},{64,32},{96,64},{128,96},{160,128},{192,160},{224,192},{0,2... | collective-permute-start | bytes 589832 | tf_op jit(solution)/shard_map/while/body/eval_jaxpr/ppermute | solution.py:32
  84.9 4.1 %collective-permute-done = bf16[128,768]{1,0:T(8,128)(2,1)S(1)} collective-permute-done((bf16[128,768]{1,0:T(8,128)(2,1)S(1)}, bf16[128,768]{1,0:T(8,128)(2,1)S(1)}, u32[]{:S(2)}, u32[]{:S(2)}) %collective-permute-start) | collective-permute-done | bytes 196640 | tf_op jit(solution)/shard_map/while/body/eval_jaxpr/ppermute | solution.py:28
  91.9 3.2 %collective-permute-done = bf16[128,768]{1,0:T(8,128)(2,1)S(1)} collective-permute-done((bf16[128,768]{1,0:T(8,128)(2,1)S(1)}, bf16[128,768]{1,0:T(8,128)(2,1)S(1)}, u32[]{:S(2)}, u32[]{:S(2)}) %collective-permute-start) | collective-permute-done | bytes 196640 | tf_op jit(solution)/shard_map/while/body/eval_jaxpr/ppermute | solution.py:28
  98.6 2.9 %collective-permute-done = bf16[128,768]{1,0:T(8,128)(2,1)S(1)} collective-permute-done((bf16[128,768]{1,0:T(8,128)(2,1)S(1)}, bf16[128,768]{1,0:T(8,128)(2,1)S(1)}, u32[]{:S(2)}, u32[]{:S(2)}) %collective-permute-start) | collective-permute-done | bytes 196640 | tf_op jit(solution)/shard_map/while/body/eval_jaxpr/ppermute | solution.py:28
  101.8 10.6 %collective-permute-start.21 = (bf16[1024,768]{1,0:T(8,128)(2,1)S(1)}, bf16[1024,768]{1,0:T(8,128)(2,1)S(1)}, u32[]{:S(2)}, u32[]{:S(2)}) collective-permute-start(bf16[1024,768]{1,0:T(8,128)(2,1)S(1)} %constant_dynamic-update-slice_fusion.5), channel_id=1, source_target_pairs={{0,16},{16,0},{1,17},{17,1},{2,18},{18,2},{3,19},{19,3},{4,20},{20... | collective-permute-start | bytes 4718600 | tf_op jit(solution)/shard_map/ppermute | solution.py:24
  115.4 16.7 %newton_schulz.1 = (f32[128,768]{1,0:T(8,128)}, bf16[128,768]{1,0:T(8,128)(2,1)S(1)}) custom-call(f32[768,768]{1,0:T(8,128)S(1)} %fusion.4.gram_ref, bf16[1024,768]{1,0:T(8,128)(2,1)S(1)} %collective-permute-done.21.other_ref, f32[128,768]{1,0:T(8,128)S(1)} %get-tuple-element.218.mom_ref, bf16[128,768]{1,0:T(8,128)(2,1)S(1)} %bitcast.26), custom_call_target="tpu_custom_call" | custom-call | flops 12683575296 | bytes 4718592 | tf_op jit(solution)/shard_map/newton_schulz/pallas_call | solution.py:308
  132.1 3.0 %collective-permute-start.24 = (bf16[128,768]{1,0:T(8,128)(2,1)S(1)}, bf16[128,768]{1,0:T(8,128)(2,1)S(1)}, u32[]{:S(2)}, u32[]{:S(2)}) collective-permute-start(bf16[128,768]{1,0:T(8,128)(2,1)S(1)} %get-tuple-element.194.refs_0_), channel_id=1, source_target_pairs={{0,12},{4,0},{8,4},{12,8},{1,13},{5,1},{9,5},{13,9},{2,14},{6,2},{... | collective-permute-start | bytes 589832 | tf_op jit(solution)/shard_map/ppermute | solution.py:36
  135.8 7.4 %collective-permute-done.24.refs_3_ = bf16[128,768]{1,0:T(8,128)(2,1)S(1)} collective-permute-done((bf16[128,768]{1,0:T(8,128)(2,1)S(1)}, bf16[128,768]{1,0:T(8,128)(2,1)S(1)}, u32[]{:S(2)}, u32[]{:S(2)}) %collective-permute-start.24) | collective-permute-done | bytes 196640 | tf_op jit(solution)/shard_map/ppermute | solution.py:36
  143.2 4.0 %collective-permute-done.22.refs_1_ = bf16[128,768]{1,0:T(8,128)(2,1)S(1)} collective-permute-done((bf16[128,768]{1,0:T(8,128)(2,1)S(1)}, bf16[128,768]{1,0:T(8,128)(2,1)S(1)}, u32[]{:S(2)}, u32[]{:S(2)}) %collective-permute-start.22) | collective-permute-done | bytes 196640 | tf_op jit(solution)/shard_map/ppermute | solution.py:36
  151.2 4.1 %collective-permute-done.25.refs_1_ = bf16[128,768]{1,0:T(8,128)(2,1)S(1)} collective-permute-done((bf16[128,768]{1,0:T(8,128)(2,1)S(1)}, bf16[128,768]{1,0:T(8,128)(2,1)S(1)}, u32[]{:S(2)}, u32[]{:S(2)}) %collective-permute-start.25) | collective-permute-done | bytes 196640 | tf_op jit(solution)/shard_map/ppermute | solution.py:36
  155.3 3.7 %collective-permute-done.26.refs_2_ = bf16[128,768]{1,0:T(8,128)(2,1)S(1)} collective-permute-done((bf16[128,768]{1,0:T(8,128)(2,1)S(1)}, bf16[128,768]{1,0:T(8,128)(2,1)S(1)}, u32[]{:S(2)}, u32[]{:S(2)}) %collective-permute-start.26) | collective-permute-done | bytes 196640 | tf_op jit(solution)/shard_map/ppermute | solution.py:36
  160.7 26.0 %while.35 = (s32[]{:T(128)}, bf16[128,768]{1,0:T(8,128)(2,1)S(1)}, bf16[128,768]{1,0:T(8,128)(2,1)S(1)}, bf16[1024,768]{1,0:T(8,128)(2,1)S(1)}, s32[]{:T(128)}, ...) while((s32[]{:T(128)}, bf16[128,768]{1,0:T(8,128)(2,1)S(1)}, bf16[128,768]{1,0:T(8,128)(2,1)S(1)}, ...), condition=%wide.region_3.0_spmd, body=%wide.region_2.0_spmd.sunk | while | flops 12 | bytes 3146025 | solution.py:351
  163.6 2.9 %collective-permute-done.2 = bf16[128,768]{1,0:T(8,128)(2,1)S(1)} collective-permute-done((bf16[128,768]{1,0:T(8,128)(2,1)S(1)}, bf16[128,768]{1,0:T(8,128)(2,1)S(1)}, u32[]{:S(2)}, u32[]{:S(2)}) %collective-permute-start.2) | collective-permute-done | bytes 196640 | tf_op jit(solution)/shard_map/while/body/eval_jaxpr/ppermute | solution.py:28
  169.8 2.9 %collective-permute-done.2 = bf16[128,768]{1,0:T(8,128)(2,1)S(1)} collective-permute-done((bf16[128,768]{1,0:T(8,128)(2,1)S(1)}, bf16[128,768]{1,0:T(8,128)(2,1)S(1)}, u32[]{:S(2)}, u32[]{:S(2)}) %collective-permute-start.2) | collective-permute-done | bytes 196640 | tf_op jit(solution)/shard_map/while/body/eval_jaxpr/ppermute | solution.py:28
  175.9 2.9 %collective-permute-done.2 = bf16[128,768]{1,0:T(8,128)(2,1)S(1)} collective-permute-done((bf16[128,768]{1,0:T(8,128)(2,1)S(1)}, bf16[128,768]{1,0:T(8,128)(2,1)S(1)}, u32[]{:S(2)}, u32[]{:S(2)}) %collective-permute-start.2) | collective-permute-done | bytes 196640 | tf_op jit(solution)/shard_map/while/body/eval_jaxpr/ppermute | solution.py:28
  182.3 3.5 %collective-permute-done.2 = bf16[128,768]{1,0:T(8,128)(2,1)S(1)} collective-permute-done((bf16[128,768]{1,0:T(8,128)(2,1)S(1)}, bf16[128,768]{1,0:T(8,128)(2,1)S(1)}, u32[]{:S(2)}, u32[]{:S(2)}) %collective-permute-start.2) | collective-permute-done | bytes 196640 | tf_op jit(solution)/shard_map/while/body/eval_jaxpr/ppermute | solution.py:28
  186.7 7.4 %collective-permute-start.28 = (bf16[1024,768]{1,0:T(8,128)(2,1)S(1)}, bf16[1024,768]{1,0:T(8,128)(2,1)S(1)}, u32[]{:S(2)}, u32[]{:S(2)}) collective-permute-start(bf16[1024,768]{1,0:T(8,128)(2,1)S(1)} %constant_dynamic-update-slice_fusion.4.blocks_ref), channel_id=1, source_target_pairs={{0,16},{16,0},{1,17},{17,1},{2,18},{18,2},{3,19},{19,3},{4,20},{20... | collective-permute-start | bytes 4718600 | tf_op jit(solution)/shard_map/ppermute | solution.py:24
  (142 shorter events, 60.7 us)
Async XLA Ops:
  0.6 6.4 %collective-permute-start.5 = (bf16[256,2048]{1,0:T(8,128)(2,1)}, bf16[256,2048]{1,0:T(8,128)(2,1)S(1)}, u32[]{:S(2)}, u32[]{:S(2)}) collective-permute-start(bf16[256,2048]{1,0:T(8,128)(2,1)} %bitcast.16), channel_id=1, source_target_pairs={{0,16},{16,0},{1,17},{17,1},{2,18},{18,2},{3,19},{19,3},{4,20},{20... | collective-permute-start | bytes 3145736 | tf_op jit(solution)/shard_map/ppermute | solution.py:24
  12.7 9.1 %collective-permute-start.11 = (bf16[128,768]{1,0:T(8,128)(2,1)S(1)}, bf16[128,768]{1,0:T(8,128)(2,1)S(1)}, u32[]{:S(2)}, u32[]{:S(2)}) collective-permute-start(bf16[128,768]{1,0:T(8,128)(2,1)S(1)} %get-tuple-element.220), channel_id=1, source_target_pairs={{32,0},{64,32},{96,64},{128,96},{160,128},{192,160},{224,192},{0,2... | collective-permute-start | bytes 589832 | tf_op jit(solution)/shard_map/ppermute | solution.py:32
  16.6 8.0 %collective-permute-start.7 = (bf16[128,768]{1,0:T(8,128)(2,1)S(1)}, bf16[128,768]{1,0:T(8,128)(2,1)S(1)}, u32[]{:S(2)}, u32[]{:S(2)}) collective-permute-start(bf16[128,768]{1,0:T(8,128)(2,1)S(1)} %get-tuple-element.219), channel_id=1, source_target_pairs={{0,32},{32,64},{64,96},{96,128},{128,160},{160,192},{192,224},{224... | collective-permute-start | bytes 589832 | tf_op jit(solution)/shard_map/ppermute | solution.py:28
  21.9 10.2 %collective-permute-start.12 = (bf16[256,768]{1,0:T(8,128)(2,1)S(1)}, bf16[256,768]{1,0:T(8,128)(2,1)S(1)}, u32[]{:S(2)}, u32[]{:S(2)}) collective-permute-start(bf16[256,768]{1,0:T(8,128)(2,1)S(1)} %pad_maximum_fusion.1), channel_id=1, source_target_pairs={{32,0},{64,32},{96,64},{128,96},{160,128},{192,160},{224,192},{0,2... | collective-permute-start | bytes 1179656 | tf_op jit(solution)/shard_map/ppermute | solution.py:32
  24.7 11.0 %collective-permute-start.8 = (bf16[256,768]{1,0:T(8,128)(2,1)S(1)}, bf16[256,768]{1,0:T(8,128)(2,1)S(1)}, u32[]{:S(2)}, u32[]{:S(2)}) collective-permute-start(bf16[256,768]{1,0:T(8,128)(2,1)S(1)} %pad_maximum_fusion), channel_id=1, source_target_pairs={{0,32},{32,64},{64,96},{96,128},{128,160},{160,192},{192,224},{224... | collective-permute-start | bytes 1179656 | tf_op jit(solution)/shard_map/ppermute | solution.py:28
  32.2 10.1 %collective-permute-start.13 = (bf16[256,768]{1,0:T(8,128)(2,1)S(1)}, bf16[256,768]{1,0:T(8,128)(2,1)S(1)}, u32[]{:S(2)}, u32[]{:S(2)}) collective-permute-start(bf16[256,768]{1,0:T(8,128)(2,1)S(1)} %add_convert_fusion.1), channel_id=1, source_target_pairs={{32,0},{64,32},{96,64},{128,96},{160,128},{192,160},{224,192},{0,2... | collective-permute-start | bytes 1179656 | tf_op jit(solution)/shard_map/ppermute | solution.py:32
  35.8 10.1 %collective-permute-start.9 = (bf16[256,768]{1,0:T(8,128)(2,1)S(1)}, bf16[256,768]{1,0:T(8,128)(2,1)S(1)}, u32[]{:S(2)}, u32[]{:S(2)}) collective-permute-start(bf16[256,768]{1,0:T(8,128)(2,1)S(1)} %add_convert_fusion.3), channel_id=1, source_target_pairs={{0,32},{32,64},{64,96},{96,128},{128,160},{160,192},{192,224},{224... | collective-permute-start | bytes 1179656 | tf_op jit(solution)/shard_map/ppermute | solution.py:28
  42.4 9.1 %collective-permute-start.14 = (bf16[256,768]{1,0:T(8,128)(2,1)S(1)}, bf16[256,768]{1,0:T(8,128)(2,1)S(1)}, u32[]{:S(2)}, u32[]{:S(2)}) collective-permute-start(bf16[256,768]{1,0:T(8,128)(2,1)S(1)} %add_convert_fusion), channel_id=1, source_target_pairs={{32,0},{64,32},{96,64},{128,96},{160,128},{192,160},{224,192},{0,2... | collective-permute-start | bytes 1179656 | tf_op jit(solution)/shard_map/ppermute | solution.py:32
  46.0 8.9 %collective-permute-start.10 = (bf16[256,768]{1,0:T(8,128)(2,1)S(1)}, bf16[256,768]{1,0:T(8,128)(2,1)S(1)}, u32[]{:S(2)}, u32[]{:S(2)}) collective-permute-start(bf16[256,768]{1,0:T(8,128)(2,1)S(1)} %add_convert_fusion.2), channel_id=1, source_target_pairs={{0,32},{32,64},{64,96},{96,128},{128,160},{160,192},{192,224},{224... | collective-permute-start | bytes 1179656 | tf_op jit(solution)/shard_map/ppermute | solution.py:28
  55.0 7.6 %collective-permute-start.17 = (bf16[128,768]{1,0:T(8,128)(2,1)S(1)}, bf16[128,768]{1,0:T(8,128)(2,1)S(1)}, u32[]{:S(2)}, u32[]{:S(2)}) collective-permute-start(bf16[128,768]{1,0:T(8,128)(2,1)S(1)} %slice.43.refs_0_), channel_id=1, source_target_pairs={{0,3},{1,0},{2,1},{3,2},{4,7},{5,4},{6,5},{7,6},{8,11},{9,8},{10,9... | collective-permute-start | bytes 589832 | tf_op jit(solution)/shard_map/ppermute | solution.py:36
  57.9 6.1 %collective-permute-start.16 = (bf16[128,768]{1,0:T(8,128)(2,1)S(1)}, bf16[128,768]{1,0:T(8,128)(2,1)S(1)}, u32[]{:S(2)}, u32[]{:S(2)}) collective-permute-start(bf16[128,768]{1,0:T(8,128)(2,1)S(1)} %slice.43.refs_0_), channel_id=1, source_target_pairs={{0,2},{1,3},{2,0},{3,1},{4,6},{5,7},{6,4},{7,5},{8,10},{9,11},{10,... | collective-permute-start | bytes 589832 | tf_op jit(solution)/shard_map/ppermute | solution.py:36
  58.1 7.8 %collective-permute-start.15 = (bf16[128,768]{1,0:T(8,128)(2,1)S(1)}, bf16[128,768]{1,0:T(8,128)(2,1)S(1)}, u32[]{:S(2)}, u32[]{:S(2)}) collective-permute-start(bf16[128,768]{1,0:T(8,128)(2,1)S(1)} %slice.43.refs_0_), channel_id=1, source_target_pairs={{0,1},{1,2},{2,3},{3,0},{4,5},{5,6},{6,7},{7,4},{8,9},{9,10},{10,1... | collective-permute-start | bytes 589832 | tf_op jit(solution)/shard_map/ppermute | solution.py:36
  67.0 6.1 %collective-permute-start.18 = (bf16[128,768]{1,0:T(8,128)(2,1)S(1)}, bf16[128,768]{1,0:T(8,128)(2,1)S(1)}, u32[]{:S(2)}, u32[]{:S(2)}) collective-permute-start(bf16[128,768]{1,0:T(8,128)(2,1)S(1)} %get-tuple-element.188), channel_id=1, source_target_pairs={{0,8},{4,12},{8,0},{12,4},{1,9},{5,13},{9,1},{13,5},{2,10},{6,14},... | collective-permute-start | bytes 589832 | tf_op jit(solution)/shard_map/ppermute | solution.py:36
  75.9 6.1 %collective-permute-start = (bf16[128,768]{1,0:T(8,128)(2,1)S(1)}, bf16[128,768]{1,0:T(8,128)(2,1)S(1)}, u32[]{:S(2)}, u32[]{:S(2)}) collective-permute-start(bf16[128,768]{1,0:T(8,128)(2,1)S(1)} %copy.19), channel_id=1, source_target_pairs={{0,32},{32,64},{64,96},{96,128},{128,160},{160,192},{192,224},{224... | collective-permute-start | bytes 589832 | tf_op jit(solution)/shard_map/while/body/eval_jaxpr/ppermute | solution.py:28
  76.0 6.0 %collective-permute-start.1 = (bf16[128,768]{1,0:T(8,128)(2,1)S(1)}, bf16[128,768]{1,0:T(8,128)(2,1)S(1)}, u32[]{:S(2)}, u32[]{:S(2)}) collective-permute-start(bf16[128,768]{1,0:T(8,128)(2,1)S(1)} %copy.20), channel_id=1, source_target_pairs={{32,0},{64,32},{96,64},{128,96},{160,128},{192,160},{224,192},{0,2... | collective-permute-start | bytes 589832 | tf_op jit(solution)/shard_map/while/body/eval_jaxpr/ppermute | solution.py:32
  82.0 7.0 %collective-permute-start = (bf16[128,768]{1,0:T(8,128)(2,1)S(1)}, bf16[128,768]{1,0:T(8,128)(2,1)S(1)}, u32[]{:S(2)}, u32[]{:S(2)}) collective-permute-start(bf16[128,768]{1,0:T(8,128)(2,1)S(1)} %copy.19), channel_id=1, source_target_pairs={{0,32},{32,64},{64,96},{96,128},{128,160},{160,192},{192,224},{224... | collective-permute-start | bytes 589832 | tf_op jit(solution)/shard_map/while/body/eval_jaxpr/ppermute | solution.py:28
  82.1 6.9 %collective-permute-start.1 = (bf16[128,768]{1,0:T(8,128)(2,1)S(1)}, bf16[128,768]{1,0:T(8,128)(2,1)S(1)}, u32[]{:S(2)}, u32[]{:S(2)}) collective-permute-start(bf16[128,768]{1,0:T(8,128)(2,1)S(1)} %copy.20), channel_id=1, source_target_pairs={{32,0},{64,32},{96,64},{128,96},{160,128},{192,160},{224,192},{0,2... | collective-permute-start | bytes 589832 | tf_op jit(solution)/shard_map/while/body/eval_jaxpr/ppermute | solution.py:32
  89.0 6.1 %collective-permute-start = (bf16[128,768]{1,0:T(8,128)(2,1)S(1)}, bf16[128,768]{1,0:T(8,128)(2,1)S(1)}, u32[]{:S(2)}, u32[]{:S(2)}) collective-permute-start(bf16[128,768]{1,0:T(8,128)(2,1)S(1)} %copy.19), channel_id=1, source_target_pairs={{0,32},{32,64},{64,96},{96,128},{128,160},{160,192},{192,224},{224... | collective-permute-start | bytes 589832 | tf_op jit(solution)/shard_map/while/body/eval_jaxpr/ppermute | solution.py:28
  89.1 6.6 %collective-permute-start.1 = (bf16[128,768]{1,0:T(8,128)(2,1)S(1)}, bf16[128,768]{1,0:T(8,128)(2,1)S(1)}, u32[]{:S(2)}, u32[]{:S(2)}) collective-permute-start(bf16[128,768]{1,0:T(8,128)(2,1)S(1)} %copy.20), channel_id=1, source_target_pairs={{32,0},{64,32},{96,64},{128,96},{160,128},{192,160},{224,192},{0,2... | collective-permute-start | bytes 589832 | tf_op jit(solution)/shard_map/while/body/eval_jaxpr/ppermute | solution.py:32
  95.7 5.8 %collective-permute-start = (bf16[128,768]{1,0:T(8,128)(2,1)S(1)}, bf16[128,768]{1,0:T(8,128)(2,1)S(1)}, u32[]{:S(2)}, u32[]{:S(2)}) collective-permute-start(bf16[128,768]{1,0:T(8,128)(2,1)S(1)} %copy.19), channel_id=1, source_target_pairs={{0,32},{32,64},{64,96},{96,128},{128,160},{160,192},{192,224},{224... | collective-permute-start | bytes 589832 | tf_op jit(solution)/shard_map/while/body/eval_jaxpr/ppermute | solution.py:28
  101.8 13.6 %collective-permute-start.21 = (bf16[1024,768]{1,0:T(8,128)(2,1)S(1)}, bf16[1024,768]{1,0:T(8,128)(2,1)S(1)}, u32[]{:S(2)}, u32[]{:S(2)}) collective-permute-start(bf16[1024,768]{1,0:T(8,128)(2,1)S(1)} %constant_dynamic-update-slice_fusion.5), channel_id=1, source_target_pairs={{0,16},{16,0},{1,17},{17,1},{2,18},{18,2},{3,19},{19,3},{4,20},{20... | collective-permute-start | bytes 4718600 | tf_op jit(solution)/shard_map/ppermute | solution.py:24
  132.1 11.0 %collective-permute-start.24 = (bf16[128,768]{1,0:T(8,128)(2,1)S(1)}, bf16[128,768]{1,0:T(8,128)(2,1)S(1)}, u32[]{:S(2)}, u32[]{:S(2)}) collective-permute-start(bf16[128,768]{1,0:T(8,128)(2,1)S(1)} %get-tuple-element.194.refs_0_), channel_id=1, source_target_pairs={{0,12},{4,0},{8,4},{12,8},{1,13},{5,1},{9,5},{13,9},{2,14},{6,2},{... | collective-permute-start | bytes 589832 | tf_op jit(solution)/shard_map/ppermute | solution.py:36
  135.2 8.0 %collective-permute-start.23 = (bf16[128,768]{1,0:T(8,128)(2,1)S(1)}, bf16[128,768]{1,0:T(8,128)(2,1)S(1)}, u32[]{:S(2)}, u32[]{:S(2)}) collective-permute-start(bf16[128,768]{1,0:T(8,128)(2,1)S(1)} %get-tuple-element.194.refs_0_), channel_id=1, source_target_pairs={{0,8},{4,12},{8,0},{12,4},{1,9},{5,13},{9,1},{13,5},{2,10},{6,14},... | collective-permute-start | bytes 589832 | tf_op jit(solution)/shard_map/ppermute | solution.py:36
  135.2 11.9 %collective-permute-start.22 = (bf16[128,768]{1,0:T(8,128)(2,1)S(1)}, bf16[128,768]{1,0:T(8,128)(2,1)S(1)}, u32[]{:S(2)}, u32[]{:S(2)}) collective-permute-start(bf16[128,768]{1,0:T(8,128)(2,1)S(1)} %get-tuple-element.194.refs_0_), channel_id=1, source_target_pairs={{0,4},{4,8},{8,12},{12,0},{1,5},{5,9},{9,13},{13,1},{2,6},{6,10},{... | collective-permute-start | bytes 589832 | tf_op jit(solution)/shard_map/ppermute | solution.py:36
  147.8 7.5 %collective-permute-start.25 = (bf16[128,768]{1,0:T(8,128)(2,1)S(1)}, bf16[128,768]{1,0:T(8,128)(2,1)S(1)}, u32[]{:S(2)}, u32[]{:S(2)}) collective-permute-start(bf16[128,768]{1,0:T(8,128)(2,1)S(1)} %get-tuple-element.196), channel_id=1, source_target_pairs={{0,1},{1,2},{2,3},{3,0},{4,5},{5,6},{6,7},{7,4},{8,9},{9,10},{10,1... | collective-permute-start | bytes 589832 | tf_op jit(solution)/shard_map/ppermute | solution.py:36
  148.2 10.8 %collective-permute-start.26 = (bf16[128,768]{1,0:T(8,128)(2,1)S(1)}, bf16[128,768]{1,0:T(8,128)(2,1)S(1)}, u32[]{:S(2)}, u32[]{:S(2)}) collective-permute-start(bf16[128,768]{1,0:T(8,128)(2,1)S(1)} %get-tuple-element.197), channel_id=1, source_target_pairs={{0,2},{1,3},{2,0},{3,1},{4,6},{5,7},{6,4},{7,5},{8,10},{9,11},{10,... | collective-permute-start | bytes 589832 | tf_op jit(solution)/shard_map/ppermute | solution.py:36
  150.2 9.8 %collective-permute-start.27 = (bf16[128,768]{1,0:T(8,128)(2,1)S(1)}, bf16[128,768]{1,0:T(8,128)(2,1)S(1)}, u32[]{:S(2)}, u32[]{:S(2)}) collective-permute-start(bf16[128,768]{1,0:T(8,128)(2,1)S(1)} %get-tuple-element.198), channel_id=1, source_target_pairs={{0,3},{1,0},{2,1},{3,2},{4,7},{5,4},{6,5},{7,6},{8,11},{9,8},{10,9... | collective-permute-start | bytes 589832 | tf_op jit(solution)/shard_map/ppermute | solution.py:36
  160.7 5.8 %collective-permute-start.2 = (bf16[128,768]{1,0:T(8,128)(2,1)S(1)}, bf16[128,768]{1,0:T(8,128)(2,1)S(1)}, u32[]{:S(2)}, u32[]{:S(2)}) collective-permute-start(bf16[128,768]{1,0:T(8,128)(2,1)S(1)} %copy.32), channel_id=1, source_target_pairs={{0,32},{32,64},{64,96},{96,128},{128,160},{160,192},{192,224},{224... | collective-permute-start | bytes 589832 | tf_op jit(solution)/shard_map/while/body/eval_jaxpr/ppermute | solution.py:28
  166.9 5.8 %collective-permute-start.2 = (bf16[128,768]{1,0:T(8,128)(2,1)S(1)}, bf16[128,768]{1,0:T(8,128)(2,1)S(1)}, u32[]{:S(2)}, u32[]{:S(2)}) collective-permute-start(bf16[128,768]{1,0:T(8,128)(2,1)S(1)} %copy.32), channel_id=1, source_target_pairs={{0,32},{32,64},{64,96},{96,128},{128,160},{160,192},{192,224},{224... | collective-permute-start | bytes 589832 | tf_op jit(solution)/shard_map/while/body/eval_jaxpr/ppermute | solution.py:28
  179.4 6.4 %collective-permute-start.2 = (bf16[128,768]{1,0:T(8,128)(2,1)S(1)}, bf16[128,768]{1,0:T(8,128)(2,1)S(1)}, u32[]{:S(2)}, u32[]{:S(2)}) collective-permute-start(bf16[128,768]{1,0:T(8,128)(2,1)S(1)} %copy.32), channel_id=1, source_target_pairs={{0,32},{32,64},{64,96},{96,128},{128,160},{160,192},{192,224},{224... | collective-permute-start | bytes 589832 | tf_op jit(solution)/shard_map/while/body/eval_jaxpr/ppermute | solution.py:28
  180.4 6.3 %collective-permute-start.3 = (bf16[128,768]{1,0:T(8,128)(2,1)S(1)}, bf16[128,768]{1,0:T(8,128)(2,1)S(1)}, u32[]{:S(2)}, u32[]{:S(2)}) collective-permute-start(bf16[128,768]{1,0:T(8,128)(2,1)S(1)} %copy.33), channel_id=1, source_target_pairs={{32,0},{64,32},{96,64},{128,96},{160,128},{192,160},{224,192},{0,2... | collective-permute-start | bytes 589832 | tf_op jit(solution)/shard_map/while/body/eval_jaxpr/ppermute | solution.py:32
  186.7 10.4 %collective-permute-start.28 = (bf16[1024,768]{1,0:T(8,128)(2,1)S(1)}, bf16[1024,768]{1,0:T(8,128)(2,1)S(1)}, u32[]{:S(2)}, u32[]{:S(2)}) collective-permute-start(bf16[1024,768]{1,0:T(8,128)(2,1)S(1)} %constant_dynamic-update-slice_fusion.4.blocks_ref), channel_id=1, source_target_pairs={{0,16},{16,0},{1,17},{17,1},{2,18},{18,2},{3,19},{19,3},{4,20},{20... | collective-permute-start | bytes 4718600 | tf_op jit(solution)/shard_map/ppermute | solution.py:24
  (23 other events, 187.0 us)

commit v2 on v0

--- a/solution.py
+++ b/solution.py
@@ -16,6 +16,7 @@
 norm_eps = 1e-07
 
 NZ, NC, NX, NY = 8, 2, 4, 4
+FAR_LAST, FAR_FIRST = (0, 1, 3, 2), (0, 2, 1, 3)
 BF = jnp.bfloat16
 F32 = jnp.float32
 
@@ -88,7 +89,7 @@
     pieces, outs = refs[:NY], refs[NY:]
     x, y = here_ref[2], here_ref[3]
     totals = [jnp.zeros(outs[0].shape, F32) for _ in range(NX)]
-    for offset, piece in enumerate(pieces):
+    for offset, piece in zip(FAR_LAST, pieces, strict=True):
         target = list_ref[x * NY + lax.rem(y + NY - offset, NY)]
         value = piece[...].astype(F32)
         for ahead in range(NX):
@@ -116,7 +117,7 @@
     for offset, out in enumerate(outs):
         source = list_ref[x * NY + lax.rem(y + offset, NY)]
         behind = lax.rem(x + NX - lax.div(source, NY), NX)
-        for k, piece in enumerate(pieces):
+        for k, piece in zip(FAR_LAST, pieces, strict=True):
 
             @pl.when(behind == k)
             def _():
@@ -139,7 +140,7 @@
     pieces, out = refs[:NY], refs[NY]
     x, y = here_ref[2], here_ref[3]
     behind = lax.rem(y + NY - lax.rem(list_ref[x * NY + y], NY), NY)
-    for k, piece in enumerate(pieces):
+    for k, piece in zip(FAR_FIRST, pieces, strict=True):
 
         @pl.when(behind == k)
         def _():
@@ -190,6 +191,58 @@
         out_ref[rows:] = totals[1][span].astype(BF)
 
 
+def far_kernel(
+    here_ref, counts_ref, got_counts_ref, acts_ref, got_ref, grads_ref, got_grads_ref, out_ref, *scratch
+):
+    *held, sems = scratch
+    rows = out_ref.shape[0] // 2
+    z, core = here_ref[0], here_ref[1]
+    start = pl.multiple_of((NC * lax.rem(z + NZ // 2, NZ) + core) * rows, rows)
+    sources = (
+        acts_ref.at[:, pl.ds(start, rows)],
+        got_ref.at[:, pl.ds(start, rows)],
+        grads_ref,
+        got_grads_ref,
+    )
+    copies = [
+        pltpu.make_async_copy(source, target, sems.at[index])
+        for index, (source, target) in enumerate(zip(sources, held, strict=True))
+    ]
+    for copy in copies:
+        copy.start()
+    for copy in copies:
+        copy.wait()
+    acts, got, grads, got_grads = held
+    tok_rows, width = grads.shape
+    slot = lax.broadcasted_iota(jnp.int32, (tok_rows, width), 0)
+    for which in range(2):
+        total = jnp.zeros((rows, width), F32)
+        for left, value, counts in ((acts, grads, counts_ref), (got, got_grads, got_counts_ref)):
+            home, copy = counts[0, 0], counts[0, 1]
+            low, high = (0, home) if which else (home, home + copy)
+            right = jnp.where((slot >= low) & (slot < high), value[...].astype(F32), 0.0).astype(BF)
+            total = total + lax.dot_general(
+                left[...], right, (((0,), (0,)), ((), ())), preferred_element_type=F32
+            )
+        out_ref[which * rows : (which + 1) * rows] = total.astype(BF)
+
+
+def far_terms(here, counts, got_counts, acts, got, grads, got_grads):
+    tok_rows, width = grads.shape
+    rows = acts.shape[1] // (NZ * NC)
+    return pl.pallas_call(
+        far_kernel,
+        out_shape=jax.ShapeDtypeStruct((2 * rows, width), BF),
+        in_specs=[SMEM] * 3 + [HBM] * 4,
+        out_specs=VMEM,
+        scratch_shapes=[pltpu.VMEM((tok_rows, rows), BF)] * 2
+        + [pltpu.VMEM((tok_rows, width), BF)] * 2
+        + [pltpu.SemaphoreType.DMA((4,))],
+        compiler_params=small(56),
+        name="far_terms",
+    )(here, counts, got_counts, acts, got, grads, got_grads)
+
+
 def terms(here, counts, got_counts, acts, got, grads, got_grads, offsets):
     tok_rows, width = grads.shape
     rows = acts.shape[1] // (NZ * NC)
@@ -263,17 +316,19 @@
     same = lax.broadcasted_iota(jnp.int32, (tile, tile), 0) == lax.broadcasted_iota(
         jnp.int32, (tile, tile), 1
     )
-    total = jnp.zeros((1, 1), F32)
-    for span in spans:
-        value = gram_ref[span, :] + lax.dot_general(
+
+    def add_other(index, total):
+        span = pl.ds(pl.multiple_of(index * tile, tile), tile)
+        full_ref[span, :] = gram_ref[span, :] + lax.dot_general(
             other_ref[:, span],
             other_ref[...],
             (((0,), (0,)), ((), ())),
             preferred_element_type=F32,
         )
-        full_ref[span, :] = value
-        on = jnp.where(same, value[:, span], 0.0)
-        total = total + jnp.sum(jnp.sum(on, axis=1, keepdims=True), axis=0, keepdims=True)
+        on = jnp.where(same, full_ref[span, span], 0.0)
+        return total + jnp.sum(jnp.sum(on, axis=1, keepdims=True), axis=0, keepdims=True)
+
+    total = lax.fori_loop(0, 3, add_other, jnp.zeros((1, 1), F32))
     scale = 1.0 / (jnp.sqrt(total) + norm_eps)
 
     @pl.loop(0, width // CHUNK)
@@ -341,7 +396,8 @@
         below, above = up(below), down(above)
         return add_bf(below, on_up[step]), add_bf(above, on_down[step])
 
-    return lax.fori_loop(0, 3, one, (below, above))
+    below, above = lax.fori_loop(0, 3, one, (below, above))
+    return below.astype(F32) + above.astype(F32)
 
 
 def ring(block):
@@ -356,6 +412,15 @@
     got = jnp.zeros((NZ * rows, width), block.dtype)
     far, _, got = lax.fori_loop(0, 4, one, (block, block, got))
     return lax.dynamic_update_slice(got, far, (0, 0))
+
+
+def free_ring(block):
+    below, above = [block], [block]
+    for _ in range(3):
+        below.append(up(below[-1]))
+        above.append(down(above[-1]))
+    far = up(below[-1])
+    return jnp.concatenate([far, *below[:0:-1], *above], axis=0)
 
 
 def body(tokens_in, out_grads, counts, copy_list, weights, momentum):
@@ -366,15 +431,13 @@
     here = jnp.stack([lax.axis_index(name) for name in ("z", "core", "x", "y")]).astype(jnp.int32)
 
     tokens = (counts[0], swap(counts[0]), acts, swap(acts), grads, swap(grads))
-    (far,) = terms(here, *tokens, (4,))
+    far = far_terms(here, *tokens)
     near = terms(here, *tokens, (3, 2, 1, 0, -1, -2, -3))
-    below, above = ring_sum(far, near)
-    rows = below.shape[0] // 2
-    total = below.astype(F32) + above.astype(F32)
+    total = ring_sum(far, near)
+    rows = total.shape[0] // 2
     copy_sum, home_sum = total[:rows].astype(BF), total[rows:]
 
-    pieces = {offset: shift(copy_sum, "y", offset) for offset in (2, 1, 3)}
-    pieces = [copy_sum] + [pieces[offset] for offset in range(1, NY)]
+    pieces = [copy_sum] + [shift(copy_sum, "y", offset) for offset in FAR_LAST[1:]]
     copies, *sent = buckets(here, copy_list, pieces)
     for ahead in (2, 1, 3):
         copies = copies + shift(sent[ahead - 1], "x", ahead).astype(F32)
@@ -386,14 +449,12 @@
         gram, swap(own), fresh_mom, weights[0], max(model_width, width)
     )
 
-    pieces = {offset: shift(fresh, "x", offset) for offset in (2, 1, 3)}
-    pieces = [fresh] + [pieces[offset] for offset in range(1, NX)]
+    pieces = [fresh] + [shift(fresh, "x", offset) for offset in FAR_LAST[1:]]
     kept, *sent = wanted(here, copy_list, pieces)
-    pieces = {offset: shift(sent[offset - 1], "y", offset) for offset in (2, 1, 3)}
-    pieces = [kept] + [pieces[offset] for offset in range(1, NY)]
+    pieces = [kept] + [shift(sent[offset - 1], "y", offset) for offset in FAR_FIRST[1:]]
     replica = pick(here, copy_list, pieces)
 
-    own = ring(replica)
+    own = free_ring(replica)
     full = place(1, here, swap(own), place(0, here, own))
     return (fresh_mom[None], update[None], full[None])
 

time: 199 us -> 199 us (level)
  starting transfers between devices: 67.3 us -> 62.9 us
  Pallas kernels: 25.7 us -> 28.5 us
  local copies, waits for them, and re-layouts: 3.85 us -> 6.26 us
    ppermute x12, starting transfers between devices: 10.3 us -> 4.26 us  [up(): return lax.ppermute(value, 'z', [(i, (i + 1) % NZ) for i in range(NZ)])]
    ppermute x12 -> x11, starting transfers between devices: 21.3 us -> 25.2 us  [down(): return lax.ppermute(value, 'z', [((i + 1) % NZ, i) for i in range(NZ)])]
    ppermute x5, starting transfers between devices: 20.4 us -> 16.6 us  [swap(): return lax.ppermute(value, 'core', [(0, 1), (1, 0)])]
    pallas_call x0 -> x1, Pallas kernels: none -> 3.07 us  [far_terms(): pl.pallas_call(far_kernel, out_shape=jax.ShapeDtypeStruct((2 * rows, widt...]
    ppermute x12 -> x11, waiting for transfers between devices: 24.4 us -> 21.4 us  [down(): return lax.ppermute(value, 'z', [((i + 1) % NZ, i) for i in range(NZ)])]
    ppermute x12, waiting for transfers between devices: 33.9 us -> 36.4 us  [up(): return lax.ppermute(value, 'z', [(i, (i + 1) % NZ) for i in range(NZ)])]
    unnamed x16 -> x36, local copies, waits for them, and re-layouts: 2.93 us -> 4.68 us
  transfers between devices with their start and end apart: 41 -> 40, of which waited for: 33 -> 27; matrix products, arithmetic and copies ran while one was open for 2% -> 3% of each run, Pallas kernels for 2% -> 2%
where the time goes in v2:
time: 199 us
  waiting for transfers between devices  92.5 us (46%)
  starting transfers between devices  62.9 us (32%)
  Pallas kernels  28.5 us (14%)
  local copies, waits for them, and re-layouts  6.26 us (3%)
  other arithmetic  5.92 us (3%)
    ppermute x12, waiting for transfers between devices, up(): return lax.ppermute(value, 'z', [(i, (i + 1) % NZ) for i in range(NZ)])  36.4 us
    ppermute x12, waiting for transfers between devices, shift(): return lax.ppermute(value, axis, [(i, (i + offset) % 4) for i in range(4)])  30 us
    ppermute x11, starting transfers between devices, down(): return lax.ppermute(value, 'z', [((i + 1) % NZ, i) for i in range(NZ)])  25.2 us
    ppermute x11, waiting for transfers between devices, down(): return lax.ppermute(value, 'z', [((i + 1) % NZ, i) for i in range(NZ)])  21.4 us
    pallas_call x1, Pallas kernels, newton_schulz(): pl.pallas_call(functools.partial(newton_kernel, 0.2 * math.sqrt(longest))...  17.4 us
    ppermute x12, starting transfers between devices, shift(): return lax.ppermute(value, axis, [(i, (i + offset) % 4) for i in range(4)])  16.8 us
    ppermute x5, starting transfers between devices, swap(): return lax.ppermute(value, 'core', [(0, 1), (1, 0)])  16.6 us
    unnamed x36, local copies, waits for them, and re-layouts  4.68 us
  transfers between devices with their start and end apart: 40, of which 27 were waited for; matrix products, arithmetic and copies ran while one was open for 3% of the time, Pallas kernels for 2%

profile of v2, /device:TPU:1, one launch (start us, length us, event | category | flops | bytes accessed | tf_op | source)
XLA Modules:
  0.0 198.8 jit_solution(12727870889653977948)
XLA Ops:
  0.6 3.3 %collective-permute-start.5 = (bf16[256,2048]{1,0:T(8,128)(2,1)}, bf16[256,2048]{1,0:T(8,128)(2,1)S(1)}, u32[]{:S(2)}, u32[]{:S(2)}) collective-permute-start(bf16[256,2048]{1,0:T(8,128)(2,1)} %bitcast.32), channel_id=1, source_target_pairs={{0,16},{16,0},{1,17},{17,1},{2,18},{18,2},{3,19},{19,3},{4,20},{20... | collective-permute-start | bytes 3145736 | tf_op jit(solution)/shard_map/ppermute | solution.py:25
  8.7 3.1 %far_terms.1 = bf16[256,768]{1,0:T(8,128)(2,1)} custom-call(s32[4]{0:T(128)} %pad_add_fusion.here_ref, s32[1,2]{1,0:T(1,128)} %bitcast.45, s32[1,2]{1,0:T(1,128)} %copy-done.10, bf16[256,2048]{1,0:T(8,128)(2,1)} %bitcast.33, bf16[256,2048]{1,0:T(8,128)(2,1)} %copy-done.1, bf16[256,768]{1,0:T(8,128)(2,1)} %bitcast.36, bf16[256,768]{1,0:T(8,128)(2,1)} %copy-done.5), custom_call_target="tpu_custom_call" | custom-call | tf_op jit(solution)/shard_map/far_terms/pallas_call | solution.py:233
  12.9 3.9 %collective-permute-start.8 = (bf16[128,768]{1,0:T(8,128)(2,1)S(1)}, bf16[128,768]{1,0:T(8,128)(2,1)S(1)}, u32[]{:S(2)}, u32[]{:S(2)}) collective-permute-start(bf16[128,768]{1,0:T(8,128)(2,1)S(1)} %get-tuple-element.236), channel_id=1, source_target_pairs={{32,0},{64,32},{96,64},{128,96},{160,128},{192,160},{224,192},{0,2... | collective-permute-start | bytes 589832 | tf_op jit(solution)/shard_map/ppermute | solution.py:33
  24.7 33.4 %while.32 = (s32[]{:T(128)}, bf16[256,768]{1,0:T(8,128)(2,1)S(1)}, bf16[256,768]{1,0:T(8,128)(2,1)}, bf16[3,256,768]{2,1,0:T(8,128)(2,1)S(1)}, bf16[3,256,768]{2,1,0:T(8,128)(2,1)S(1)}, /*index=5*/s32[]{:T(128)}) while((s32[]{:T(128)}, bf16[256,768]{1,0:T(8,128)(2,1)S(1)}, bf16[256,768]{1,0:T(8,128)(2,1)}, bf16[3,256,768]{2,1,0:T(8,128)(2,1)S(1)}, ...), condition=%wide.region_1.0_spmd, body=%wide.region_0.0_spmd.sunk | while | flops 1572866 | bytes 5505189 | solution.py:399
  26.2 7.8 %collective-permute-done.1 = bf16[256,768]{1,0:T(8,128)(2,1)S(1)} collective-permute-done((bf16[256,768]{1,0:T(8,128)(2,1)}, bf16[256,768]{1,0:T(8,128)(2,1)S(1)}, u32[]{:S(2)}, u32[]{:S(2)}) %collective-permute-start.1) | collective-permute-done | bytes 393248 | tf_op jit(solution)/shard_map/while/body/eval_jaxpr/ppermute | solution.py:33
  38.1 7.2 %collective-permute-done.1 = bf16[256,768]{1,0:T(8,128)(2,1)S(1)} collective-permute-done((bf16[256,768]{1,0:T(8,128)(2,1)}, bf16[256,768]{1,0:T(8,128)(2,1)S(1)}, u32[]{:S(2)}, u32[]{:S(2)}) %collective-permute-start.1) | collective-permute-done | bytes 393248 | tf_op jit(solution)/shard_map/while/body/eval_jaxpr/ppermute | solution.py:33
  49.3 6.3 %collective-permute-done.1 = bf16[256,768]{1,0:T(8,128)(2,1)S(1)} collective-permute-done((bf16[256,768]{1,0:T(8,128)(2,1)}, bf16[256,768]{1,0:T(8,128)(2,1)S(1)}, u32[]{:S(2)}, u32[]{:S(2)}) %collective-permute-start.1) | collective-permute-done | bytes 393248 | tf_op jit(solution)/shard_map/while/body/eval_jaxpr/ppermute | solution.py:33
  59.3 2.9 %collective-permute-start.11 = (bf16[128,768]{1,0:T(8,128)(2,1)S(1)}, bf16[128,768]{1,0:T(8,128)(2,1)S(1)}, u32[]{:S(2)}, u32[]{:S(2)}) collective-permute-start(bf16[128,768]{1,0:T(8,128)(2,1)S(1)} %slice.43.refs_0_), channel_id=1, source_target_pairs={{0,2},{1,3},{2,0},{3,1},{4,6},{5,7},{6,4},{7,5},{8,10},{9,11},{10,... | collective-permute-start | bytes 589832 | tf_op jit(solution)/shard_map/ppermute | solution.py:37
  65.4 2.7 %collective-permute-done.10.refs_2_ = bf16[128,768]{1,0:T(8,128)(2,1)S(1)} collective-permute-done((bf16[128,768]{1,0:T(8,128)(2,1)S(1)}, bf16[128,768]{1,0:T(8,128)(2,1)S(1)}, u32[]{:S(2)}, u32[]{:S(2)}) %collective-permute-start.10) | collective-permute-done | bytes 196640 | tf_op jit(solution)/shard_map/ppermute | solution.py:37
  68.1 2.8 %collective-permute-done.9.refs_1_ = bf16[128,768]{1,0:T(8,128)(2,1)S(1)} collective-permute-done((bf16[128,768]{1,0:T(8,128)(2,1)S(1)}, bf16[128,768]{1,0:T(8,128)(2,1)S(1)}, u32[]{:S(2)}, u32[]{:S(2)}) %collective-permute-start.9) | collective-permute-done | bytes 196640 | tf_op jit(solution)/shard_map/ppermute | solution.py:37
  71.9 2.8 %collective-permute-start.12 = (bf16[128,768]{1,0:T(8,128)(2,1)S(1)}, bf16[128,768]{1,0:T(8,128)(2,1)S(1)}, u32[]{:S(2)}, u32[]{:S(2)}) collective-permute-start(bf16[128,768]{1,0:T(8,128)(2,1)S(1)} %get-tuple-element.205), channel_id=1, source_target_pairs={{0,8},{4,12},{8,0},{12,4},{1,9},{5,13},{9,1},{13,5},{2,10},{6,14},... | collective-permute-start | bytes 589832 | tf_op jit(solution)/shard_map/ppermute | solution.py:37
  78.0 4.6 %collective-permute-done.13 = bf16[128,768]{1,0:T(8,128)(2,1)S(1)} collective-permute-done((bf16[128,768]{1,0:T(8,128)(2,1)S(1)}, bf16[128,768]{1,0:T(8,128)(2,1)S(1)}, u32[]{:S(2)}, u32[]{:S(2)}) %collective-permute-start.13) | collective-permute-done | bytes 196640 | tf_op jit(solution)/shard_map/ppermute | solution.py:37
  82.9 26.3 %while.33 = (s32[]{:T(128)}, bf16[128,768]{1,0:T(8,128)(2,1)S(1)}, bf16[128,768]{1,0:T(8,128)(2,1)S(1)}, bf16[1024,768]{1,0:T(8,128)(2,1)S(1)}, s32[]{:T(128)}, ...) while((s32[]{:T(128)}, bf16[128,768]{1,0:T(8,128)(2,1)S(1)}, bf16[128,768]{1,0:T(8,128)(2,1)S(1)}, ...), condition=%wide.region_3.0_spmd, body=%wide.region_2.0_spmd.sunk | while | flops 12 | bytes 3146025 | solution.py:413
  83.0 2.7 %collective-permute-start.3 = (bf16[128,768]{1,0:T(8,128)(2,1)S(1)}, bf16[128,768]{1,0:T(8,128)(2,1)S(1)}, u32[]{:S(2)}, u32[]{:S(2)}) collective-permute-start(bf16[128,768]{1,0:T(8,128)(2,1)S(1)} %copy.27), channel_id=1, source_target_pairs={{32,0},{64,32},{96,64},{128,96},{160,128},{192,160},{224,192},{0,2... | collective-permute-start | bytes 589832 | tf_op jit(solution)/shard_map/while/body/eval_jaxpr/ppermute | solution.py:33
  85.8 2.9 %collective-permute-done.2 = bf16[128,768]{1,0:T(8,128)(2,1)S(1)} collective-permute-done((bf16[128,768]{1,0:T(8,128)(2,1)S(1)}, bf16[128,768]{1,0:T(8,128)(2,1)S(1)}, u32[]{:S(2)}, u32[]{:S(2)}) %collective-permute-start.2) | collective-permute-done | bytes 196640 | tf_op jit(solution)/shard_map/while/body/eval_jaxpr/ppermute | solution.py:29
  88.9 2.8 %collective-permute-start.3 = (bf16[128,768]{1,0:T(8,128)(2,1)S(1)}, bf16[128,768]{1,0:T(8,128)(2,1)S(1)}, u32[]{:S(2)}, u32[]{:S(2)}) collective-permute-start(bf16[128,768]{1,0:T(8,128)(2,1)S(1)} %copy.27), channel_id=1, source_target_pairs={{32,0},{64,32},{96,64},{128,96},{160,128},{192,160},{224,192},{0,2... | collective-permute-start | bytes 589832 | tf_op jit(solution)/shard_map/while/body/eval_jaxpr/ppermute | solution.py:33
  91.7 2.9 %collective-permute-done.2 = bf16[128,768]{1,0:T(8,128)(2,1)S(1)} collective-permute-done((bf16[128,768]{1,0:T(8,128)(2,1)S(1)}, bf16[128,768]{1,0:T(8,128)(2,1)S(1)}, u32[]{:S(2)}, u32[]{:S(2)}) %collective-permute-start.2) | collective-permute-done | bytes 196640 | tf_op jit(solution)/shard_map/while/body/eval_jaxpr/ppermute | solution.py:29
  97.7 3.5 %collective-permute-done.2 = bf16[128,768]{1,0:T(8,128)(2,1)S(1)} collective-permute-done((bf16[128,768]{1,0:T(8,128)(2,1)S(1)}, bf16[128,768]{1,0:T(8,128)(2,1)S(1)}, u32[]{:S(2)}, u32[]{:S(2)}) %collective-permute-start.2) | collective-permute-done | bytes 196640 | tf_op jit(solution)/shard_map/while/body/eval_jaxpr/ppermute | solution.py:29
  104.5 4.6 %collective-permute-done.2 = bf16[128,768]{1,0:T(8,128)(2,1)S(1)} collective-permute-done((bf16[128,768]{1,0:T(8,128)(2,1)S(1)}, bf16[128,768]{1,0:T(8,128)(2,1)S(1)}, u32[]{:S(2)}, u32[]{:S(2)}) %collective-permute-start.2) | collective-permute-done | bytes 196640 | tf_op jit(solution)/shard_map/while/body/eval_jaxpr/ppermute | solution.py:29
  109.2 8.2 %collective-permute-start.15 = (bf16[1024,768]{1,0:T(8,128)(2,1)S(1)}, bf16[1024,768]{1,0:T(8,128)(2,1)S(1)}, u32[]{:S(2)}, u32[]{:S(2)}) collective-permute-start(bf16[1024,768]{1,0:T(8,128)(2,1)S(1)} %constant_dynamic-update-slice_fusion.10), channel_id=1, source_target_pairs={{0,16},{16,0},{1,17},{17,1},{2,18},{18,2},{3,19},{19,3},{4,20},{20... | collective-permute-start | bytes 4718600 | tf_op jit(solution)/shard_map/ppermute | solution.py:25
  120.5 17.4 %newton_schulz.1 = (f32[128,768]{1,0:T(8,128)}, bf16[128,768]{1,0:T(8,128)(2,1)S(1)}) custom-call(f32[768,768]{1,0:T(8,128)S(1)} %fusion.6.gram_ref, bf16[1024,768]{1,0:T(8,128)(2,1)S(1)} %collective-permute-done.15.other_ref, f32[128,768]{1,0:T(8,128)S(1)} %get-tuple-element.235.mom_ref, bf16[128,768]{1,0:T(8,128)(2,1)S(1)} %bitcast.47), custom_call_target="tpu_custom_call" | custom-call | flops 12683575296 | bytes 4718592 | tf_op jit(solution)/shard_map/newton_schulz/pallas_call | solution.py:363
  142.0 3.5 %collective-permute-done.18.refs_3_ = bf16[128,768]{1,0:T(8,128)(2,1)S(1)} collective-permute-done((bf16[128,768]{1,0:T(8,128)(2,1)S(1)}, bf16[128,768]{1,0:T(8,128)(2,1)S(1)}, u32[]{:S(2)}, u32[]{:S(2)}) %collective-permute-start.18) | collective-permute-done | bytes 196640 | tf_op jit(solution)/shard_map/ppermute | solution.py:37
  145.5 4.7 %collective-permute-done.17.refs_2_ = bf16[128,768]{1,0:T(8,128)(2,1)S(1)} collective-permute-done((bf16[128,768]{1,0:T(8,128)(2,1)S(1)}, bf16[128,768]{1,0:T(8,128)(2,1)S(1)}, u32[]{:S(2)}, u32[]{:S(2)}) %collective-permute-start.17) | collective-permute-done | bytes 196640 | tf_op jit(solution)/shard_map/ppermute | solution.py:37
  153.8 4.0 %collective-permute-done.19.refs_1_ = bf16[128,768]{1,0:T(8,128)(2,1)S(1)} collective-permute-done((bf16[128,768]{1,0:T(8,128)(2,1)S(1)}, bf16[128,768]{1,0:T(8,128)(2,1)S(1)}, u32[]{:S(2)}, u32[]{:S(2)}) %collective-permute-start.19) | collective-permute-done | bytes 196640 | tf_op jit(solution)/shard_map/ppermute | solution.py:37
  157.8 5.3 %collective-permute-done.20.refs_2_ = bf16[128,768]{1,0:T(8,128)(2,1)S(1)} collective-permute-done((bf16[128,768]{1,0:T(8,128)(2,1)S(1)}, bf16[128,768]{1,0:T(8,128)(2,1)S(1)}, u32[]{:S(2)}, u32[]{:S(2)}) %collective-permute-start.20) | collective-permute-done | bytes 196640 | tf_op jit(solution)/shard_map/ppermute | solution.py:37
  164.8 6.6 %collective-permute-done.22 = bf16[128,768]{1,0:T(8,128)(2,1)S(1)} collective-permute-done((bf16[128,768]{1,0:T(8,128)(2,1)S(1)}, bf16[128,768]{1,0:T(8,128)(2,1)S(1)}, u32[]{:S(2)}, u32[]{:S(2)}) %collective-permute-start.22) | collective-permute-done | bytes 196640 | tf_op jit(solution)/shard_map/ppermute | solution.py:29
  174.0 3.6 %collective-permute-done.23 = bf16[128,768]{1,0:T(8,128)(2,1)S(1)} collective-permute-done((bf16[128,768]{1,0:T(8,128)(2,1)S(1)}, bf16[128,768]{1,0:T(8,128)(2,1)S(1)}, u32[]{:S(2)}, u32[]{:S(2)}) %collective-permute-start.23) | collective-permute-done | bytes 196640 | tf_op jit(solution)/shard_map/ppermute | solution.py:29
  177.6 2.7 %collective-permute-start.27 = (bf16[128,768]{1,0:T(8,128)(2,1)S(1)}, bf16[128,768]{1,0:T(8,128)(2,1)S(1)}, u32[]{:S(2)}, u32[]{:S(2)}) collective-permute-start(bf16[128,768]{1,0:T(8,128)(2,1)S(1)} %collective-permute-done.26), channel_id=1, source_target_pairs={{32,0},{64,32},{96,64},{128,96},{160,128},{192,160},{224,192},{0,2... | collective-permute-start | bytes 589832 | tf_op jit(solution)/shard_map/ppermute | solution.py:33
  180.3 3.0 %collective-permute-done.24 = bf16[128,768]{1,0:T(8,128)(2,1)S(1)} collective-permute-done((bf16[128,768]{1,0:T(8,128)(2,1)S(1)}, bf16[128,768]{1,0:T(8,128)(2,1)S(1)}, u32[]{:S(2)}, u32[]{:S(2)}) %collective-permute-start.24) | collective-permute-done | bytes 196640 | tf_op jit(solution)/shard_map/ppermute | solution.py:29
  183.4 2.7 %collective-permute-start.28 = (bf16[128,768]{1,0:T(8,128)(2,1)S(1)}, bf16[128,768]{1,0:T(8,128)(2,1)S(1)}, u32[]{:S(2)}, u32[]{:S(2)}) collective-permute-start(bf16[128,768]{1,0:T(8,128)(2,1)S(1)} %collective-permute-done.27), channel_id=1, source_target_pairs={{32,0},{64,32},{96,64},{128,96},{160,128},{192,160},{224,192},{0,2... | collective-permute-start | bytes 589832 | tf_op jit(solution)/shard_map/ppermute | solution.py:33
  186.0 3.0 %collective-permute-done.25 = bf16[128,768]{1,0:T(8,128)(2,1)S(1)} collective-permute-done((bf16[128,768]{1,0:T(8,128)(2,1)S(1)}, bf16[128,768]{1,0:T(8,128)(2,1)S(1)}, u32[]{:S(2)}, u32[]{:S(2)}) %collective-permute-start.25) | collective-permute-done | bytes 196640 | tf_op jit(solution)/shard_map/ppermute | solution.py:29
  189.3 4.6 %collective-permute-start.29 = (bf16[1024,768]{1,0:T(8,128)(2,1)S(1)}, bf16[1024,768]{1,0:T(8,128)(2,1)S(1)}, u32[]{:S(2)}, u32[]{:S(2)}) collective-permute-start(bf16[1024,768]{1,0:T(8,128)(2,1)S(1)} %constant_dynamic-update-slice_fusion.2.blocks_ref), channel_id=1, source_target_pairs={{0,16},{16,0},{1,17},{17,1},{2,18},{18,2},{3,19},{19,3},{4,20},{20... | collective-permute-start | bytes 4718600 | tf_op jit(solution)/shard_map/ppermute | solution.py:25
  (133 shorter events, 61.1 us)
Async XLA Ops:
  0.6 6.4 %collective-permute-start.5 = (bf16[256,2048]{1,0:T(8,128)(2,1)}, bf16[256,2048]{1,0:T(8,128)(2,1)S(1)}, u32[]{:S(2)}, u32[]{:S(2)}) collective-permute-start(bf16[256,2048]{1,0:T(8,128)(2,1)} %bitcast.32), channel_id=1, source_target_pairs={{0,16},{16,0},{1,17},{17,1},{2,18},{18,2},{3,19},{19,3},{4,20},{20... | collective-permute-start | bytes 3145736 | tf_op jit(solution)/shard_map/ppermute | solution.py:25
  12.9 11.0 %collective-permute-start.8 = (bf16[128,768]{1,0:T(8,128)(2,1)S(1)}, bf16[128,768]{1,0:T(8,128)(2,1)S(1)}, u32[]{:S(2)}, u32[]{:S(2)}) collective-permute-start(bf16[128,768]{1,0:T(8,128)(2,1)S(1)} %get-tuple-element.236), channel_id=1, source_target_pairs={{32,0},{64,32},{96,64},{128,96},{160,128},{192,160},{224,192},{0,2... | collective-permute-start | bytes 589832 | tf_op jit(solution)/shard_map/ppermute | solution.py:33
  16.8 7.0 %collective-permute-start.7 = (bf16[128,768]{1,0:T(8,128)(2,1)S(1)}, bf16[128,768]{1,0:T(8,128)(2,1)S(1)}, u32[]{:S(2)}, u32[]{:S(2)}) collective-permute-start(bf16[128,768]{1,0:T(8,128)(2,1)S(1)} %get-tuple-element.237), channel_id=1, source_target_pairs={{0,32},{32,64},{64,96},{96,128},{128,160},{160,192},{192,224},{224... | collective-permute-start | bytes 589832 | tf_op jit(solution)/shard_map/ppermute | solution.py:29
  24.7 9.3 %collective-permute-start.1 = (bf16[256,768]{1,0:T(8,128)(2,1)}, bf16[256,768]{1,0:T(8,128)(2,1)S(1)}, u32[]{:S(2)}, u32[]{:S(2)}) collective-permute-start(bf16[256,768]{1,0:T(8,128)(2,1)} %get-tuple-element.304), channel_id=1, source_target_pairs={{32,0},{64,32},{96,64},{128,96},{160,128},{192,160},{224,192},{0,2... | collective-permute-start | bytes 1179656 | tf_op jit(solution)/shard_map/while/body/eval_jaxpr/ppermute | solution.py:33
  25.8 10.6 %collective-permute-start = (bf16[256,768]{1,0:T(8,128)(2,1)S(1)}, bf16[256,768]{1,0:T(8,128)(2,1)S(1)}, u32[]{:S(2)}, u32[]{:S(2)}) collective-permute-start(bf16[256,768]{1,0:T(8,128)(2,1)S(1)} %get-tuple-element.303), channel_id=1, source_target_pairs={{0,32},{32,64},{64,96},{96,128},{128,160},{160,192},{192,224},{224... | collective-permute-start | bytes 1179656 | tf_op jit(solution)/shard_map/while/body/eval_jaxpr/ppermute | solution.py:29
  36.5 8.8 %collective-permute-start.1 = (bf16[256,768]{1,0:T(8,128)(2,1)}, bf16[256,768]{1,0:T(8,128)(2,1)S(1)}, u32[]{:S(2)}, u32[]{:S(2)}) collective-permute-start(bf16[256,768]{1,0:T(8,128)(2,1)} %get-tuple-element.304), channel_id=1, source_target_pairs={{32,0},{64,32},{96,64},{128,96},{160,128},{192,160},{224,192},{0,2... | collective-permute-start | bytes 1179656 | tf_op jit(solution)/shard_map/while/body/eval_jaxpr/ppermute | solution.py:33
  37.9 9.7 %collective-permute-start = (bf16[256,768]{1,0:T(8,128)(2,1)S(1)}, bf16[256,768]{1,0:T(8,128)(2,1)S(1)}, u32[]{:S(2)}, u32[]{:S(2)}) collective-permute-start(bf16[256,768]{1,0:T(8,128)(2,1)S(1)} %get-tuple-element.303), channel_id=1, source_target_pairs={{0,32},{32,64},{64,96},{96,128},{128,160},{160,192},{192,224},{224... | collective-permute-start | bytes 1179656 | tf_op jit(solution)/shard_map/while/body/eval_jaxpr/ppermute | solution.py:29
  47.8 7.9 %collective-permute-start.1 = (bf16[256,768]{1,0:T(8,128)(2,1)}, bf16[256,768]{1,0:T(8,128)(2,1)S(1)}, u32[]{:S(2)}, u32[]{:S(2)}) collective-permute-start(bf16[256,768]{1,0:T(8,128)(2,1)} %get-tuple-element.304), channel_id=1, source_target_pairs={{32,0},{64,32},{96,64},{128,96},{160,128},{192,160},{224,192},{0,2... | collective-permute-start | bytes 1179656 | tf_op jit(solution)/shard_map/while/body/eval_jaxpr/ppermute | solution.py:33
  49.2 8.8 %collective-permute-start = (bf16[256,768]{1,0:T(8,128)(2,1)S(1)}, bf16[256,768]{1,0:T(8,128)(2,1)S(1)}, u32[]{:S(2)}, u32[]{:S(2)}) collective-permute-start(bf16[256,768]{1,0:T(8,128)(2,1)S(1)} %get-tuple-element.303), channel_id=1, source_target_pairs={{0,32},{32,64},{64,96},{96,128},{128,160},{160,192},{192,224},{224... | collective-permute-start | bytes 1179656 | tf_op jit(solution)/shard_map/while/body/eval_jaxpr/ppermute | solution.py:29
  59.3 6.1 %collective-permute-start.11 = (bf16[128,768]{1,0:T(8,128)(2,1)S(1)}, bf16[128,768]{1,0:T(8,128)(2,1)S(1)}, u32[]{:S(2)}, u32[]{:S(2)}) collective-permute-start(bf16[128,768]{1,0:T(8,128)(2,1)S(1)} %slice.43.refs_0_), channel_id=1, source_target_pairs={{0,2},{1,3},{2,0},{3,1},{4,6},{5,7},{6,4},{7,5},{8,10},{9,11},{10,... | collective-permute-start | bytes 589832 | tf_op jit(solution)/shard_map/ppermute | solution.py:37
  62.2 5.9 %collective-permute-start.10 = (bf16[128,768]{1,0:T(8,128)(2,1)S(1)}, bf16[128,768]{1,0:T(8,128)(2,1)S(1)}, u32[]{:S(2)}, u32[]{:S(2)}) collective-permute-start(bf16[128,768]{1,0:T(8,128)(2,1)S(1)} %slice.43.refs_0_), channel_id=1, source_target_pairs={{0,3},{1,0},{2,1},{3,2},{4,7},{5,4},{6,5},{7,6},{8,11},{9,8},{10,9... | collective-permute-start | bytes 589832 | tf_op jit(solution)/shard_map/ppermute | solution.py:37
  63.1 7.8 %collective-permute-start.9 = (bf16[128,768]{1,0:T(8,128)(2,1)S(1)}, bf16[128,768]{1,0:T(8,128)(2,1)S(1)}, u32[]{:S(2)}, u32[]{:S(2)}) collective-permute-start(bf16[128,768]{1,0:T(8,128)(2,1)S(1)} %slice.43.refs_0_), channel_id=1, source_target_pairs={{0,1},{1,2},{2,3},{3,0},{4,5},{5,6},{6,7},{7,4},{8,9},{9,10},{10,1... | collective-permute-start | bytes 589832 | tf_op jit(solution)/shard_map/ppermute | solution.py:37
  71.9 6.1 %collective-permute-start.12 = (bf16[128,768]{1,0:T(8,128)(2,1)S(1)}, bf16[128,768]{1,0:T(8,128)(2,1)S(1)}, u32[]{:S(2)}, u32[]{:S(2)}) collective-permute-start(bf16[128,768]{1,0:T(8,128)(2,1)S(1)} %get-tuple-element.205), channel_id=1, source_target_pairs={{0,8},{4,12},{8,0},{12,4},{1,9},{5,13},{9,1},{13,5},{2,10},{6,14},... | collective-permute-start | bytes 589832 | tf_op jit(solution)/shard_map/ppermute | solution.py:37
  74.7 7.9 %collective-permute-start.13 = (bf16[128,768]{1,0:T(8,128)(2,1)S(1)}, bf16[128,768]{1,0:T(8,128)(2,1)S(1)}, u32[]{:S(2)}, u32[]{:S(2)}) collective-permute-start(bf16[128,768]{1,0:T(8,128)(2,1)S(1)} %get-tuple-element.206), channel_id=1, source_target_pairs={{0,4},{4,8},{8,12},{12,0},{1,5},{5,9},{9,13},{13,1},{2,6},{6,10},{... | collective-permute-start | bytes 589832 | tf_op jit(solution)/shard_map/ppermute | solution.py:37
  75.0 7.6 %collective-permute-start.14 = (bf16[128,768]{1,0:T(8,128)(2,1)S(1)}, bf16[128,768]{1,0:T(8,128)(2,1)S(1)}, u32[]{:S(2)}, u32[]{:S(2)}) collective-permute-start(bf16[128,768]{1,0:T(8,128)(2,1)S(1)} %get-tuple-element.207), channel_id=1, source_target_pairs={{0,12},{4,0},{8,4},{12,8},{1,13},{5,1},{9,5},{13,9},{2,14},{6,2},{... | collective-permute-start | bytes 589832 | tf_op jit(solution)/shard_map/ppermute | solution.py:37
  82.9 5.8 %collective-permute-start.2 = (bf16[128,768]{1,0:T(8,128)(2,1)S(1)}, bf16[128,768]{1,0:T(8,128)(2,1)S(1)}, u32[]{:S(2)}, u32[]{:S(2)}) collective-permute-start(bf16[128,768]{1,0:T(8,128)(2,1)S(1)} %copy.26), channel_id=1, source_target_pairs={{0,32},{32,64},{64,96},{96,128},{128,160},{160,192},{192,224},{224... | collective-permute-start | bytes 589832 | tf_op jit(solution)/shard_map/while/body/eval_jaxpr/ppermute | solution.py:29
  88.7 5.9 %collective-permute-start.2 = (bf16[128,768]{1,0:T(8,128)(2,1)S(1)}, bf16[128,768]{1,0:T(8,128)(2,1)S(1)}, u32[]{:S(2)}, u32[]{:S(2)}) collective-permute-start(bf16[128,768]{1,0:T(8,128)(2,1)S(1)} %copy.26), channel_id=1, source_target_pairs={{0,32},{32,64},{64,96},{96,128},{128,160},{160,192},{192,224},{224... | collective-permute-start | bytes 589832 | tf_op jit(solution)/shard_map/while/body/eval_jaxpr/ppermute | solution.py:29
  94.7 6.5 %collective-permute-start.2 = (bf16[128,768]{1,0:T(8,128)(2,1)S(1)}, bf16[128,768]{1,0:T(8,128)(2,1)S(1)}, u32[]{:S(2)}, u32[]{:S(2)}) collective-permute-start(bf16[128,768]{1,0:T(8,128)(2,1)S(1)} %copy.26), channel_id=1, source_target_pairs={{0,32},{32,64},{64,96},{96,128},{128,160},{160,192},{192,224},{224... | collective-permute-start | bytes 589832 | tf_op jit(solution)/shard_map/while/body/eval_jaxpr/ppermute | solution.py:29
  101.2 7.9 %collective-permute-start.2 = (bf16[128,768]{1,0:T(8,128)(2,1)S(1)}, bf16[128,768]{1,0:T(8,128)(2,1)S(1)}, u32[]{:S(2)}, u32[]{:S(2)}) collective-permute-start(bf16[128,768]{1,0:T(8,128)(2,1)S(1)} %copy.26), channel_id=1, source_target_pairs={{0,32},{32,64},{64,96},{96,128},{128,160},{160,192},{192,224},{224... | collective-permute-start | bytes 589832 | tf_op jit(solution)/shard_map/while/body/eval_jaxpr/ppermute | solution.py:29
  102.2 7.0 %collective-permute-start.3 = (bf16[128,768]{1,0:T(8,128)(2,1)S(1)}, bf16[128,768]{1,0:T(8,128)(2,1)S(1)}, u32[]{:S(2)}, u32[]{:S(2)}) collective-permute-start(bf16[128,768]{1,0:T(8,128)(2,1)S(1)} %copy.27), channel_id=1, source_target_pairs={{32,0},{64,32},{96,64},{128,96},{160,128},{192,160},{224,192},{0,2... | collective-permute-start | bytes 589832 | tf_op jit(solution)/shard_map/while/body/eval_jaxpr/ppermute | solution.py:33
  109.2 11.2 %collective-permute-start.15 = (bf16[1024,768]{1,0:T(8,128)(2,1)S(1)}, bf16[1024,768]{1,0:T(8,128)(2,1)S(1)}, u32[]{:S(2)}, u32[]{:S(2)}) collective-permute-start(bf16[1024,768]{1,0:T(8,128)(2,1)S(1)} %constant_dynamic-update-slice_fusion.10), channel_id=1, source_target_pairs={{0,16},{16,0},{1,17},{17,1},{2,18},{18,2},{3,19},{19,3},{4,20},{20... | collective-permute-start | bytes 4718600 | tf_op jit(solution)/shard_map/ppermute | solution.py:25
  137.9 7.6 %collective-permute-start.18 = (bf16[128,768]{1,0:T(8,128)(2,1)S(1)}, bf16[128,768]{1,0:T(8,128)(2,1)S(1)}, u32[]{:S(2)}, u32[]{:S(2)}) collective-permute-start(bf16[128,768]{1,0:T(8,128)(2,1)S(1)} %get-tuple-element.211.refs_0_), channel_id=1, source_target_pairs={{0,8},{4,12},{8,0},{12,4},{1,9},{5,13},{9,1},{13,5},{2,10},{6,14},... | collective-permute-start | bytes 589832 | tf_op jit(solution)/shard_map/ppermute | solution.py:37
  140.2 10.0 %collective-permute-start.17 = (bf16[128,768]{1,0:T(8,128)(2,1)S(1)}, bf16[128,768]{1,0:T(8,128)(2,1)S(1)}, u32[]{:S(2)}, u32[]{:S(2)}) collective-permute-start(bf16[128,768]{1,0:T(8,128)(2,1)S(1)} %get-tuple-element.211.refs_0_), channel_id=1, source_target_pairs={{0,12},{4,0},{8,4},{12,8},{1,13},{5,1},{9,5},{13,9},{2,14},{6,2},{... | collective-permute-start | bytes 589832 | tf_op jit(solution)/shard_map/ppermute | solution.py:37
  142.0 8.2 %collective-permute-start.16 = (bf16[128,768]{1,0:T(8,128)(2,1)S(1)}, bf16[128,768]{1,0:T(8,128)(2,1)S(1)}, u32[]{:S(2)}, u32[]{:S(2)}) collective-permute-start(bf16[128,768]{1,0:T(8,128)(2,1)S(1)} %get-tuple-element.211.refs_0_), channel_id=1, source_target_pairs={{0,4},{4,8},{8,12},{12,0},{1,5},{5,9},{9,13},{13,1},{2,6},{6,10},{... | collective-permute-start | bytes 589832 | tf_op jit(solution)/shard_map/ppermute | solution.py:37
  150.9 6.9 %collective-permute-start.19 = (bf16[128,768]{1,0:T(8,128)(2,1)S(1)}, bf16[128,768]{1,0:T(8,128)(2,1)S(1)}, u32[]{:S(2)}, u32[]{:S(2)}) collective-permute-start(bf16[128,768]{1,0:T(8,128)(2,1)S(1)} %get-tuple-element.213), channel_id=1, source_target_pairs={{0,2},{1,3},{2,0},{3,1},{4,6},{5,7},{6,4},{7,5},{8,10},{9,11},{10,... | collective-permute-start | bytes 589832 | tf_op jit(solution)/shard_map/ppermute | solution.py:37
  151.0 12.1 %collective-permute-start.20 = (bf16[128,768]{1,0:T(8,128)(2,1)S(1)}, bf16[128,768]{1,0:T(8,128)(2,1)S(1)}, u32[]{:S(2)}, u32[]{:S(2)}) collective-permute-start(bf16[128,768]{1,0:T(8,128)(2,1)S(1)} %get-tuple-element.214), channel_id=1, source_target_pairs={{0,1},{1,2},{2,3},{3,0},{4,5},{5,6},{6,7},{7,4},{8,9},{9,10},{10,1... | collective-permute-start | bytes 589832 | tf_op jit(solution)/shard_map/ppermute | solution.py:37
  151.1 12.0 %collective-permute-start.21 = (bf16[128,768]{1,0:T(8,128)(2,1)S(1)}, bf16[128,768]{1,0:T(8,128)(2,1)S(1)}, u32[]{:S(2)}, u32[]{:S(2)}) collective-permute-start(bf16[128,768]{1,0:T(8,128)(2,1)S(1)} %get-tuple-element.215), channel_id=1, source_target_pairs={{0,3},{1,0},{2,1},{3,2},{4,7},{5,4},{6,5},{7,6},{8,11},{9,8},{10,9... | collective-permute-start | bytes 589832 | tf_op jit(solution)/shard_map/ppermute | solution.py:37
  163.7 7.6 %collective-permute-start.22 = (bf16[128,768]{1,0:T(8,128)(2,1)S(1)}, bf16[128,768]{1,0:T(8,128)(2,1)S(1)}, u32[]{:S(2)}, u32[]{:S(2)}) collective-permute-start(bf16[128,768]{1,0:T(8,128)(2,1)S(1)} %pick.1), channel_id=1, source_target_pairs={{0,32},{32,64},{64,96},{96,128},{128,160},{160,192},{192,224},{224... | collective-permute-start | bytes 589832 | tf_op jit(solution)/shard_map/ppermute | solution.py:29
  171.3 6.3 %collective-permute-start.23 = (bf16[128,768]{1,0:T(8,128)(2,1)S(1)}, bf16[128,768]{1,0:T(8,128)(2,1)S(1)}, u32[]{:S(2)}, u32[]{:S(2)}) collective-permute-start(bf16[128,768]{1,0:T(8,128)(2,1)S(1)} %collective-permute-done.22), channel_id=1, source_target_pairs={{0,32},{32,64},{64,96},{96,128},{128,160},{160,192},{192,224},{224... | collective-permute-start | bytes 589832 | tf_op jit(solution)/shard_map/ppermute | solution.py:29
  171.3 6.3 %collective-permute-start.26 = (bf16[128,768]{1,0:T(8,128)(2,1)S(1)}, bf16[128,768]{1,0:T(8,128)(2,1)S(1)}, u32[]{:S(2)}, u32[]{:S(2)}) collective-permute-start(bf16[128,768]{1,0:T(8,128)(2,1)S(1)} %pick.1), channel_id=1, source_target_pairs={{32,0},{64,32},{96,64},{128,96},{160,128},{192,160},{224,192},{0,2... | collective-permute-start | bytes 589832 | tf_op jit(solution)/shard_map/ppermute | solution.py:33
  183.4 5.9 %collective-permute-start.28 = (bf16[128,768]{1,0:T(8,128)(2,1)S(1)}, bf16[128,768]{1,0:T(8,128)(2,1)S(1)}, u32[]{:S(2)}, u32[]{:S(2)}) collective-permute-start(bf16[128,768]{1,0:T(8,128)(2,1)S(1)} %collective-permute-done.27), channel_id=1, source_target_pairs={{32,0},{64,32},{96,64},{128,96},{160,128},{192,160},{224,192},{0,2... | collective-permute-start | bytes 589832 | tf_op jit(solution)/shard_map/ppermute | solution.py:33
  189.3 7.6 %collective-permute-start.29 = (bf16[1024,768]{1,0:T(8,128)(2,1)S(1)}, bf16[1024,768]{1,0:T(8,128)(2,1)S(1)}, u32[]{:S(2)}, u32[]{:S(2)}) collective-permute-start(bf16[1024,768]{1,0:T(8,128)(2,1)S(1)} %constant_dynamic-update-slice_fusion.2.blocks_ref), channel_id=1, source_target_pairs={{0,16},{16,0},{1,17},{17,1},{2,18},{18,2},{3,19},{19,3},{4,20},{20... | collective-permute-start | bytes 4718600 | tf_op jit(solution)/shard_map/ppermute | solution.py:25
  (22 other events, 177.6 us)

commit v3 on v1

--- a/solution.py
+++ b/solution.py
@@ -16,6 +16,7 @@
 norm_eps = 1e-07
 
 NZ, NC, NX, NY = 8, 2, 4, 4
+FAR_LAST, FAR_FIRST = (0, 1, 3, 2), (0, 2, 1, 3)
 BF = jnp.bfloat16
 F32 = jnp.float32
 
@@ -43,7 +44,6 @@
 SMEM = pl.BlockSpec(memory_space=pltpu.SMEM)
 VMEM = pl.BlockSpec(memory_space=pltpu.VMEM)
 ANY = pl.BlockSpec(memory_space=pl.ANY)
-HBM = pl.BlockSpec(memory_space=pltpu.HBM)
 
 
 def small(limit=8):
@@ -88,7 +88,7 @@
     pieces, outs = refs[:NY], refs[NY:]
     x, y = here_ref[2], here_ref[3]
     totals = [jnp.zeros(outs[0].shape, F32) for _ in range(NX)]
-    for offset, piece in enumerate(pieces):
+    for offset, piece in zip(FAR_LAST, pieces, strict=True):
         target = list_ref[x * NY + lax.rem(y + NY - offset, NY)]
         value = piece[...].astype(F32)
         for ahead in range(NX):
@@ -116,7 +116,7 @@
     for offset, out in enumerate(outs):
         source = list_ref[x * NY + lax.rem(y + offset, NY)]
         behind = lax.rem(x + NX - lax.div(source, NY), NX)
-        for k, piece in enumerate(pieces):
+        for k, piece in zip(FAR_LAST, pieces, strict=True):
 
             @pl.when(behind == k)
             def _():
@@ -139,7 +139,7 @@
     pieces, out = refs[:NY], refs[NY]
     x, y = here_ref[2], here_ref[3]
     behind = lax.rem(y + NY - lax.rem(list_ref[x * NY + y], NY), NY)
-    for k, piece in enumerate(pieces):
+    for k, piece in zip(FAR_FIRST, pieces, strict=True):
 
         @pl.when(behind == k)
         def _():
@@ -190,6 +190,44 @@
         out_ref[rows:] = totals[1][span].astype(BF)
 
 
+def far_kernel(here_ref, counts_ref, acts_ref, grads_ref, *refs):
+    *before, copy_ref, home_ref = refs
+    rows = copy_ref.shape[0]
+    tok_rows, width = grads_ref.shape
+    z, core = here_ref[0], here_ref[1]
+    start = pl.multiple_of((NC * lax.rem(z + NZ // 2, NZ) + core) * rows, rows)
+    left = acts_ref[:, pl.ds(start, rows)]
+    slot = lax.broadcasted_iota(jnp.int32, (tok_rows, width), 0)
+    home, copy = counts_ref[0, 0], counts_ref[0, 1]
+    value = grads_ref[...].astype(F32)
+    for which, (low, high, out_ref) in enumerate(
+        ((home, home + copy, copy_ref), (0, home, home_ref))
+    ):
+        right = jnp.where((slot >= low) & (slot < high), value, 0.0).astype(BF)
+        total = lax.dot_general(
+            left, right, (((0,), (0,)), ((), ())), preferred_element_type=F32
+        )
+        if before:
+            total = total + before[which][...]
+        out_ref[...] = total.astype(out_ref.dtype)
+
+
+def far_terms(here, counts, acts, grads, before=()):
+    tok_rows, width = grads.shape
+    rows = acts.shape[1] // (NZ * NC)
+    return pl.pallas_call(
+        far_kernel,
+        out_shape=(jax.ShapeDtypeStruct((rows, width), BF if before else F32),) * 2,
+        in_specs=[SMEM] * 2 + [VMEM] * (2 + len(before)),
+        out_specs=(VMEM, VMEM),
+        compiler_params=small(),
+        cost_estimate=pl.CostEstimate(
+            flops=4 * tok_rows * rows * width, bytes_accessed=4 * tok_rows * width, transcendentals=0
+        ),
+        name="far_terms",
+    )(here, counts, acts, grads, *before)
+
+
 def terms(here, counts, got_counts, acts, got, grads, got_grads, offsets):
     tok_rows, width = grads.shape
     rows = acts.shape[1] // (NZ * NC)
@@ -198,7 +236,7 @@
         out_shape=(jax.ShapeDtypeStruct((2 * rows, width), BF),) * len(offsets),
         in_specs=[SMEM] * 3 + [VMEM] * 4,
         out_specs=(VMEM,) * len(offsets),
-        compiler_params=small(56 if len(offsets) == 1 else 20),
+        compiler_params=small(20),
         cost_estimate=pl.CostEstimate(
             flops=8 * tok_rows * rows * len(offsets) * width,
             bytes_accessed=4 * tok_rows * rows * NZ,
@@ -328,9 +366,9 @@
 
 
 def ring_sum(far, near):
-    rows = far.shape[0] // 2
+    rows = far[0].shape[0]
     up3, up2, up1, mine, down1, down2, down3 = near
-    copies, homes = up(far[:rows]), down(far[rows:])
+    copies, homes = up(far[0]), down(far[1])
     below = jnp.concatenate([add_bf(up3[:rows], copies), up3[rows:]], axis=0)
     above = jnp.concatenate([down3[:rows], add_bf(down3[rows:], homes)], axis=0)
     for near_up, near_down in ((up2, down2), (up1, down1)):
@@ -360,14 +398,15 @@
     here = jnp.stack([lax.axis_index(name) for name in ("z", "core", "x", "y")]).astype(jnp.int32)
 
     tokens = (counts[0], swap(counts[0]), acts, swap(acts), grads, swap(grads))
-    (far,) = terms(here, *tokens, (4,))
+    got_counts, got, got_grads = tokens[1::2]
+    far = far_terms(here, counts[0], acts, grads)
+    far = far_terms(here, got_counts, got, got_grads, far)
     near = terms(here, *tokens, (3, 2, 1, 0, -1, -2, -3))
     total = ring_sum(far, near)
     rows = total.shape[0] // 2
     copy_sum, home_sum = total[:rows].astype(BF), total[rows:]
 
-    pieces = {offset: shift(copy_sum, "y", offset) for offset in (3, 1, 2)}
-    pieces = [copy_sum] + [pieces[offset] for offset in range(1, NY)]
+    pieces = [copy_sum] + [shift(copy_sum, "y", offset) for offset in FAR_LAST[1:]]
     copies, *sent = buckets(here, copy_list, pieces)
     for ahead in (2, 1, 3):
         copies = copies + shift(sent[ahead - 1], "x", ahead).astype(F32)
@@ -379,11 +418,9 @@
         gram, swap(own), fresh_mom, weights[0], max(model_width, width)
     )
 
-    pieces = {offset: shift(fresh, "x", offset) for offset in (3, 1, 2)}
-    pieces = [fresh] + [pieces[offset] for offset in range(1, NX)]
+    pieces = [fresh] + [shift(fresh, "x", offset) for offset in FAR_LAST[1:]]
     kept, *sent = wanted(here, copy_list, pieces)
-    pieces = {offset: shift(sent[offset - 1], "y", offset) for offset in (2, 1, 3)}
-    pieces = [kept] + [pieces[offset] for offset in range(1, NY)]
+    pieces = [kept] + [shift(sent[offset - 1], "y", offset) for offset in FAR_FIRST[1:]]
     replica = pick(here, copy_list, pieces)
 
     own = ring(replica)

time: 199 us -> 192 us (0.965)
  local copies, waits for them, and re-layouts: 6.48 us -> 3.76 us
    ppermute x5, starting transfers between devices: 21.8 us -> 17.8 us  [swap(): return lax.ppermute(value, 'core', [(0, 1), (1, 0)])]
    ppermute x12, starting transfers between devices: 29.1 us -> 32.2 us  [down(): return lax.ppermute(value, 'z', [((i + 1) % NZ, i) for i in range(NZ)])]
    pallas_call x2 -> x1, Pallas kernels: 5.14 us -> 2.21 us  [terms(): pl.pallas_call(functools.partial(terms_kernel, offsets), out_shape=(jax.S...]
    unnamed x30 -> x22, local copies, waits for them, and re-layouts: 4.61 us -> 2.94 us
  transfers between devices with their start and end apart: 41 -> 41, of which waited for: 31 -> 24; matrix products, arithmetic and copies ran while one was open for 2% -> 1% of each run, Pallas kernels for 2% -> 2%
where the time goes in v3:
time: 192 us
  waiting for transfers between devices  84.8 us (44%)
  starting transfers between devices  73.6 us (38%)
  Pallas kernels  26.3 us (14%)
  local copies, waits for them, and re-layouts  3.76 us (2%)
    ppermute x12, starting transfers between devices, down(): return lax.ppermute(value, 'z', [((i + 1) % NZ, i) for i in range(NZ)])  32.2 us
    ppermute x12, waiting for transfers between devices, up(): return lax.ppermute(value, 'z', [(i, (i + 1) % NZ) for i in range(NZ)])  31 us
    ppermute x12, waiting for transfers between devices, shift(): return lax.ppermute(value, axis, [(i, (i + offset) % 4) for i in range(4)])  29.6 us
    ppermute x12, waiting for transfers between devices, down(): return lax.ppermute(value, 'z', [((i + 1) % NZ, i) for i in range(NZ)])  21.3 us
    ppermute x5, starting transfers between devices, swap(): return lax.ppermute(value, 'core', [(0, 1), (1, 0)])  17.8 us
    ppermute x12, starting transfers between devices, shift(): return lax.ppermute(value, axis, [(i, (i + offset) % 4) for i in range(4)])  17.4 us
    pallas_call x1, Pallas kernels, newton_schulz(): pl.pallas_call(functools.partial(newton_kernel, 0.2 * math.sqrt(longest))...  16.6 us
    ppermute x12, starting transfers between devices, up(): return lax.ppermute(value, 'z', [(i, (i + 1) % NZ) for i in range(NZ)])  6.16 us
  transfers between devices with their start and end apart: 41, of which 24 were waited for; matrix products, arithmetic and copies ran while one was open for 1% of the time, Pallas kernels for 2%

profile of v3, /device:TPU:1, one launch (start us, length us, event | category | flops | bytes accessed | tf_op | source)
XLA Modules:
  0.0 192.2 jit_solution(9634483729389763217)
XLA Ops:
  0.6 3.3 %collective-permute-start.5 = (bf16[256,2048]{1,0:T(8,128)(2,1)}, bf16[256,2048]{1,0:T(8,128)(2,1)S(1)}, u32[]{:S(2)}, u32[]{:S(2)}) collective-permute-start(bf16[256,2048]{1,0:T(8,128)(2,1)} %bitcast.16), channel_id=1, source_target_pairs={{0,16},{16,0},{1,17},{17,1},{2,18},{18,2},{3,19},{19,3},{4,20},{20... | collective-permute-start | bytes 3145736 | tf_op jit(solution)/shard_map/ppermute | solution.py:25
  9.2 3.9 %collective-permute-start.11 = (bf16[128,768]{1,0:T(8,128)(2,1)S(1)}, bf16[128,768]{1,0:T(8,128)(2,1)S(1)}, u32[]{:S(2)}, u32[]{:S(2)}) collective-permute-start(bf16[128,768]{1,0:T(8,128)(2,1)S(1)} %get-tuple-element.194), channel_id=1, source_target_pairs={{32,0},{64,32},{96,64},{128,96},{160,128},{192,160},{224,192},{0,2... | collective-permute-start | bytes 589832 | tf_op jit(solution)/shard_map/ppermute | solution.py:33
  17.4 3.5 %collective-permute-start.12 = (bf16[256,768]{1,0:T(8,128)(2,1)S(1)}, bf16[256,768]{1,0:T(8,128)(2,1)S(1)}, u32[]{:S(2)}, u32[]{:S(2)}) collective-permute-start(bf16[256,768]{1,0:T(8,128)(2,1)S(1)} %pad_maximum_fusion.1), channel_id=1, source_target_pairs={{32,0},{64,32},{96,64},{128,96},{160,128},{192,160},{224,192},{0,2... | collective-permute-start | bytes 1179656 | tf_op jit(solution)/shard_map/ppermute | solution.py:33
  21.1 7.4 %collective-permute-done.12 = bf16[256,768]{1,0:T(8,128)(2,1)S(1)} collective-permute-done((bf16[256,768]{1,0:T(8,128)(2,1)S(1)}, bf16[256,768]{1,0:T(8,128)(2,1)S(1)}, u32[]{:S(2)}, u32[]{:S(2)}) %collective-permute-start.12) | collective-permute-done | bytes 393248 | tf_op jit(solution)/shard_map/ppermute | solution.py:33
  28.6 3.5 %collective-permute-start.13 = (bf16[256,768]{1,0:T(8,128)(2,1)S(1)}, bf16[256,768]{1,0:T(8,128)(2,1)S(1)}, u32[]{:S(2)}, u32[]{:S(2)}) collective-permute-start(bf16[256,768]{1,0:T(8,128)(2,1)S(1)} %add_convert_fusion.1), channel_id=1, source_target_pairs={{32,0},{64,32},{96,64},{128,96},{160,128},{192,160},{224,192},{0,2... | collective-permute-start | bytes 1179656 | tf_op jit(solution)/shard_map/ppermute | solution.py:33
  32.3 6.4 %collective-permute-done.13 = bf16[256,768]{1,0:T(8,128)(2,1)S(1)} collective-permute-done((bf16[256,768]{1,0:T(8,128)(2,1)S(1)}, bf16[256,768]{1,0:T(8,128)(2,1)S(1)}, u32[]{:S(2)}, u32[]{:S(2)}) %collective-permute-start.13) | collective-permute-done | bytes 393248 | tf_op jit(solution)/shard_map/ppermute | solution.py:33
  38.8 3.5 %collective-permute-start.14 = (bf16[256,768]{1,0:T(8,128)(2,1)S(1)}, bf16[256,768]{1,0:T(8,128)(2,1)S(1)}, u32[]{:S(2)}, u32[]{:S(2)}) collective-permute-start(bf16[256,768]{1,0:T(8,128)(2,1)S(1)} %add_convert_fusion), channel_id=1, source_target_pairs={{32,0},{64,32},{96,64},{128,96},{160,128},{192,160},{224,192},{0,2... | collective-permute-start | bytes 1179656 | tf_op jit(solution)/shard_map/ppermute | solution.py:33
  42.5 5.5 %collective-permute-done.14 = bf16[256,768]{1,0:T(8,128)(2,1)S(1)} collective-permute-done((bf16[256,768]{1,0:T(8,128)(2,1)S(1)}, bf16[256,768]{1,0:T(8,128)(2,1)S(1)}, u32[]{:S(2)}, u32[]{:S(2)}) %collective-permute-start.14) | collective-permute-done | bytes 393248 | tf_op jit(solution)/shard_map/ppermute | solution.py:33
  48.0 3.3 %collective-permute-done.10 = bf16[256,768]{1,0:T(8,128)(2,1)S(1)} collective-permute-done((bf16[256,768]{1,0:T(8,128)(2,1)S(1)}, bf16[256,768]{1,0:T(8,128)(2,1)S(1)}, u32[]{:S(2)}, u32[]{:S(2)}) %collective-permute-start.10) | collective-permute-done | bytes 393248 | tf_op jit(solution)/shard_map/ppermute | solution.py:29
  51.5 3.0 %collective-permute-start.17 = (bf16[128,768]{1,0:T(8,128)(2,1)S(1)}, bf16[128,768]{1,0:T(8,128)(2,1)S(1)}, u32[]{:S(2)}, u32[]{:S(2)}) collective-permute-start(bf16[128,768]{1,0:T(8,128)(2,1)S(1)} %slice.33.refs_0_), channel_id=1, source_target_pairs={{0,2},{1,3},{2,0},{3,1},{4,6},{5,7},{6,4},{7,5},{8,10},{9,11},{10,... | collective-permute-start | bytes 589832 | tf_op jit(solution)/shard_map/ppermute | solution.py:37
  57.6 2.7 %collective-permute-done.16.refs_2_ = bf16[128,768]{1,0:T(8,128)(2,1)S(1)} collective-permute-done((bf16[128,768]{1,0:T(8,128)(2,1)S(1)}, bf16[128,768]{1,0:T(8,128)(2,1)S(1)}, u32[]{:S(2)}, u32[]{:S(2)}) %collective-permute-start.16) | collective-permute-done | bytes 196640 | tf_op jit(solution)/shard_map/ppermute | solution.py:37
  60.4 2.8 %collective-permute-done.15.refs_1_ = bf16[128,768]{1,0:T(8,128)(2,1)S(1)} collective-permute-done((bf16[128,768]{1,0:T(8,128)(2,1)S(1)}, bf16[128,768]{1,0:T(8,128)(2,1)S(1)}, u32[]{:S(2)}, u32[]{:S(2)}) %collective-permute-start.15) | collective-permute-done | bytes 196640 | tf_op jit(solution)/shard_map/ppermute | solution.py:37
  64.1 2.8 %collective-permute-start.18 = (bf16[128,768]{1,0:T(8,128)(2,1)S(1)}, bf16[128,768]{1,0:T(8,128)(2,1)S(1)}, u32[]{:S(2)}, u32[]{:S(2)}) collective-permute-start(bf16[128,768]{1,0:T(8,128)(2,1)S(1)} %get-tuple-element.196), channel_id=1, source_target_pairs={{0,8},{4,12},{8,0},{12,4},{1,9},{5,13},{9,1},{13,5},{2,10},{6,14},... | collective-permute-start | bytes 589832 | tf_op jit(solution)/shard_map/ppermute | solution.py:37
  70.2 4.6 %collective-permute-done.19 = bf16[128,768]{1,0:T(8,128)(2,1)S(1)} collective-permute-done((bf16[128,768]{1,0:T(8,128)(2,1)S(1)}, bf16[128,768]{1,0:T(8,128)(2,1)S(1)}, u32[]{:S(2)}, u32[]{:S(2)}) %collective-permute-start.19) | collective-permute-done | bytes 196640 | tf_op jit(solution)/shard_map/ppermute | solution.py:37
  75.1 26.3 %while.34 = (s32[]{:T(128)}, bf16[128,768]{1,0:T(8,128)(2,1)S(1)}, bf16[128,768]{1,0:T(8,128)(2,1)S(1)}, bf16[1024,768]{1,0:T(8,128)(2,1)S(1)}, s32[]{:T(128)}, ...) while((s32[]{:T(128)}, bf16[128,768]{1,0:T(8,128)(2,1)S(1)}, bf16[128,768]{1,0:T(8,128)(2,1)S(1)}, ...), condition=%wide.region_1.0_spmd, body=%wide.region_0.0_spmd.sunk | while | flops 12 | bytes 3146025 | solution.py:389
  78.0 2.9 %collective-permute-done = bf16[128,768]{1,0:T(8,128)(2,1)S(1)} collective-permute-done((bf16[128,768]{1,0:T(8,128)(2,1)S(1)}, bf16[128,768]{1,0:T(8,128)(2,1)S(1)}, u32[]{:S(2)}, u32[]{:S(2)}) %collective-permute-start) | collective-permute-done | bytes 196640 | tf_op jit(solution)/shard_map/while/body/eval_jaxpr/ppermute | solution.py:29
  81.1 2.8 %collective-permute-start.1 = (bf16[128,768]{1,0:T(8,128)(2,1)S(1)}, bf16[128,768]{1,0:T(8,128)(2,1)S(1)}, u32[]{:S(2)}, u32[]{:S(2)}) collective-permute-start(bf16[128,768]{1,0:T(8,128)(2,1)S(1)} %copy.20), channel_id=1, source_target_pairs={{32,0},{64,32},{96,64},{128,96},{160,128},{192,160},{224,192},{0,2... | collective-permute-start | bytes 589832 | tf_op jit(solution)/shard_map/while/body/eval_jaxpr/ppermute | solution.py:33
  84.0 2.9 %collective-permute-done = bf16[128,768]{1,0:T(8,128)(2,1)S(1)} collective-permute-done((bf16[128,768]{1,0:T(8,128)(2,1)S(1)}, bf16[128,768]{1,0:T(8,128)(2,1)S(1)}, u32[]{:S(2)}, u32[]{:S(2)}) %collective-permute-start) | collective-permute-done | bytes 196640 | tf_op jit(solution)/shard_map/while/body/eval_jaxpr/ppermute | solution.py:29
  89.9 3.5 %collective-permute-done = bf16[128,768]{1,0:T(8,128)(2,1)S(1)} collective-permute-done((bf16[128,768]{1,0:T(8,128)(2,1)S(1)}, bf16[128,768]{1,0:T(8,128)(2,1)S(1)}, u32[]{:S(2)}, u32[]{:S(2)}) %collective-permute-start) | collective-permute-done | bytes 196640 | tf_op jit(solution)/shard_map/while/body/eval_jaxpr/ppermute | solution.py:29
  96.7 4.6 %collective-permute-done = bf16[128,768]{1,0:T(8,128)(2,1)S(1)} collective-permute-done((bf16[128,768]{1,0:T(8,128)(2,1)S(1)}, bf16[128,768]{1,0:T(8,128)(2,1)S(1)}, u32[]{:S(2)}, u32[]{:S(2)}) %collective-permute-start) | collective-permute-done | bytes 196640 | tf_op jit(solution)/shard_map/while/body/eval_jaxpr/ppermute | solution.py:29
  101.4 8.4 %collective-permute-start.21 = (bf16[1024,768]{1,0:T(8,128)(2,1)S(1)}, bf16[1024,768]{1,0:T(8,128)(2,1)S(1)}, u32[]{:S(2)}, u32[]{:S(2)}) collective-permute-start(bf16[1024,768]{1,0:T(8,128)(2,1)S(1)} %constant_dynamic-update-slice_fusion.5), channel_id=1, source_target_pairs={{0,16},{16,0},{1,17},{17,1},{2,18},{18,2},{3,19},{19,3},{4,20},{20... | collective-permute-start | bytes 4718600 | tf_op jit(solution)/shard_map/ppermute | solution.py:25
  112.8 16.6 %newton_schulz.1 = (f32[128,768]{1,0:T(8,128)}, bf16[128,768]{1,0:T(8,128)(2,1)S(1)}) custom-call(f32[768,768]{1,0:T(8,128)S(1)} %fusion.3.gram_ref, bf16[1024,768]{1,0:T(8,128)(2,1)S(1)} %collective-permute-done.21.other_ref, f32[128,768]{1,0:T(8,128)S(1)} %get-tuple-element.226.mom_ref, bf16[128,768]{1,0:T(8,128)(2,1)S(1)} %bitcast.26), custom_call_target="tpu_custom_call" | custom-call | flops 12683575296 | bytes 4718592 | tf_op jit(solution)/shard_map/newton_schulz/pallas_call | solution.py:346
  133.8 3.2 %collective-permute-done.24.refs_3_ = bf16[128,768]{1,0:T(8,128)(2,1)S(1)} collective-permute-done((bf16[128,768]{1,0:T(8,128)(2,1)S(1)}, bf16[128,768]{1,0:T(8,128)(2,1)S(1)}, u32[]{:S(2)}, u32[]{:S(2)}) %collective-permute-start.24) | collective-permute-done | bytes 196640 | tf_op jit(solution)/shard_map/ppermute | solution.py:37
  137.1 4.7 %collective-permute-done.23.refs_2_ = bf16[128,768]{1,0:T(8,128)(2,1)S(1)} collective-permute-done((bf16[128,768]{1,0:T(8,128)(2,1)S(1)}, bf16[128,768]{1,0:T(8,128)(2,1)S(1)}, u32[]{:S(2)}, u32[]{:S(2)}) %collective-permute-start.23) | collective-permute-done | bytes 196640 | tf_op jit(solution)/shard_map/ppermute | solution.py:37
  145.6 4.0 %collective-permute-done.25.refs_1_ = bf16[128,768]{1,0:T(8,128)(2,1)S(1)} collective-permute-done((bf16[128,768]{1,0:T(8,128)(2,1)S(1)}, bf16[128,768]{1,0:T(8,128)(2,1)S(1)}, u32[]{:S(2)}, u32[]{:S(2)}) %collective-permute-start.25) | collective-permute-done | bytes 196640 | tf_op jit(solution)/shard_map/ppermute | solution.py:37
  149.6 5.3 %collective-permute-done.26.refs_2_ = bf16[128,768]{1,0:T(8,128)(2,1)S(1)} collective-permute-done((bf16[128,768]{1,0:T(8,128)(2,1)S(1)}, bf16[128,768]{1,0:T(8,128)(2,1)S(1)}, u32[]{:S(2)}, u32[]{:S(2)}) %collective-permute-start.26) | collective-permute-done | bytes 196640 | tf_op jit(solution)/shard_map/ppermute | solution.py:37
  155.7 25.9 %while.35 = (s32[]{:T(128)}, bf16[128,768]{1,0:T(8,128)(2,1)S(1)}, bf16[128,768]{1,0:T(8,128)(2,1)S(1)}, bf16[1024,768]{1,0:T(8,128)(2,1)S(1)}, s32[]{:T(128)}, ...) while((s32[]{:T(128)}, bf16[128,768]{1,0:T(8,128)(2,1)S(1)}, bf16[128,768]{1,0:T(8,128)(2,1)S(1)}, ...), condition=%wide.region_3.0_spmd, body=%wide.region_2.0_spmd.sunk | while | flops 12 | bytes 3146025 | solution.py:389
  159.0 4.4 %collective-permute-done.2 = bf16[128,768]{1,0:T(8,128)(2,1)S(1)} collective-permute-done((bf16[128,768]{1,0:T(8,128)(2,1)S(1)}, bf16[128,768]{1,0:T(8,128)(2,1)S(1)}, u32[]{:S(2)}, u32[]{:S(2)}) %collective-permute-start.2) | collective-permute-done | bytes 196640 | tf_op jit(solution)/shard_map/while/body/eval_jaxpr/ppermute | solution.py:29
  166.3 3.5 %collective-permute-done.2 = bf16[128,768]{1,0:T(8,128)(2,1)S(1)} collective-permute-done((bf16[128,768]{1,0:T(8,128)(2,1)S(1)}, bf16[128,768]{1,0:T(8,128)(2,1)S(1)}, u32[]{:S(2)}, u32[]{:S(2)}) %collective-permute-start.2) | collective-permute-done | bytes 196640 | tf_op jit(solution)/shard_map/while/body/eval_jaxpr/ppermute | solution.py:29
  172.8 2.9 %collective-permute-done.2 = bf16[128,768]{1,0:T(8,128)(2,1)S(1)} collective-permute-done((bf16[128,768]{1,0:T(8,128)(2,1)S(1)}, bf16[128,768]{1,0:T(8,128)(2,1)S(1)}, u32[]{:S(2)}, u32[]{:S(2)}) %collective-permute-start.2) | collective-permute-done | bytes 196640 | tf_op jit(solution)/shard_map/while/body/eval_jaxpr/ppermute | solution.py:29
  178.7 2.9 %collective-permute-done.2 = bf16[128,768]{1,0:T(8,128)(2,1)S(1)} collective-permute-done((bf16[128,768]{1,0:T(8,128)(2,1)S(1)}, bf16[128,768]{1,0:T(8,128)(2,1)S(1)}, u32[]{:S(2)}, u32[]{:S(2)}) %collective-permute-start.2) | collective-permute-done | bytes 196640 | tf_op jit(solution)/shard_map/while/body/eval_jaxpr/ppermute | solution.py:29
  181.6 5.6 %collective-permute-start.28 = (bf16[1024,768]{1,0:T(8,128)(2,1)S(1)}, bf16[1024,768]{1,0:T(8,128)(2,1)S(1)}, u32[]{:S(2)}, u32[]{:S(2)}) collective-permute-start(bf16[1024,768]{1,0:T(8,128)(2,1)S(1)} %constant_dynamic-update-slice_fusion.4.blocks_ref), channel_id=1, source_target_pairs={{0,16},{16,0},{1,17},{17,1},{2,18},{18,2},{3,19},{19,3},{4,20},{20... | collective-permute-start | bytes 4718600 | tf_op jit(solution)/shard_map/ppermute | solution.py:25
  (134 shorter events, 56.1 us)
Async XLA Ops:
  0.6 7.7 %collective-permute-start.5 = (bf16[256,2048]{1,0:T(8,128)(2,1)}, bf16[256,2048]{1,0:T(8,128)(2,1)S(1)}, u32[]{:S(2)}, u32[]{:S(2)}) collective-permute-start(bf16[256,2048]{1,0:T(8,128)(2,1)} %bitcast.16), channel_id=1, source_target_pairs={{0,16},{16,0},{1,17},{17,1},{2,18},{18,2},{3,19},{19,3},{4,20},{20... | collective-permute-start | bytes 3145736 | tf_op jit(solution)/shard_map/ppermute | solution.py:25
  9.2 8.2 %collective-permute-start.11 = (bf16[128,768]{1,0:T(8,128)(2,1)S(1)}, bf16[128,768]{1,0:T(8,128)(2,1)S(1)}, u32[]{:S(2)}, u32[]{:S(2)}) collective-permute-start(bf16[128,768]{1,0:T(8,128)(2,1)S(1)} %get-tuple-element.194), channel_id=1, source_target_pairs={{32,0},{64,32},{96,64},{128,96},{160,128},{192,160},{224,192},{0,2... | collective-permute-start | bytes 589832 | tf_op jit(solution)/shard_map/ppermute | solution.py:33
  13.1 7.8 %collective-permute-start.7 = (bf16[128,768]{1,0:T(8,128)(2,1)S(1)}, bf16[128,768]{1,0:T(8,128)(2,1)S(1)}, u32[]{:S(2)}, u32[]{:S(2)}) collective-permute-start(bf16[128,768]{1,0:T(8,128)(2,1)S(1)} %get-tuple-element.190), channel_id=1, source_target_pairs={{0,32},{32,64},{64,96},{96,128},{128,160},{160,192},{192,224},{224... | collective-permute-start | bytes 589832 | tf_op jit(solution)/shard_map/ppermute | solution.py:29
  17.4 11.0 %collective-permute-start.12 = (bf16[256,768]{1,0:T(8,128)(2,1)S(1)}, bf16[256,768]{1,0:T(8,128)(2,1)S(1)}, u32[]{:S(2)}, u32[]{:S(2)}) collective-permute-start(bf16[256,768]{1,0:T(8,128)(2,1)S(1)} %pad_maximum_fusion.1), channel_id=1, source_target_pairs={{32,0},{64,32},{96,64},{128,96},{160,128},{192,160},{224,192},{0,2... | collective-permute-start | bytes 1179656 | tf_op jit(solution)/shard_map/ppermute | solution.py:33
  21.0 11.1 %collective-permute-start.8 = (bf16[256,768]{1,0:T(8,128)(2,1)S(1)}, bf16[256,768]{1,0:T(8,128)(2,1)S(1)}, u32[]{:S(2)}, u32[]{:S(2)}) collective-permute-start(bf16[256,768]{1,0:T(8,128)(2,1)S(1)} %pad_maximum_fusion), channel_id=1, source_target_pairs={{0,32},{32,64},{64,96},{96,128},{128,160},{160,192},{192,224},{224... | collective-permute-start | bytes 1179656 | tf_op jit(solution)/shard_map/ppermute | solution.py:29
  28.6 10.1 %collective-permute-start.13 = (bf16[256,768]{1,0:T(8,128)(2,1)S(1)}, bf16[256,768]{1,0:T(8,128)(2,1)S(1)}, u32[]{:S(2)}, u32[]{:S(2)}) collective-permute-start(bf16[256,768]{1,0:T(8,128)(2,1)S(1)} %add_convert_fusion.1), channel_id=1, source_target_pairs={{32,0},{64,32},{96,64},{128,96},{160,128},{192,160},{224,192},{0,2... | collective-permute-start | bytes 1179656 | tf_op jit(solution)/shard_map/ppermute | solution.py:33
  32.2 10.1 %collective-permute-start.9 = (bf16[256,768]{1,0:T(8,128)(2,1)S(1)}, bf16[256,768]{1,0:T(8,128)(2,1)S(1)}, u32[]{:S(2)}, u32[]{:S(2)}) collective-permute-start(bf16[256,768]{1,0:T(8,128)(2,1)S(1)} %add_convert_fusion.3), channel_id=1, source_target_pairs={{0,32},{32,64},{64,96},{96,128},{128,160},{160,192},{192,224},{224... | collective-permute-start | bytes 1179656 | tf_op jit(solution)/shard_map/ppermute | solution.py:29
  38.8 9.2 %collective-permute-start.14 = (bf16[256,768]{1,0:T(8,128)(2,1)S(1)}, bf16[256,768]{1,0:T(8,128)(2,1)S(1)}, u32[]{:S(2)}, u32[]{:S(2)}) collective-permute-start(bf16[256,768]{1,0:T(8,128)(2,1)S(1)} %add_convert_fusion), channel_id=1, source_target_pairs={{32,0},{64,32},{96,64},{128,96},{160,128},{192,160},{224,192},{0,2... | collective-permute-start | bytes 1179656 | tf_op jit(solution)/shard_map/ppermute | solution.py:33
  42.4 8.9 %collective-permute-start.10 = (bf16[256,768]{1,0:T(8,128)(2,1)S(1)}, bf16[256,768]{1,0:T(8,128)(2,1)S(1)}, u32[]{:S(2)}, u32[]{:S(2)}) collective-permute-start(bf16[256,768]{1,0:T(8,128)(2,1)S(1)} %add_convert_fusion.2), channel_id=1, source_target_pairs={{0,32},{32,64},{64,96},{96,128},{128,160},{160,192},{192,224},{224... | collective-permute-start | bytes 1179656 | tf_op jit(solution)/shard_map/ppermute | solution.py:29
  51.5 6.1 %collective-permute-start.17 = (bf16[128,768]{1,0:T(8,128)(2,1)S(1)}, bf16[128,768]{1,0:T(8,128)(2,1)S(1)}, u32[]{:S(2)}, u32[]{:S(2)}) collective-permute-start(bf16[128,768]{1,0:T(8,128)(2,1)S(1)} %slice.33.refs_0_), channel_id=1, source_target_pairs={{0,2},{1,3},{2,0},{3,1},{4,6},{5,7},{6,4},{7,5},{8,10},{9,11},{10,... | collective-permute-start | bytes 589832 | tf_op jit(solution)/shard_map/ppermute | solution.py:37
  54.5 5.9 %collective-permute-start.16 = (bf16[128,768]{1,0:T(8,128)(2,1)S(1)}, bf16[128,768]{1,0:T(8,128)(2,1)S(1)}, u32[]{:S(2)}, u32[]{:S(2)}) collective-permute-start(bf16[128,768]{1,0:T(8,128)(2,1)S(1)} %slice.33.refs_0_), channel_id=1, source_target_pairs={{0,3},{1,0},{2,1},{3,2},{4,7},{5,4},{6,5},{7,6},{8,11},{9,8},{10,9... | collective-permute-start | bytes 589832 | tf_op jit(solution)/shard_map/ppermute | solution.py:37
  55.3 7.8 %collective-permute-start.15 = (bf16[128,768]{1,0:T(8,128)(2,1)S(1)}, bf16[128,768]{1,0:T(8,128)(2,1)S(1)}, u32[]{:S(2)}, u32[]{:S(2)}) collective-permute-start(bf16[128,768]{1,0:T(8,128)(2,1)S(1)} %slice.33.refs_0_), channel_id=1, source_target_pairs={{0,1},{1,2},{2,3},{3,0},{4,5},{5,6},{6,7},{7,4},{8,9},{9,10},{10,1... | collective-permute-start | bytes 589832 | tf_op jit(solution)/shard_map/ppermute | solution.py:37
  64.1 6.1 %collective-permute-start.18 = (bf16[128,768]{1,0:T(8,128)(2,1)S(1)}, bf16[128,768]{1,0:T(8,128)(2,1)S(1)}, u32[]{:S(2)}, u32[]{:S(2)}) collective-permute-start(bf16[128,768]{1,0:T(8,128)(2,1)S(1)} %get-tuple-element.196), channel_id=1, source_target_pairs={{0,8},{4,12},{8,0},{12,4},{1,9},{5,13},{9,1},{13,5},{2,10},{6,14},... | collective-permute-start | bytes 589832 | tf_op jit(solution)/shard_map/ppermute | solution.py:37
  67.0 7.8 %collective-permute-start.19 = (bf16[128,768]{1,0:T(8,128)(2,1)S(1)}, bf16[128,768]{1,0:T(8,128)(2,1)S(1)}, u32[]{:S(2)}, u32[]{:S(2)}) collective-permute-start(bf16[128,768]{1,0:T(8,128)(2,1)S(1)} %get-tuple-element.197), channel_id=1, source_target_pairs={{0,4},{4,8},{8,12},{12,0},{1,5},{5,9},{9,13},{13,1},{2,6},{6,10},{... | collective-permute-start | bytes 589832 | tf_op jit(solution)/shard_map/ppermute | solution.py:37
  67.3 7.5 %collective-permute-start.20 = (bf16[128,768]{1,0:T(8,128)(2,1)S(1)}, bf16[128,768]{1,0:T(8,128)(2,1)S(1)}, u32[]{:S(2)}, u32[]{:S(2)}) collective-permute-start(bf16[128,768]{1,0:T(8,128)(2,1)S(1)} %get-tuple-element.198), channel_id=1, source_target_pairs={{0,12},{4,0},{8,4},{12,8},{1,13},{5,1},{9,5},{13,9},{2,14},{6,2},{... | collective-permute-start | bytes 589832 | tf_op jit(solution)/shard_map/ppermute | solution.py:37
  81.0 5.9 %collective-permute-start = (bf16[128,768]{1,0:T(8,128)(2,1)S(1)}, bf16[128,768]{1,0:T(8,128)(2,1)S(1)}, u32[]{:S(2)}, u32[]{:S(2)}) collective-permute-start(bf16[128,768]{1,0:T(8,128)(2,1)S(1)} %copy.19), channel_id=1, source_target_pairs={{0,32},{32,64},{64,96},{96,128},{128,160},{160,192},{192,224},{224... | collective-permute-start | bytes 589832 | tf_op jit(solution)/shard_map/while/body/eval_jaxpr/ppermute | solution.py:29
  86.9 6.5 %collective-permute-start = (bf16[128,768]{1,0:T(8,128)(2,1)S(1)}, bf16[128,768]{1,0:T(8,128)(2,1)S(1)}, u32[]{:S(2)}, u32[]{:S(2)}) collective-permute-start(bf16[128,768]{1,0:T(8,128)(2,1)S(1)} %copy.19), channel_id=1, source_target_pairs={{0,32},{32,64},{64,96},{96,128},{128,160},{160,192},{192,224},{224... | collective-permute-start | bytes 589832 | tf_op jit(solution)/shard_map/while/body/eval_jaxpr/ppermute | solution.py:29
  93.4 7.9 %collective-permute-start = (bf16[128,768]{1,0:T(8,128)(2,1)S(1)}, bf16[128,768]{1,0:T(8,128)(2,1)S(1)}, u32[]{:S(2)}, u32[]{:S(2)}) collective-permute-start(bf16[128,768]{1,0:T(8,128)(2,1)S(1)} %copy.19), channel_id=1, source_target_pairs={{0,32},{32,64},{64,96},{96,128},{128,160},{160,192},{192,224},{224... | collective-permute-start | bytes 589832 | tf_op jit(solution)/shard_map/while/body/eval_jaxpr/ppermute | solution.py:29
  94.3 7.1 %collective-permute-start.1 = (bf16[128,768]{1,0:T(8,128)(2,1)S(1)}, bf16[128,768]{1,0:T(8,128)(2,1)S(1)}, u32[]{:S(2)}, u32[]{:S(2)}) collective-permute-start(bf16[128,768]{1,0:T(8,128)(2,1)S(1)} %copy.20), channel_id=1, source_target_pairs={{32,0},{64,32},{96,64},{128,96},{160,128},{192,160},{224,192},{0,2... | collective-permute-start | bytes 589832 | tf_op jit(solution)/shard_map/while/body/eval_jaxpr/ppermute | solution.py:33
  101.4 11.4 %collective-permute-start.21 = (bf16[1024,768]{1,0:T(8,128)(2,1)S(1)}, bf16[1024,768]{1,0:T(8,128)(2,1)S(1)}, u32[]{:S(2)}, u32[]{:S(2)}) collective-permute-start(bf16[1024,768]{1,0:T(8,128)(2,1)S(1)} %constant_dynamic-update-slice_fusion.5), channel_id=1, source_target_pairs={{0,16},{16,0},{1,17},{17,1},{2,18},{18,2},{3,19},{19,3},{4,20},{20... | collective-permute-start | bytes 4718600 | tf_op jit(solution)/shard_map/ppermute | solution.py:25
  129.5 7.6 %collective-permute-start.24 = (bf16[128,768]{1,0:T(8,128)(2,1)S(1)}, bf16[128,768]{1,0:T(8,128)(2,1)S(1)}, u32[]{:S(2)}, u32[]{:S(2)}) collective-permute-start(bf16[128,768]{1,0:T(8,128)(2,1)S(1)} %get-tuple-element.202.refs_0_), channel_id=1, source_target_pairs={{0,8},{4,12},{8,0},{12,4},{1,9},{5,13},{9,1},{13,5},{2,10},{6,14},... | collective-permute-start | bytes 589832 | tf_op jit(solution)/shard_map/ppermute | solution.py:37
  132.0 9.8 %collective-permute-start.23 = (bf16[128,768]{1,0:T(8,128)(2,1)S(1)}, bf16[128,768]{1,0:T(8,128)(2,1)S(1)}, u32[]{:S(2)}, u32[]{:S(2)}) collective-permute-start(bf16[128,768]{1,0:T(8,128)(2,1)S(1)} %get-tuple-element.202.refs_0_), channel_id=1, source_target_pairs={{0,12},{4,0},{8,4},{12,8},{1,13},{5,1},{9,5},{13,9},{2,14},{6,2},{... | collective-permute-start | bytes 589832 | tf_op jit(solution)/shard_map/ppermute | solution.py:37
  133.8 8.0 %collective-permute-start.22 = (bf16[128,768]{1,0:T(8,128)(2,1)S(1)}, bf16[128,768]{1,0:T(8,128)(2,1)S(1)}, u32[]{:S(2)}, u32[]{:S(2)}) collective-permute-start(bf16[128,768]{1,0:T(8,128)(2,1)S(1)} %get-tuple-element.202.refs_0_), channel_id=1, source_target_pairs={{0,4},{4,8},{8,12},{12,0},{1,5},{5,9},{9,13},{13,1},{2,6},{6,10},{... | collective-permute-start | bytes 589832 | tf_op jit(solution)/shard_map/ppermute | solution.py:37
  142.5 7.1 %collective-permute-start.25 = (bf16[128,768]{1,0:T(8,128)(2,1)S(1)}, bf16[128,768]{1,0:T(8,128)(2,1)S(1)}, u32[]{:S(2)}, u32[]{:S(2)}) collective-permute-start(bf16[128,768]{1,0:T(8,128)(2,1)S(1)} %get-tuple-element.204), channel_id=1, source_target_pairs={{0,2},{1,3},{2,0},{3,1},{4,6},{5,7},{6,4},{7,5},{8,10},{9,11},{10,... | collective-permute-start | bytes 589832 | tf_op jit(solution)/shard_map/ppermute | solution.py:37
  142.9 12.1 %collective-permute-start.26 = (bf16[128,768]{1,0:T(8,128)(2,1)S(1)}, bf16[128,768]{1,0:T(8,128)(2,1)S(1)}, u32[]{:S(2)}, u32[]{:S(2)}) collective-permute-start(bf16[128,768]{1,0:T(8,128)(2,1)S(1)} %get-tuple-element.205), channel_id=1, source_target_pairs={{0,1},{1,2},{2,3},{3,0},{4,5},{5,6},{6,7},{7,4},{8,9},{9,10},{10,1... | collective-permute-start | bytes 589832 | tf_op jit(solution)/shard_map/ppermute | solution.py:37
  143.0 12.0 %collective-permute-start.27 = (bf16[128,768]{1,0:T(8,128)(2,1)S(1)}, bf16[128,768]{1,0:T(8,128)(2,1)S(1)}, u32[]{:S(2)}, u32[]{:S(2)}) collective-permute-start(bf16[128,768]{1,0:T(8,128)(2,1)S(1)} %get-tuple-element.206), channel_id=1, source_target_pairs={{0,3},{1,0},{2,1},{3,2},{4,7},{5,4},{6,5},{7,6},{8,11},{9,8},{10,9... | collective-permute-start | bytes 589832 | tf_op jit(solution)/shard_map/ppermute | solution.py:37
  155.7 7.7 %collective-permute-start.2 = (bf16[128,768]{1,0:T(8,128)(2,1)S(1)}, bf16[128,768]{1,0:T(8,128)(2,1)S(1)}, u32[]{:S(2)}, u32[]{:S(2)}) collective-permute-start(bf16[128,768]{1,0:T(8,128)(2,1)S(1)} %copy.32), channel_id=1, source_target_pairs={{0,32},{32,64},{64,96},{96,128},{128,160},{160,192},{192,224},{224... | collective-permute-start | bytes 589832 | tf_op jit(solution)/shard_map/while/body/eval_jaxpr/ppermute | solution.py:29
  156.8 6.6 %collective-permute-start.3 = (bf16[128,768]{1,0:T(8,128)(2,1)S(1)}, bf16[128,768]{1,0:T(8,128)(2,1)S(1)}, u32[]{:S(2)}, u32[]{:S(2)}) collective-permute-start(bf16[128,768]{1,0:T(8,128)(2,1)S(1)} %copy.33), channel_id=1, source_target_pairs={{32,0},{64,32},{96,64},{128,96},{160,128},{192,160},{224,192},{0,2... | collective-permute-start | bytes 589832 | tf_op jit(solution)/shard_map/while/body/eval_jaxpr/ppermute | solution.py:33
  163.4 6.4 %collective-permute-start.2 = (bf16[128,768]{1,0:T(8,128)(2,1)S(1)}, bf16[128,768]{1,0:T(8,128)(2,1)S(1)}, u32[]{:S(2)}, u32[]{:S(2)}) collective-permute-start(bf16[128,768]{1,0:T(8,128)(2,1)S(1)} %copy.32), channel_id=1, source_target_pairs={{0,32},{32,64},{64,96},{96,128},{128,160},{160,192},{192,224},{224... | collective-permute-start | bytes 589832 | tf_op jit(solution)/shard_map/while/body/eval_jaxpr/ppermute | solution.py:29
  169.9 5.8 %collective-permute-start.2 = (bf16[128,768]{1,0:T(8,128)(2,1)S(1)}, bf16[128,768]{1,0:T(8,128)(2,1)S(1)}, u32[]{:S(2)}, u32[]{:S(2)}) collective-permute-start(bf16[128,768]{1,0:T(8,128)(2,1)S(1)} %copy.32), channel_id=1, source_target_pairs={{0,32},{32,64},{64,96},{96,128},{128,160},{160,192},{192,224},{224... | collective-permute-start | bytes 589832 | tf_op jit(solution)/shard_map/while/body/eval_jaxpr/ppermute | solution.py:29
  175.7 5.9 %collective-permute-start.2 = (bf16[128,768]{1,0:T(8,128)(2,1)S(1)}, bf16[128,768]{1,0:T(8,128)(2,1)S(1)}, u32[]{:S(2)}, u32[]{:S(2)}) collective-permute-start(bf16[128,768]{1,0:T(8,128)(2,1)S(1)} %copy.32), channel_id=1, source_target_pairs={{0,32},{32,64},{64,96},{96,128},{128,160},{160,192},{192,224},{224... | collective-permute-start | bytes 589832 | tf_op jit(solution)/shard_map/while/body/eval_jaxpr/ppermute | solution.py:29
  181.6 8.7 %collective-permute-start.28 = (bf16[1024,768]{1,0:T(8,128)(2,1)S(1)}, bf16[1024,768]{1,0:T(8,128)(2,1)S(1)}, u32[]{:S(2)}, u32[]{:S(2)}) collective-permute-start(bf16[1024,768]{1,0:T(8,128)(2,1)S(1)} %constant_dynamic-update-slice_fusion.4.blocks_ref), channel_id=1, source_target_pairs={{0,16},{16,0},{1,17},{17,1},{2,18},{18,2},{3,19},{19,3},{4,20},{20... | collective-permute-start | bytes 4718600 | tf_op jit(solution)/shard_map/ppermute | solution.py:25
  (19 other events, 160.0 us)

commit v4 on v3

--- a/solution.py
+++ b/solution.py
@@ -270,6 +270,7 @@
     t_hi,
     t_lo,
     iterate_ref,
+    side_ref,
     full_ref,
 ):
     width = gram_ref.shape[0]
@@ -327,14 +328,26 @@
         for i, j in pairs:
             store(*k, i, j, coef_b * load(*s, i, j) + coef_c * product(s, s, i, j))
         iterate_ref[...] = coef_a * iterate_ref[...] + times(iterate_ref[...], k)
-        for i, j in pairs:
-            store(*t, i, j, coef_a * load(*s, i, j) + product(s, k, i, j))
-        for i, j in pairs:
-            store(*s, i, j, coef_a * load(*t, i, j) + product(t, k, i, j))
+
+        @pl.when(step == 0)
+        def _():
+            for i, j in pairs:
+                store(*t, i, j, coef_a * load(*s, i, j) + product(s, k, i, j))
+            for i, j in pairs:
+                store(*s, i, j, coef_a * load(*t, i, j) + product(t, k, i, j))
+
+    side_ref[...] = iterate_ref[...]
+    iterate_ref[...] = coef_a * iterate_ref[...]
+
+    @pl.loop(0, 2)
+    def _(index):
+        side = side_ref[...]
+        side = times(coef_a * side + times(side, k), s)
+        side = coef_a * side + times(side, k)
+        side_ref[...] = side
+        iterate_ref[...] += jnp.where(index == 0, coef_b, coef_c) * side
 
     iterate = iterate_ref[...]
-    side = times(iterate, s)
-    iterate = coef_a * iterate + (coef_b * side + coef_c * times(side, s))
     update = factor * iterate
     update_ref[...] = update
     fresh_ref[...] = (weight_ref[...].astype(F32) - learn_rate * update).astype(BF)
@@ -352,7 +365,8 @@
         in_specs=[vmem] * 4,
         out_specs=(vmem, vmem),
         scratch_shapes=[pltpu.VMEM((width, width), BF)] * 6
-        + [pltpu.VMEM((rows, width), F32), pltpu.VMEM((width, width), F32)],
+        + [pltpu.VMEM((rows, width), F32)] * 2
+        + [pltpu.VMEM((width, width), F32)],
         compiler_params=small(20),
         cost_estimate=pl.CostEstimate(
             flops=28 * width**3, bytes_accessed=8 * width * width, transcendentals=0

time: 192 us -> 191 us (level)
  transfers between devices with their start and end apart: 41 -> 41, of which waited for: 24 -> 24; matrix products, arithmetic and copies ran while one was open for 1% -> 1% of each run, Pallas kernels for 2% -> 3%
where the time goes in v4:
time: 191 us
  waiting for transfers between devices  84.8 us (44%)
  starting transfers between devices  73.3 us (38%)
  Pallas kernels  25.7 us (13%)
  local copies, waits for them, and re-layouts  3.76 us (2%)
    ppermute x12, starting transfers between devices, down(): return lax.ppermute(value, 'z', [((i + 1) % NZ, i) for i in range(NZ)])  32.1 us
    ppermute x12, waiting for transfers between devices, up(): return lax.ppermute(value, 'z', [(i, (i + 1) % NZ) for i in range(NZ)])  31 us
    ppermute x12, waiting for transfers between devices, shift(): return lax.ppermute(value, axis, [(i, (i + offset) % 4) for i in range(4)])  29.6 us
    ppermute x12, waiting for transfers between devices, down(): return lax.ppermute(value, 'z', [((i + 1) % NZ, i) for i in range(NZ)])  21.3 us
    ppermute x5, starting transfers between devices, swap(): return lax.ppermute(value, 'core', [(0, 1), (1, 0)])  17.8 us
    ppermute x12, starting transfers between devices, shift(): return lax.ppermute(value, axis, [(i, (i + offset) % 4) for i in range(4)])  17.2 us
    pallas_call x1, Pallas kernels, newton_schulz(): pl.pallas_call(functools.partial(newton_kernel, 0.2 * math.sqrt(longest))...  15.7 us
    ppermute x12, starting transfers between devices, up(): return lax.ppermute(value, 'z', [(i, (i + 1) % NZ) for i in range(NZ)])  6.22 us
  transfers between devices with their start and end apart: 41, of which 24 were waited for; matrix products, arithmetic and copies ran while one was open for 1% of the time, Pallas kernels for 3%

profile of v4, /device:TPU:1, one launch (start us, length us, event | category | flops | bytes accessed | tf_op | source)
XLA Modules:
  0.0 191.3 jit_solution(15584131855310677488)
XLA Ops:
  0.6 3.3 %collective-permute-start.5 = (bf16[256,2048]{1,0:T(8,128)(2,1)}, bf16[256,2048]{1,0:T(8,128)(2,1)S(1)}, u32[]{:S(2)}, u32[]{:S(2)}) collective-permute-start(bf16[256,2048]{1,0:T(8,128)(2,1)} %bitcast.16), channel_id=1, source_target_pairs={{0,16},{16,0},{1,17},{17,1},{2,18},{18,2},{3,19},{19,3},{4,20},{20... | collective-permute-start | bytes 3145736 | tf_op jit(solution)/shard_map/ppermute | solution.py:25
  9.2 3.9 %collective-permute-start.11 = (bf16[128,768]{1,0:T(8,128)(2,1)S(1)}, bf16[128,768]{1,0:T(8,128)(2,1)S(1)}, u32[]{:S(2)}, u32[]{:S(2)}) collective-permute-start(bf16[128,768]{1,0:T(8,128)(2,1)S(1)} %get-tuple-element.194), channel_id=1, source_target_pairs={{32,0},{64,32},{96,64},{128,96},{160,128},{192,160},{224,192},{0,2... | collective-permute-start | bytes 589832 | tf_op jit(solution)/shard_map/ppermute | solution.py:33
  17.4 3.5 %collective-permute-start.12 = (bf16[256,768]{1,0:T(8,128)(2,1)S(1)}, bf16[256,768]{1,0:T(8,128)(2,1)S(1)}, u32[]{:S(2)}, u32[]{:S(2)}) collective-permute-start(bf16[256,768]{1,0:T(8,128)(2,1)S(1)} %pad_maximum_fusion.1), channel_id=1, source_target_pairs={{32,0},{64,32},{96,64},{128,96},{160,128},{192,160},{224,192},{0,2... | collective-permute-start | bytes 1179656 | tf_op jit(solution)/shard_map/ppermute | solution.py:33
  21.1 7.4 %collective-permute-done.12 = bf16[256,768]{1,0:T(8,128)(2,1)S(1)} collective-permute-done((bf16[256,768]{1,0:T(8,128)(2,1)S(1)}, bf16[256,768]{1,0:T(8,128)(2,1)S(1)}, u32[]{:S(2)}, u32[]{:S(2)}) %collective-permute-start.12) | collective-permute-done | bytes 393248 | tf_op jit(solution)/shard_map/ppermute | solution.py:33
  28.6 3.5 %collective-permute-start.13 = (bf16[256,768]{1,0:T(8,128)(2,1)S(1)}, bf16[256,768]{1,0:T(8,128)(2,1)S(1)}, u32[]{:S(2)}, u32[]{:S(2)}) collective-permute-start(bf16[256,768]{1,0:T(8,128)(2,1)S(1)} %add_convert_fusion.1), channel_id=1, source_target_pairs={{32,0},{64,32},{96,64},{128,96},{160,128},{192,160},{224,192},{0,2... | collective-permute-start | bytes 1179656 | tf_op jit(solution)/shard_map/ppermute | solution.py:33
  32.3 6.4 %collective-permute-done.13 = bf16[256,768]{1,0:T(8,128)(2,1)S(1)} collective-permute-done((bf16[256,768]{1,0:T(8,128)(2,1)S(1)}, bf16[256,768]{1,0:T(8,128)(2,1)S(1)}, u32[]{:S(2)}, u32[]{:S(2)}) %collective-permute-start.13) | collective-permute-done | bytes 393248 | tf_op jit(solution)/shard_map/ppermute | solution.py:33
  38.8 3.5 %collective-permute-start.14 = (bf16[256,768]{1,0:T(8,128)(2,1)S(1)}, bf16[256,768]{1,0:T(8,128)(2,1)S(1)}, u32[]{:S(2)}, u32[]{:S(2)}) collective-permute-start(bf16[256,768]{1,0:T(8,128)(2,1)S(1)} %add_convert_fusion), channel_id=1, source_target_pairs={{32,0},{64,32},{96,64},{128,96},{160,128},{192,160},{224,192},{0,2... | collective-permute-start | bytes 1179656 | tf_op jit(solution)/shard_map/ppermute | solution.py:33
  42.5 5.5 %collective-permute-done.14 = bf16[256,768]{1,0:T(8,128)(2,1)S(1)} collective-permute-done((bf16[256,768]{1,0:T(8,128)(2,1)S(1)}, bf16[256,768]{1,0:T(8,128)(2,1)S(1)}, u32[]{:S(2)}, u32[]{:S(2)}) %collective-permute-start.14) | collective-permute-done | bytes 393248 | tf_op jit(solution)/shard_map/ppermute | solution.py:33
  48.0 3.3 %collective-permute-done.10 = bf16[256,768]{1,0:T(8,128)(2,1)S(1)} collective-permute-done((bf16[256,768]{1,0:T(8,128)(2,1)S(1)}, bf16[256,768]{1,0:T(8,128)(2,1)S(1)}, u32[]{:S(2)}, u32[]{:S(2)}) %collective-permute-start.10) | collective-permute-done | bytes 393248 | tf_op jit(solution)/shard_map/ppermute | solution.py:29
  51.5 3.0 %collective-permute-start.17 = (bf16[128,768]{1,0:T(8,128)(2,1)S(1)}, bf16[128,768]{1,0:T(8,128)(2,1)S(1)}, u32[]{:S(2)}, u32[]{:S(2)}) collective-permute-start(bf16[128,768]{1,0:T(8,128)(2,1)S(1)} %slice.33.refs_0_), channel_id=1, source_target_pairs={{0,2},{1,3},{2,0},{3,1},{4,6},{5,7},{6,4},{7,5},{8,10},{9,11},{10,... | collective-permute-start | bytes 589832 | tf_op jit(solution)/shard_map/ppermute | solution.py:37
  57.6 2.7 %collective-permute-done.16.refs_2_ = bf16[128,768]{1,0:T(8,128)(2,1)S(1)} collective-permute-done((bf16[128,768]{1,0:T(8,128)(2,1)S(1)}, bf16[128,768]{1,0:T(8,128)(2,1)S(1)}, u32[]{:S(2)}, u32[]{:S(2)}) %collective-permute-start.16) | collective-permute-done | bytes 196640 | tf_op jit(solution)/shard_map/ppermute | solution.py:37
  60.4 2.8 %collective-permute-done.15.refs_1_ = bf16[128,768]{1,0:T(8,128)(2,1)S(1)} collective-permute-done((bf16[128,768]{1,0:T(8,128)(2,1)S(1)}, bf16[128,768]{1,0:T(8,128)(2,1)S(1)}, u32[]{:S(2)}, u32[]{:S(2)}) %collective-permute-start.15) | collective-permute-done | bytes 196640 | tf_op jit(solution)/shard_map/ppermute | solution.py:37
  64.1 2.8 %collective-permute-start.18 = (bf16[128,768]{1,0:T(8,128)(2,1)S(1)}, bf16[128,768]{1,0:T(8,128)(2,1)S(1)}, u32[]{:S(2)}, u32[]{:S(2)}) collective-permute-start(bf16[128,768]{1,0:T(8,128)(2,1)S(1)} %get-tuple-element.196), channel_id=1, source_target_pairs={{0,8},{4,12},{8,0},{12,4},{1,9},{5,13},{9,1},{13,5},{2,10},{6,14},... | collective-permute-start | bytes 589832 | tf_op jit(solution)/shard_map/ppermute | solution.py:37
  70.2 4.6 %collective-permute-done.19 = bf16[128,768]{1,0:T(8,128)(2,1)S(1)} collective-permute-done((bf16[128,768]{1,0:T(8,128)(2,1)S(1)}, bf16[128,768]{1,0:T(8,128)(2,1)S(1)}, u32[]{:S(2)}, u32[]{:S(2)}) %collective-permute-start.19) | collective-permute-done | bytes 196640 | tf_op jit(solution)/shard_map/ppermute | solution.py:37
  75.1 26.3 %while.34 = (s32[]{:T(128)}, bf16[128,768]{1,0:T(8,128)(2,1)S(1)}, bf16[128,768]{1,0:T(8,128)(2,1)S(1)}, bf16[1024,768]{1,0:T(8,128)(2,1)S(1)}, s32[]{:T(128)}, ...) while((s32[]{:T(128)}, bf16[128,768]{1,0:T(8,128)(2,1)S(1)}, bf16[128,768]{1,0:T(8,128)(2,1)S(1)}, ...), condition=%wide.region_1.0_spmd, body=%wide.region_0.0_spmd.sunk | while | flops 12 | bytes 3146025 | solution.py:403
  78.0 2.9 %collective-permute-done = bf16[128,768]{1,0:T(8,128)(2,1)S(1)} collective-permute-done((bf16[128,768]{1,0:T(8,128)(2,1)S(1)}, bf16[128,768]{1,0:T(8,128)(2,1)S(1)}, u32[]{:S(2)}, u32[]{:S(2)}) %collective-permute-start) | collective-permute-done | bytes 196640 | tf_op jit(solution)/shard_map/while/body/eval_jaxpr/ppermute | solution.py:29
  81.1 2.8 %collective-permute-start.1 = (bf16[128,768]{1,0:T(8,128)(2,1)S(1)}, bf16[128,768]{1,0:T(8,128)(2,1)S(1)}, u32[]{:S(2)}, u32[]{:S(2)}) collective-permute-start(bf16[128,768]{1,0:T(8,128)(2,1)S(1)} %copy.20), channel_id=1, source_target_pairs={{32,0},{64,32},{96,64},{128,96},{160,128},{192,160},{224,192},{0,2... | collective-permute-start | bytes 589832 | tf_op jit(solution)/shard_map/while/body/eval_jaxpr/ppermute | solution.py:33
  84.0 2.9 %collective-permute-done = bf16[128,768]{1,0:T(8,128)(2,1)S(1)} collective-permute-done((bf16[128,768]{1,0:T(8,128)(2,1)S(1)}, bf16[128,768]{1,0:T(8,128)(2,1)S(1)}, u32[]{:S(2)}, u32[]{:S(2)}) %collective-permute-start) | collective-permute-done | bytes 196640 | tf_op jit(solution)/shard_map/while/body/eval_jaxpr/ppermute | solution.py:29
  89.9 3.5 %collective-permute-done = bf16[128,768]{1,0:T(8,128)(2,1)S(1)} collective-permute-done((bf16[128,768]{1,0:T(8,128)(2,1)S(1)}, bf16[128,768]{1,0:T(8,128)(2,1)S(1)}, u32[]{:S(2)}, u32[]{:S(2)}) %collective-permute-start) | collective-permute-done | bytes 196640 | tf_op jit(solution)/shard_map/while/body/eval_jaxpr/ppermute | solution.py:29
  96.7 4.6 %collective-permute-done = bf16[128,768]{1,0:T(8,128)(2,1)S(1)} collective-permute-done((bf16[128,768]{1,0:T(8,128)(2,1)S(1)}, bf16[128,768]{1,0:T(8,128)(2,1)S(1)}, u32[]{:S(2)}, u32[]{:S(2)}) %collective-permute-start) | collective-permute-done | bytes 196640 | tf_op jit(solution)/shard_map/while/body/eval_jaxpr/ppermute | solution.py:29
  101.4 8.4 %collective-permute-start.21 = (bf16[1024,768]{1,0:T(8,128)(2,1)S(1)}, bf16[1024,768]{1,0:T(8,128)(2,1)S(1)}, u32[]{:S(2)}, u32[]{:S(2)}) collective-permute-start(bf16[1024,768]{1,0:T(8,128)(2,1)S(1)} %constant_dynamic-update-slice_fusion.5), channel_id=1, source_target_pairs={{0,16},{16,0},{1,17},{17,1},{2,18},{18,2},{3,19},{19,3},{4,20},{20... | collective-permute-start | bytes 4718600 | tf_op jit(solution)/shard_map/ppermute | solution.py:25
  112.8 15.7 %newton_schulz.1 = (f32[128,768]{1,0:T(8,128)}, bf16[128,768]{1,0:T(8,128)(2,1)S(1)}) custom-call(f32[768,768]{1,0:T(8,128)S(1)} %fusion.3.gram_ref, bf16[1024,768]{1,0:T(8,128)(2,1)S(1)} %collective-permute-done.21.other_ref, f32[128,768]{1,0:T(8,128)S(1)} %get-tuple-element.226.mom_ref, bf16[128,768]{1,0:T(8,128)(2,1)S(1)} %bitcast.26), custom_call_target="tpu_custom_call" | custom-call | flops 12683575296 | bytes 4718592 | tf_op jit(solution)/shard_map/newton_schulz/pallas_call | solution.py:359
  132.9 3.3 %collective-permute-done.24.refs_3_ = bf16[128,768]{1,0:T(8,128)(2,1)S(1)} collective-permute-done((bf16[128,768]{1,0:T(8,128)(2,1)S(1)}, bf16[128,768]{1,0:T(8,128)(2,1)S(1)}, u32[]{:S(2)}, u32[]{:S(2)}) %collective-permute-start.24) | collective-permute-done | bytes 196640 | tf_op jit(solution)/shard_map/ppermute | solution.py:37
  136.1 4.7 %collective-permute-done.23.refs_2_ = bf16[128,768]{1,0:T(8,128)(2,1)S(1)} collective-permute-done((bf16[128,768]{1,0:T(8,128)(2,1)S(1)}, bf16[128,768]{1,0:T(8,128)(2,1)S(1)}, u32[]{:S(2)}, u32[]{:S(2)}) %collective-permute-start.23) | collective-permute-done | bytes 196640 | tf_op jit(solution)/shard_map/ppermute | solution.py:37
  144.7 4.0 %collective-permute-done.25.refs_1_ = bf16[128,768]{1,0:T(8,128)(2,1)S(1)} collective-permute-done((bf16[128,768]{1,0:T(8,128)(2,1)S(1)}, bf16[128,768]{1,0:T(8,128)(2,1)S(1)}, u32[]{:S(2)}, u32[]{:S(2)}) %collective-permute-start.25) | collective-permute-done | bytes 196640 | tf_op jit(solution)/shard_map/ppermute | solution.py:37
  148.7 5.3 %collective-permute-done.26.refs_2_ = bf16[128,768]{1,0:T(8,128)(2,1)S(1)} collective-permute-done((bf16[128,768]{1,0:T(8,128)(2,1)S(1)}, bf16[128,768]{1,0:T(8,128)(2,1)S(1)}, u32[]{:S(2)}, u32[]{:S(2)}) %collective-permute-start.26) | collective-permute-done | bytes 196640 | tf_op jit(solution)/shard_map/ppermute | solution.py:37
  154.8 25.9 %while.35 = (s32[]{:T(128)}, bf16[128,768]{1,0:T(8,128)(2,1)S(1)}, bf16[128,768]{1,0:T(8,128)(2,1)S(1)}, bf16[1024,768]{1,0:T(8,128)(2,1)S(1)}, s32[]{:T(128)}, ...) while((s32[]{:T(128)}, bf16[128,768]{1,0:T(8,128)(2,1)S(1)}, bf16[128,768]{1,0:T(8,128)(2,1)S(1)}, ...), condition=%wide.region_3.0_spmd, body=%wide.region_2.0_spmd.sunk | while | flops 12 | bytes 3146025 | solution.py:403
  158.0 4.4 %collective-permute-done.2 = bf16[128,768]{1,0:T(8,128)(2,1)S(1)} collective-permute-done((bf16[128,768]{1,0:T(8,128)(2,1)S(1)}, bf16[128,768]{1,0:T(8,128)(2,1)S(1)}, u32[]{:S(2)}, u32[]{:S(2)}) %collective-permute-start.2) | collective-permute-done | bytes 196640 | tf_op jit(solution)/shard_map/while/body/eval_jaxpr/ppermute | solution.py:29
  165.4 3.5 %collective-permute-done.2 = bf16[128,768]{1,0:T(8,128)(2,1)S(1)} collective-permute-done((bf16[128,768]{1,0:T(8,128)(2,1)S(1)}, bf16[128,768]{1,0:T(8,128)(2,1)S(1)}, u32[]{:S(2)}, u32[]{:S(2)}) %collective-permute-start.2) | collective-permute-done | bytes 196640 | tf_op jit(solution)/shard_map/while/body/eval_jaxpr/ppermute | solution.py:29
  171.8 2.9 %collective-permute-done.2 = bf16[128,768]{1,0:T(8,128)(2,1)S(1)} collective-permute-done((bf16[128,768]{1,0:T(8,128)(2,1)S(1)}, bf16[128,768]{1,0:T(8,128)(2,1)S(1)}, u32[]{:S(2)}, u32[]{:S(2)}) %collective-permute-start.2) | collective-permute-done | bytes 196640 | tf_op jit(solution)/shard_map/while/body/eval_jaxpr/ppermute | solution.py:29
  177.7 2.9 %collective-permute-done.2 = bf16[128,768]{1,0:T(8,128)(2,1)S(1)} collective-permute-done((bf16[128,768]{1,0:T(8,128)(2,1)S(1)}, bf16[128,768]{1,0:T(8,128)(2,1)S(1)}, u32[]{:S(2)}, u32[]{:S(2)}) %collective-permute-start.2) | collective-permute-done | bytes 196640 | tf_op jit(solution)/shard_map/while/body/eval_jaxpr/ppermute | solution.py:29
  180.7 5.6 %collective-permute-start.28 = (bf16[1024,768]{1,0:T(8,128)(2,1)S(1)}, bf16[1024,768]{1,0:T(8,128)(2,1)S(1)}, u32[]{:S(2)}, u32[]{:S(2)}) collective-permute-start(bf16[1024,768]{1,0:T(8,128)(2,1)S(1)} %constant_dynamic-update-slice_fusion.4.blocks_ref), channel_id=1, source_target_pairs={{0,16},{16,0},{1,17},{17,1},{2,18},{18,2},{3,19},{19,3},{4,20},{20... | collective-permute-start | bytes 4718600 | tf_op jit(solution)/shard_map/ppermute | solution.py:25
  (134 shorter events, 56.1 us)
Async XLA Ops:
  0.6 7.7 %collective-permute-start.5 = (bf16[256,2048]{1,0:T(8,128)(2,1)}, bf16[256,2048]{1,0:T(8,128)(2,1)S(1)}, u32[]{:S(2)}, u32[]{:S(2)}) collective-permute-start(bf16[256,2048]{1,0:T(8,128)(2,1)} %bitcast.16), channel_id=1, source_target_pairs={{0,16},{16,0},{1,17},{17,1},{2,18},{18,2},{3,19},{19,3},{4,20},{20... | collective-permute-start | bytes 3145736 | tf_op jit(solution)/shard_map/ppermute | solution.py:25
  9.2 8.2 %collective-permute-start.11 = (bf16[128,768]{1,0:T(8,128)(2,1)S(1)}, bf16[128,768]{1,0:T(8,128)(2,1)S(1)}, u32[]{:S(2)}, u32[]{:S(2)}) collective-permute-start(bf16[128,768]{1,0:T(8,128)(2,1)S(1)} %get-tuple-element.194), channel_id=1, source_target_pairs={{32,0},{64,32},{96,64},{128,96},{160,128},{192,160},{224,192},{0,2... | collective-permute-start | bytes 589832 | tf_op jit(solution)/shard_map/ppermute | solution.py:33
  13.1 7.8 %collective-permute-start.7 = (bf16[128,768]{1,0:T(8,128)(2,1)S(1)}, bf16[128,768]{1,0:T(8,128)(2,1)S(1)}, u32[]{:S(2)}, u32[]{:S(2)}) collective-permute-start(bf16[128,768]{1,0:T(8,128)(2,1)S(1)} %get-tuple-element.190), channel_id=1, source_target_pairs={{0,32},{32,64},{64,96},{96,128},{128,160},{160,192},{192,224},{224... | collective-permute-start | bytes 589832 | tf_op jit(solution)/shard_map/ppermute | solution.py:29
  17.4 11.0 %collective-permute-start.12 = (bf16[256,768]{1,0:T(8,128)(2,1)S(1)}, bf16[256,768]{1,0:T(8,128)(2,1)S(1)}, u32[]{:S(2)}, u32[]{:S(2)}) collective-permute-start(bf16[256,768]{1,0:T(8,128)(2,1)S(1)} %pad_maximum_fusion.1), channel_id=1, source_target_pairs={{32,0},{64,32},{96,64},{128,96},{160,128},{192,160},{224,192},{0,2... | collective-permute-start | bytes 1179656 | tf_op jit(solution)/shard_map/ppermute | solution.py:33
  21.0 11.1 %collective-permute-start.8 = (bf16[256,768]{1,0:T(8,128)(2,1)S(1)}, bf16[256,768]{1,0:T(8,128)(2,1)S(1)}, u32[]{:S(2)}, u32[]{:S(2)}) collective-permute-start(bf16[256,768]{1,0:T(8,128)(2,1)S(1)} %pad_maximum_fusion), channel_id=1, source_target_pairs={{0,32},{32,64},{64,96},{96,128},{128,160},{160,192},{192,224},{224... | collective-permute-start | bytes 1179656 | tf_op jit(solution)/shard_map/ppermute | solution.py:29
  28.6 10.1 %collective-permute-start.13 = (bf16[256,768]{1,0:T(8,128)(2,1)S(1)}, bf16[256,768]{1,0:T(8,128)(2,1)S(1)}, u32[]{:S(2)}, u32[]{:S(2)}) collective-permute-start(bf16[256,768]{1,0:T(8,128)(2,1)S(1)} %add_convert_fusion.1), channel_id=1, source_target_pairs={{32,0},{64,32},{96,64},{128,96},{160,128},{192,160},{224,192},{0,2... | collective-permute-start | bytes 1179656 | tf_op jit(solution)/shard_map/ppermute | solution.py:33
  32.2 10.1 %collective-permute-start.9 = (bf16[256,768]{1,0:T(8,128)(2,1)S(1)}, bf16[256,768]{1,0:T(8,128)(2,1)S(1)}, u32[]{:S(2)}, u32[]{:S(2)}) collective-permute-start(bf16[256,768]{1,0:T(8,128)(2,1)S(1)} %add_convert_fusion.3), channel_id=1, source_target_pairs={{0,32},{32,64},{64,96},{96,128},{128,160},{160,192},{192,224},{224... | collective-permute-start | bytes 1179656 | tf_op jit(solution)/shard_map/ppermute | solution.py:29
  38.8 9.2 %collective-permute-start.14 = (bf16[256,768]{1,0:T(8,128)(2,1)S(1)}, bf16[256,768]{1,0:T(8,128)(2,1)S(1)}, u32[]{:S(2)}, u32[]{:S(2)}) collective-permute-start(bf16[256,768]{1,0:T(8,128)(2,1)S(1)} %add_convert_fusion), channel_id=1, source_target_pairs={{32,0},{64,32},{96,64},{128,96},{160,128},{192,160},{224,192},{0,2... | collective-permute-start | bytes 1179656 | tf_op jit(solution)/shard_map/ppermute | solution.py:33
  42.4 8.9 %collective-permute-start.10 = (bf16[256,768]{1,0:T(8,128)(2,1)S(1)}, bf16[256,768]{1,0:T(8,128)(2,1)S(1)}, u32[]{:S(2)}, u32[]{:S(2)}) collective-permute-start(bf16[256,768]{1,0:T(8,128)(2,1)S(1)} %add_convert_fusion.2), channel_id=1, source_target_pairs={{0,32},{32,64},{64,96},{96,128},{128,160},{160,192},{192,224},{224... | collective-permute-start | bytes 1179656 | tf_op jit(solution)/shard_map/ppermute | solution.py:29
  51.5 6.1 %collective-permute-start.17 = (bf16[128,768]{1,0:T(8,128)(2,1)S(1)}, bf16[128,768]{1,0:T(8,128)(2,1)S(1)}, u32[]{:S(2)}, u32[]{:S(2)}) collective-permute-start(bf16[128,768]{1,0:T(8,128)(2,1)S(1)} %slice.33.refs_0_), channel_id=1, source_target_pairs={{0,2},{1,3},{2,0},{3,1},{4,6},{5,7},{6,4},{7,5},{8,10},{9,11},{10,... | collective-permute-start | bytes 589832 | tf_op jit(solution)/shard_map/ppermute | solution.py:37
  54.5 5.9 %collective-permute-start.16 = (bf16[128,768]{1,0:T(8,128)(2,1)S(1)}, bf16[128,768]{1,0:T(8,128)(2,1)S(1)}, u32[]{:S(2)}, u32[]{:S(2)}) collective-permute-start(bf16[128,768]{1,0:T(8,128)(2,1)S(1)} %slice.33.refs_0_), channel_id=1, source_target_pairs={{0,3},{1,0},{2,1},{3,2},{4,7},{5,4},{6,5},{7,6},{8,11},{9,8},{10,9... | collective-permute-start | bytes 589832 | tf_op jit(solution)/shard_map/ppermute | solution.py:37
  55.3 7.8 %collective-permute-start.15 = (bf16[128,768]{1,0:T(8,128)(2,1)S(1)}, bf16[128,768]{1,0:T(8,128)(2,1)S(1)}, u32[]{:S(2)}, u32[]{:S(2)}) collective-permute-start(bf16[128,768]{1,0:T(8,128)(2,1)S(1)} %slice.33.refs_0_), channel_id=1, source_target_pairs={{0,1},{1,2},{2,3},{3,0},{4,5},{5,6},{6,7},{7,4},{8,9},{9,10},{10,1... | collective-permute-start | bytes 589832 | tf_op jit(solution)/shard_map/ppermute | solution.py:37
  64.1 6.1 %collective-permute-start.18 = (bf16[128,768]{1,0:T(8,128)(2,1)S(1)}, bf16[128,768]{1,0:T(8,128)(2,1)S(1)}, u32[]{:S(2)}, u32[]{:S(2)}) collective-permute-start(bf16[128,768]{1,0:T(8,128)(2,1)S(1)} %get-tuple-element.196), channel_id=1, source_target_pairs={{0,8},{4,12},{8,0},{12,4},{1,9},{5,13},{9,1},{13,5},{2,10},{6,14},... | collective-permute-start | bytes 589832 | tf_op jit(solution)/shard_map/ppermute | solution.py:37
  67.0 7.8 %collective-permute-start.19 = (bf16[128,768]{1,0:T(8,128)(2,1)S(1)}, bf16[128,768]{1,0:T(8,128)(2,1)S(1)}, u32[]{:S(2)}, u32[]{:S(2)}) collective-permute-start(bf16[128,768]{1,0:T(8,128)(2,1)S(1)} %get-tuple-element.197), channel_id=1, source_target_pairs={{0,4},{4,8},{8,12},{12,0},{1,5},{5,9},{9,13},{13,1},{2,6},{6,10},{... | collective-permute-start | bytes 589832 | tf_op jit(solution)/shard_map/ppermute | solution.py:37
  67.3 7.5 %collective-permute-start.20 = (bf16[128,768]{1,0:T(8,128)(2,1)S(1)}, bf16[128,768]{1,0:T(8,128)(2,1)S(1)}, u32[]{:S(2)}, u32[]{:S(2)}) collective-permute-start(bf16[128,768]{1,0:T(8,128)(2,1)S(1)} %get-tuple-element.198), channel_id=1, source_target_pairs={{0,12},{4,0},{8,4},{12,8},{1,13},{5,1},{9,5},{13,9},{2,14},{6,2},{... | collective-permute-start | bytes 589832 | tf_op jit(solution)/shard_map/ppermute | solution.py:37
  75.1 5.8 %collective-permute-start = (bf16[128,768]{1,0:T(8,128)(2,1)S(1)}, bf16[128,768]{1,0:T(8,128)(2,1)S(1)}, u32[]{:S(2)}, u32[]{:S(2)}) collective-permute-start(bf16[128,768]{1,0:T(8,128)(2,1)S(1)} %copy.19), channel_id=1, source_target_pairs={{0,32},{32,64},{64,96},{96,128},{128,160},{160,192},{192,224},{224... | collective-permute-start | bytes 589832 | tf_op jit(solution)/shard_map/while/body/eval_jaxpr/ppermute | solution.py:29
  81.0 5.9 %collective-permute-start = (bf16[128,768]{1,0:T(8,128)(2,1)S(1)}, bf16[128,768]{1,0:T(8,128)(2,1)S(1)}, u32[]{:S(2)}, u32[]{:S(2)}) collective-permute-start(bf16[128,768]{1,0:T(8,128)(2,1)S(1)} %copy.19), channel_id=1, source_target_pairs={{0,32},{32,64},{64,96},{96,128},{128,160},{160,192},{192,224},{224... | collective-permute-start | bytes 589832 | tf_op jit(solution)/shard_map/while/body/eval_jaxpr/ppermute | solution.py:29
  86.9 6.5 %collective-permute-start = (bf16[128,768]{1,0:T(8,128)(2,1)S(1)}, bf16[128,768]{1,0:T(8,128)(2,1)S(1)}, u32[]{:S(2)}, u32[]{:S(2)}) collective-permute-start(bf16[128,768]{1,0:T(8,128)(2,1)S(1)} %copy.19), channel_id=1, source_target_pairs={{0,32},{32,64},{64,96},{96,128},{128,160},{160,192},{192,224},{224... | collective-permute-start | bytes 589832 | tf_op jit(solution)/shard_map/while/body/eval_jaxpr/ppermute | solution.py:29
  93.4 7.9 %collective-permute-start = (bf16[128,768]{1,0:T(8,128)(2,1)S(1)}, bf16[128,768]{1,0:T(8,128)(2,1)S(1)}, u32[]{:S(2)}, u32[]{:S(2)}) collective-permute-start(bf16[128,768]{1,0:T(8,128)(2,1)S(1)} %copy.19), channel_id=1, source_target_pairs={{0,32},{32,64},{64,96},{96,128},{128,160},{160,192},{192,224},{224... | collective-permute-start | bytes 589832 | tf_op jit(solution)/shard_map/while/body/eval_jaxpr/ppermute | solution.py:29
  94.3 7.1 %collective-permute-start.1 = (bf16[128,768]{1,0:T(8,128)(2,1)S(1)}, bf16[128,768]{1,0:T(8,128)(2,1)S(1)}, u32[]{:S(2)}, u32[]{:S(2)}) collective-permute-start(bf16[128,768]{1,0:T(8,128)(2,1)S(1)} %copy.20), channel_id=1, source_target_pairs={{32,0},{64,32},{96,64},{128,96},{160,128},{192,160},{224,192},{0,2... | collective-permute-start | bytes 589832 | tf_op jit(solution)/shard_map/while/body/eval_jaxpr/ppermute | solution.py:33
  101.4 11.4 %collective-permute-start.21 = (bf16[1024,768]{1,0:T(8,128)(2,1)S(1)}, bf16[1024,768]{1,0:T(8,128)(2,1)S(1)}, u32[]{:S(2)}, u32[]{:S(2)}) collective-permute-start(bf16[1024,768]{1,0:T(8,128)(2,1)S(1)} %constant_dynamic-update-slice_fusion.5), channel_id=1, source_target_pairs={{0,16},{16,0},{1,17},{17,1},{2,18},{18,2},{3,19},{19,3},{4,20},{20... | collective-permute-start | bytes 4718600 | tf_op jit(solution)/shard_map/ppermute | solution.py:25
  128.5 7.6 %collective-permute-start.24 = (bf16[128,768]{1,0:T(8,128)(2,1)S(1)}, bf16[128,768]{1,0:T(8,128)(2,1)S(1)}, u32[]{:S(2)}, u32[]{:S(2)}) collective-permute-start(bf16[128,768]{1,0:T(8,128)(2,1)S(1)} %get-tuple-element.202.refs_0_), channel_id=1, source_target_pairs={{0,8},{4,12},{8,0},{12,4},{1,9},{5,13},{9,1},{13,5},{2,10},{6,14},... | collective-permute-start | bytes 589832 | tf_op jit(solution)/shard_map/ppermute | solution.py:37
  131.0 9.8 %collective-permute-start.23 = (bf16[128,768]{1,0:T(8,128)(2,1)S(1)}, bf16[128,768]{1,0:T(8,128)(2,1)S(1)}, u32[]{:S(2)}, u32[]{:S(2)}) collective-permute-start(bf16[128,768]{1,0:T(8,128)(2,1)S(1)} %get-tuple-element.202.refs_0_), channel_id=1, source_target_pairs={{0,12},{4,0},{8,4},{12,8},{1,13},{5,1},{9,5},{13,9},{2,14},{6,2},{... | collective-permute-start | bytes 589832 | tf_op jit(solution)/shard_map/ppermute | solution.py:37
  132.9 8.0 %collective-permute-start.22 = (bf16[128,768]{1,0:T(8,128)(2,1)S(1)}, bf16[128,768]{1,0:T(8,128)(2,1)S(1)}, u32[]{:S(2)}, u32[]{:S(2)}) collective-permute-start(bf16[128,768]{1,0:T(8,128)(2,1)S(1)} %get-tuple-element.202.refs_0_), channel_id=1, source_target_pairs={{0,4},{4,8},{8,12},{12,0},{1,5},{5,9},{9,13},{13,1},{2,6},{6,10},{... | collective-permute-start | bytes 589832 | tf_op jit(solution)/shard_map/ppermute | solution.py:37
  141.8 6.9 %collective-permute-start.25 = (bf16[128,768]{1,0:T(8,128)(2,1)S(1)}, bf16[128,768]{1,0:T(8,128)(2,1)S(1)}, u32[]{:S(2)}, u32[]{:S(2)}) collective-permute-start(bf16[128,768]{1,0:T(8,128)(2,1)S(1)} %get-tuple-element.204), channel_id=1, source_target_pairs={{0,2},{1,3},{2,0},{3,1},{4,6},{5,7},{6,4},{7,5},{8,10},{9,11},{10,... | collective-permute-start | bytes 589832 | tf_op jit(solution)/shard_map/ppermute | solution.py:37
  141.9 12.1 %collective-permute-start.26 = (bf16[128,768]{1,0:T(8,128)(2,1)S(1)}, bf16[128,768]{1,0:T(8,128)(2,1)S(1)}, u32[]{:S(2)}, u32[]{:S(2)}) collective-permute-start(bf16[128,768]{1,0:T(8,128)(2,1)S(1)} %get-tuple-element.205), channel_id=1, source_target_pairs={{0,1},{1,2},{2,3},{3,0},{4,5},{5,6},{6,7},{7,4},{8,9},{9,10},{10,1... | collective-permute-start | bytes 589832 | tf_op jit(solution)/shard_map/ppermute | solution.py:37
  142.0 12.0 %collective-permute-start.27 = (bf16[128,768]{1,0:T(8,128)(2,1)S(1)}, bf16[128,768]{1,0:T(8,128)(2,1)S(1)}, u32[]{:S(2)}, u32[]{:S(2)}) collective-permute-start(bf16[128,768]{1,0:T(8,128)(2,1)S(1)} %get-tuple-element.206), channel_id=1, source_target_pairs={{0,3},{1,0},{2,1},{3,2},{4,7},{5,4},{6,5},{7,6},{8,11},{9,8},{10,9... | collective-permute-start | bytes 589832 | tf_op jit(solution)/shard_map/ppermute | solution.py:37
  154.8 7.6 %collective-permute-start.2 = (bf16[128,768]{1,0:T(8,128)(2,1)S(1)}, bf16[128,768]{1,0:T(8,128)(2,1)S(1)}, u32[]{:S(2)}, u32[]{:S(2)}) collective-permute-start(bf16[128,768]{1,0:T(8,128)(2,1)S(1)} %copy.32), channel_id=1, source_target_pairs={{0,32},{32,64},{64,96},{96,128},{128,160},{160,192},{192,224},{224... | collective-permute-start | bytes 589832 | tf_op jit(solution)/shard_map/while/body/eval_jaxpr/ppermute | solution.py:29
  155.8 6.6 %collective-permute-start.3 = (bf16[128,768]{1,0:T(8,128)(2,1)S(1)}, bf16[128,768]{1,0:T(8,128)(2,1)S(1)}, u32[]{:S(2)}, u32[]{:S(2)}) collective-permute-start(bf16[128,768]{1,0:T(8,128)(2,1)S(1)} %copy.33), channel_id=1, source_target_pairs={{32,0},{64,32},{96,64},{128,96},{160,128},{192,160},{224,192},{0,2... | collective-permute-start | bytes 589832 | tf_op jit(solution)/shard_map/while/body/eval_jaxpr/ppermute | solution.py:33
  162.5 6.4 %collective-permute-start.2 = (bf16[128,768]{1,0:T(8,128)(2,1)S(1)}, bf16[128,768]{1,0:T(8,128)(2,1)S(1)}, u32[]{:S(2)}, u32[]{:S(2)}) collective-permute-start(bf16[128,768]{1,0:T(8,128)(2,1)S(1)} %copy.32), channel_id=1, source_target_pairs={{0,32},{32,64},{64,96},{96,128},{128,160},{160,192},{192,224},{224... | collective-permute-start | bytes 589832 | tf_op jit(solution)/shard_map/while/body/eval_jaxpr/ppermute | solution.py:29
  174.7 5.9 %collective-permute-start.2 = (bf16[128,768]{1,0:T(8,128)(2,1)S(1)}, bf16[128,768]{1,0:T(8,128)(2,1)S(1)}, u32[]{:S(2)}, u32[]{:S(2)}) collective-permute-start(bf16[128,768]{1,0:T(8,128)(2,1)S(1)} %copy.32), channel_id=1, source_target_pairs={{0,32},{32,64},{64,96},{96,128},{128,160},{160,192},{192,224},{224... | collective-permute-start | bytes 589832 | tf_op jit(solution)/shard_map/while/body/eval_jaxpr/ppermute | solution.py:29
  180.7 8.7 %collective-permute-start.28 = (bf16[1024,768]{1,0:T(8,128)(2,1)S(1)}, bf16[1024,768]{1,0:T(8,128)(2,1)S(1)}, u32[]{:S(2)}, u32[]{:S(2)}) collective-permute-start(bf16[1024,768]{1,0:T(8,128)(2,1)S(1)} %constant_dynamic-update-slice_fusion.4.blocks_ref), channel_id=1, source_target_pairs={{0,16},{16,0},{1,17},{17,1},{2,18},{18,2},{3,19},{19,3},{4,20},{20... | collective-permute-start | bytes 4718600 | tf_op jit(solution)/shard_map/ppermute | solution.py:25
  (19 other events, 160.0 us)

commit v5 on v4

--- a/solution.py
+++ b/solution.py
@@ -404,6 +404,25 @@
     return lax.dynamic_update_slice(got, far, (0, 0))
 
 
+def split_ring(block):
+    rows, width = block.shape
+
+    def one(step, carry):
+        below, above, got = carry
+        got = lax.dynamic_update_slice(got, below, ((4 - step) * rows, 0))
+        got = lax.dynamic_update_slice(got, above, ((4 + step) * rows, 0))
+        return up(below), down(above), got
+
+    got = jnp.zeros((NZ * rows, width), block.dtype)
+    below, above, got = lax.fori_loop(0, 3, one, (block, block, got))
+    half = rows // 2
+    far = (up(below[:half]), down(above[half:]))
+    got = lax.dynamic_update_slice(got, below, (rows, 0))
+    got = lax.dynamic_update_slice(got, above, (7 * rows, 0))
+    got = lax.dynamic_update_slice(got, far[0], (0, 0))
+    return lax.dynamic_update_slice(got, far[1], (half, 0))
+
+
 def body(tokens_in, out_grads, counts, copy_list, weights, momentum):
     acts = tokens_in[0]
     grads = out_grads[0]
@@ -437,7 +456,7 @@
     pieces = [kept] + [shift(sent[offset - 1], "y", offset) for offset in FAR_FIRST[1:]]
     replica = pick(here, copy_list, pieces)
 
-    own = ring(replica)
+    own = split_ring(replica)
     full = place(1, here, swap(own), place(0, here, own))
     return (fresh_mom[None], update[None], full[None])
 

time: 191 us -> 193 us (1.010)
  transfers between devices with their start and end apart: 41 -> 41, of which waited for: 24 -> 24; matrix products, arithmetic and copies ran while one was open for 1% -> 1% of each run, Pallas kernels for 3% -> 2%
where the time goes in v5:
time: 193 us; the launch traced here: 192 us
  waiting for transfers between devices  86.6 us (45%)
  starting transfers between devices  72.7 us (38%)
  Pallas kernels  25.7 us (13%)
  local copies, waits for them, and re-layouts  3.74 us (2%)
    ppermute x12, starting transfers between devices, down(): return lax.ppermute(value, 'z', [((i + 1) % NZ, i) for i in range(NZ)])  33.2 us
    ppermute x12, waiting for transfers between devices, up(): return lax.ppermute(value, 'z', [(i, (i + 1) % NZ) for i in range(NZ)])  32.8 us
    ppermute x12, waiting for transfers between devices, shift(): return lax.ppermute(value, axis, [(i, (i + offset) % 4) for i in range(4)])  29.6 us
    ppermute x12, waiting for transfers between devices, down(): return lax.ppermute(value, 'z', [((i + 1) % NZ, i) for i in range(NZ)])  21.3 us
    ppermute x5, starting transfers between devices, swap(): return lax.ppermute(value, 'core', [(0, 1), (1, 0)])  17.3 us
    ppermute x12, starting transfers between devices, shift(): return lax.ppermute(value, axis, [(i, (i + offset) % 4) for i in range(4)])  17.2 us
    pallas_call x1, Pallas kernels, newton_schulz(): pl.pallas_call(functools.partial(newton_kernel, 0.2 * math.sqrt(longest))...  15.7 us
    ppermute x12, starting transfers between devices, up(): return lax.ppermute(value, 'z', [(i, (i + 1) % NZ) for i in range(NZ)])  4.97 us
  transfers between devices with their start and end apart: 41, of which 24 were waited for; matrix products, arithmetic and copies ran while one was open for 1% of the time, Pallas kernels for 2%

profile of v5, /device:TPU:1, one launch (start us, length us, event | category | flops | bytes accessed | tf_op | source)
XLA Modules:
  0.0 192.4 jit_solution(145691451529544459)
XLA Ops:
  0.6 3.3 %collective-permute-start.5 = (bf16[256,2048]{1,0:T(8,128)(2,1)}, bf16[256,2048]{1,0:T(8,128)(2,1)S(1)}, u32[]{:S(2)}, u32[]{:S(2)}) collective-permute-start(bf16[256,2048]{1,0:T(8,128)(2,1)} %bitcast.16), channel_id=1, source_target_pairs={{0,16},{16,0},{1,17},{17,1},{2,18},{18,2},{3,19},{19,3},{4,20},{20... | collective-permute-start | bytes 3145736 | tf_op jit(solution)/shard_map/ppermute | solution.py:25
  9.2 3.9 %collective-permute-start.11 = (bf16[128,768]{1,0:T(8,128)(2,1)S(1)}, bf16[128,768]{1,0:T(8,128)(2,1)S(1)}, u32[]{:S(2)}, u32[]{:S(2)}) collective-permute-start(bf16[128,768]{1,0:T(8,128)(2,1)S(1)} %get-tuple-element.195), channel_id=1, source_target_pairs={{32,0},{64,32},{96,64},{128,96},{160,128},{192,160},{224,192},{0,2... | collective-permute-start | bytes 589832 | tf_op jit(solution)/shard_map/ppermute | solution.py:33
  17.4 3.5 %collective-permute-start.12 = (bf16[256,768]{1,0:T(8,128)(2,1)S(1)}, bf16[256,768]{1,0:T(8,128)(2,1)S(1)}, u32[]{:S(2)}, u32[]{:S(2)}) collective-permute-start(bf16[256,768]{1,0:T(8,128)(2,1)S(1)} %pad_maximum_fusion.1), channel_id=1, source_target_pairs={{32,0},{64,32},{96,64},{128,96},{160,128},{192,160},{224,192},{0,2... | collective-permute-start | bytes 1179656 | tf_op jit(solution)/shard_map/ppermute | solution.py:33
  21.1 7.4 %collective-permute-done.12 = bf16[256,768]{1,0:T(8,128)(2,1)S(1)} collective-permute-done((bf16[256,768]{1,0:T(8,128)(2,1)S(1)}, bf16[256,768]{1,0:T(8,128)(2,1)S(1)}, u32[]{:S(2)}, u32[]{:S(2)}) %collective-permute-start.12) | collective-permute-done | bytes 393248 | tf_op jit(solution)/shard_map/ppermute | solution.py:33
  28.6 3.5 %collective-permute-start.13 = (bf16[256,768]{1,0:T(8,128)(2,1)S(1)}, bf16[256,768]{1,0:T(8,128)(2,1)S(1)}, u32[]{:S(2)}, u32[]{:S(2)}) collective-permute-start(bf16[256,768]{1,0:T(8,128)(2,1)S(1)} %add_convert_fusion.1), channel_id=1, source_target_pairs={{32,0},{64,32},{96,64},{128,96},{160,128},{192,160},{224,192},{0,2... | collective-permute-start | bytes 1179656 | tf_op jit(solution)/shard_map/ppermute | solution.py:33
  32.3 6.4 %collective-permute-done.13 = bf16[256,768]{1,0:T(8,128)(2,1)S(1)} collective-permute-done((bf16[256,768]{1,0:T(8,128)(2,1)S(1)}, bf16[256,768]{1,0:T(8,128)(2,1)S(1)}, u32[]{:S(2)}, u32[]{:S(2)}) %collective-permute-start.13) | collective-permute-done | bytes 393248 | tf_op jit(solution)/shard_map/ppermute | solution.py:33
  38.8 3.5 %collective-permute-start.14 = (bf16[256,768]{1,0:T(8,128)(2,1)S(1)}, bf16[256,768]{1,0:T(8,128)(2,1)S(1)}, u32[]{:S(2)}, u32[]{:S(2)}) collective-permute-start(bf16[256,768]{1,0:T(8,128)(2,1)S(1)} %add_convert_fusion), channel_id=1, source_target_pairs={{32,0},{64,32},{96,64},{128,96},{160,128},{192,160},{224,192},{0,2... | collective-permute-start | bytes 1179656 | tf_op jit(solution)/shard_map/ppermute | solution.py:33
  42.5 5.5 %collective-permute-done.14 = bf16[256,768]{1,0:T(8,128)(2,1)S(1)} collective-permute-done((bf16[256,768]{1,0:T(8,128)(2,1)S(1)}, bf16[256,768]{1,0:T(8,128)(2,1)S(1)}, u32[]{:S(2)}, u32[]{:S(2)}) %collective-permute-start.14) | collective-permute-done | bytes 393248 | tf_op jit(solution)/shard_map/ppermute | solution.py:33
  48.0 3.3 %collective-permute-done.10 = bf16[256,768]{1,0:T(8,128)(2,1)S(1)} collective-permute-done((bf16[256,768]{1,0:T(8,128)(2,1)S(1)}, bf16[256,768]{1,0:T(8,128)(2,1)S(1)}, u32[]{:S(2)}, u32[]{:S(2)}) %collective-permute-start.10) | collective-permute-done | bytes 393248 | tf_op jit(solution)/shard_map/ppermute | solution.py:29
  51.5 3.0 %collective-permute-start.17 = (bf16[128,768]{1,0:T(8,128)(2,1)S(1)}, bf16[128,768]{1,0:T(8,128)(2,1)S(1)}, u32[]{:S(2)}, u32[]{:S(2)}) collective-permute-start(bf16[128,768]{1,0:T(8,128)(2,1)S(1)} %slice.41.refs_0_), channel_id=1, source_target_pairs={{0,2},{1,3},{2,0},{3,1},{4,6},{5,7},{6,4},{7,5},{8,10},{9,11},{10,... | collective-permute-start | bytes 589832 | tf_op jit(solution)/shard_map/ppermute | solution.py:37
  60.4 2.8 %collective-permute-done.15.refs_1_ = bf16[128,768]{1,0:T(8,128)(2,1)S(1)} collective-permute-done((bf16[128,768]{1,0:T(8,128)(2,1)S(1)}, bf16[128,768]{1,0:T(8,128)(2,1)S(1)}, u32[]{:S(2)}, u32[]{:S(2)}) %collective-permute-start.15) | collective-permute-done | bytes 196640 | tf_op jit(solution)/shard_map/ppermute | solution.py:37
  64.1 2.8 %collective-permute-start.18 = (bf16[128,768]{1,0:T(8,128)(2,1)S(1)}, bf16[128,768]{1,0:T(8,128)(2,1)S(1)}, u32[]{:S(2)}, u32[]{:S(2)}) collective-permute-start(bf16[128,768]{1,0:T(8,128)(2,1)S(1)} %get-tuple-element.197), channel_id=1, source_target_pairs={{0,8},{4,12},{8,0},{12,4},{1,9},{5,13},{9,1},{13,5},{2,10},{6,14},... | collective-permute-start | bytes 589832 | tf_op jit(solution)/shard_map/ppermute | solution.py:37
  70.2 4.6 %collective-permute-done.19 = bf16[128,768]{1,0:T(8,128)(2,1)S(1)} collective-permute-done((bf16[128,768]{1,0:T(8,128)(2,1)S(1)}, bf16[128,768]{1,0:T(8,128)(2,1)S(1)}, u32[]{:S(2)}, u32[]{:S(2)}) %collective-permute-start.19) | collective-permute-done | bytes 196640 | tf_op jit(solution)/shard_map/ppermute | solution.py:37
  75.1 26.3 %while.34 = (s32[]{:T(128)}, bf16[128,768]{1,0:T(8,128)(2,1)S(1)}, bf16[128,768]{1,0:T(8,128)(2,1)S(1)}, bf16[1024,768]{1,0:T(8,128)(2,1)S(1)}, s32[]{:T(128)}, ...) while((s32[]{:T(128)}, bf16[128,768]{1,0:T(8,128)(2,1)S(1)}, bf16[128,768]{1,0:T(8,128)(2,1)S(1)}, ...), condition=%wide.region_1.0_spmd, body=%wide.region_0.0_spmd.sunk | while | flops 12 | bytes 3146025 | solution.py:403
  78.0 2.9 %collective-permute-done = bf16[128,768]{1,0:T(8,128)(2,1)S(1)} collective-permute-done((bf16[128,768]{1,0:T(8,128)(2,1)S(1)}, bf16[128,768]{1,0:T(8,128)(2,1)S(1)}, u32[]{:S(2)}, u32[]{:S(2)}) %collective-permute-start) | collective-permute-done | bytes 196640 | tf_op jit(solution)/shard_map/while/body/eval_jaxpr/ppermute | solution.py:29
  81.1 2.8 %collective-permute-start.1 = (bf16[128,768]{1,0:T(8,128)(2,1)S(1)}, bf16[128,768]{1,0:T(8,128)(2,1)S(1)}, u32[]{:S(2)}, u32[]{:S(2)}) collective-permute-start(bf16[128,768]{1,0:T(8,128)(2,1)S(1)} %copy.20), channel_id=1, source_target_pairs={{32,0},{64,32},{96,64},{128,96},{160,128},{192,160},{224,192},{0,2... | collective-permute-start | bytes 589832 | tf_op jit(solution)/shard_map/while/body/eval_jaxpr/ppermute | solution.py:33
  84.0 2.9 %collective-permute-done = bf16[128,768]{1,0:T(8,128)(2,1)S(1)} collective-permute-done((bf16[128,768]{1,0:T(8,128)(2,1)S(1)}, bf16[128,768]{1,0:T(8,128)(2,1)S(1)}, u32[]{:S(2)}, u32[]{:S(2)}) %collective-permute-start) | collective-permute-done | bytes 196640 | tf_op jit(solution)/shard_map/while/body/eval_jaxpr/ppermute | solution.py:29
  89.9 3.5 %collective-permute-done = bf16[128,768]{1,0:T(8,128)(2,1)S(1)} collective-permute-done((bf16[128,768]{1,0:T(8,128)(2,1)S(1)}, bf16[128,768]{1,0:T(8,128)(2,1)S(1)}, u32[]{:S(2)}, u32[]{:S(2)}) %collective-permute-start) | collective-permute-done | bytes 196640 | tf_op jit(solution)/shard_map/while/body/eval_jaxpr/ppermute | solution.py:29
  96.7 4.6 %collective-permute-done = bf16[128,768]{1,0:T(8,128)(2,1)S(1)} collective-permute-done((bf16[128,768]{1,0:T(8,128)(2,1)S(1)}, bf16[128,768]{1,0:T(8,128)(2,1)S(1)}, u32[]{:S(2)}, u32[]{:S(2)}) %collective-permute-start) | collective-permute-done | bytes 196640 | tf_op jit(solution)/shard_map/while/body/eval_jaxpr/ppermute | solution.py:29
  101.4 8.4 %collective-permute-start.21 = (bf16[1024,768]{1,0:T(8,128)(2,1)S(1)}, bf16[1024,768]{1,0:T(8,128)(2,1)S(1)}, u32[]{:S(2)}, u32[]{:S(2)}) collective-permute-start(bf16[1024,768]{1,0:T(8,128)(2,1)S(1)} %constant_dynamic-update-slice_fusion.8), channel_id=1, source_target_pairs={{0,16},{16,0},{1,17},{17,1},{2,18},{18,2},{3,19},{19,3},{4,20},{20... | collective-permute-start | bytes 4718600 | tf_op jit(solution)/shard_map/ppermute | solution.py:25
  112.8 15.7 %newton_schulz.1 = (f32[128,768]{1,0:T(8,128)}, bf16[128,768]{1,0:T(8,128)(2,1)S(1)}) custom-call(f32[768,768]{1,0:T(8,128)S(1)} %fusion.3.gram_ref, bf16[1024,768]{1,0:T(8,128)(2,1)S(1)} %collective-permute-done.21.other_ref, f32[128,768]{1,0:T(8,128)S(1)} %get-tuple-element.228.mom_ref, bf16[128,768]{1,0:T(8,128)(2,1)S(1)} %bitcast.26), custom_call_target="tpu_custom_call" | custom-call | flops 12683575296 | bytes 4718592 | tf_op jit(solution)/shard_map/newton_schulz/pallas_call | solution.py:359
  132.9 3.3 %collective-permute-done.24.refs_3_ = bf16[128,768]{1,0:T(8,128)(2,1)S(1)} collective-permute-done((bf16[128,768]{1,0:T(8,128)(2,1)S(1)}, bf16[128,768]{1,0:T(8,128)(2,1)S(1)}, u32[]{:S(2)}, u32[]{:S(2)}) %collective-permute-start.24) | collective-permute-done | bytes 196640 | tf_op jit(solution)/shard_map/ppermute | solution.py:37
  136.1 4.7 %collective-permute-done.23.refs_2_ = bf16[128,768]{1,0:T(8,128)(2,1)S(1)} collective-permute-done((bf16[128,768]{1,0:T(8,128)(2,1)S(1)}, bf16[128,768]{1,0:T(8,128)(2,1)S(1)}, u32[]{:S(2)}, u32[]{:S(2)}) %collective-permute-start.23) | collective-permute-done | bytes 196640 | tf_op jit(solution)/shard_map/ppermute | solution.py:37
  144.7 4.0 %collective-permute-done.25.refs_1_ = bf16[128,768]{1,0:T(8,128)(2,1)S(1)} collective-permute-done((bf16[128,768]{1,0:T(8,128)(2,1)S(1)}, bf16[128,768]{1,0:T(8,128)(2,1)S(1)}, u32[]{:S(2)}, u32[]{:S(2)}) %collective-permute-start.25) | collective-permute-done | bytes 196640 | tf_op jit(solution)/shard_map/ppermute | solution.py:37
  148.7 5.3 %collective-permute-done.26.refs_2_ = bf16[128,768]{1,0:T(8,128)(2,1)S(1)} collective-permute-done((bf16[128,768]{1,0:T(8,128)(2,1)S(1)}, bf16[128,768]{1,0:T(8,128)(2,1)S(1)}, u32[]{:S(2)}, u32[]{:S(2)}) %collective-permute-start.26) | collective-permute-done | bytes 196640 | tf_op jit(solution)/shard_map/ppermute | solution.py:37
  154.8 19.9 %while.35 = (s32[]{:T(128)}, bf16[128,768]{1,0:T(8,128)(2,1)S(1)}, bf16[128,768]{1,0:T(8,128)(2,1)S(1)}, bf16[1024,768]{1,0:T(8,128)(2,1)S(1)}, s32[]{:T(128)}, ...) while((s32[]{:T(128)}, bf16[128,768]{1,0:T(8,128)(2,1)S(1)}, bf16[128,768]{1,0:T(8,128)(2,1)S(1)}, ...), condition=%wide.region_3.0_spmd, body=%wide.region_2.0_spmd.sunk | while | flops 12 | bytes 3146025 | solution.py:417
  158.0 4.4 %collective-permute-done.2 = bf16[128,768]{1,0:T(8,128)(2,1)S(1)} collective-permute-done((bf16[128,768]{1,0:T(8,128)(2,1)S(1)}, bf16[128,768]{1,0:T(8,128)(2,1)S(1)}, u32[]{:S(2)}, u32[]{:S(2)}) %collective-permute-start.2) | collective-permute-done | bytes 196640 | tf_op jit(solution)/shard_map/while/body/eval_jaxpr/ppermute | solution.py:29
  165.4 3.5 %collective-permute-done.2 = bf16[128,768]{1,0:T(8,128)(2,1)S(1)} collective-permute-done((bf16[128,768]{1,0:T(8,128)(2,1)S(1)}, bf16[128,768]{1,0:T(8,128)(2,1)S(1)}, u32[]{:S(2)}, u32[]{:S(2)}) %collective-permute-start.2) | collective-permute-done | bytes 196640 | tf_op jit(solution)/shard_map/while/body/eval_jaxpr/ppermute | solution.py:29
  171.8 2.9 %collective-permute-done.2 = bf16[128,768]{1,0:T(8,128)(2,1)S(1)} collective-permute-done((bf16[128,768]{1,0:T(8,128)(2,1)S(1)}, bf16[128,768]{1,0:T(8,128)(2,1)S(1)}, u32[]{:S(2)}, u32[]{:S(2)}) %collective-permute-start.2) | collective-permute-done | bytes 196640 | tf_op jit(solution)/shard_map/while/body/eval_jaxpr/ppermute | solution.py:29
  174.8 2.8 %collective-permute-start.29 = (bf16[64,768]{1,0:T(8,128)(2,1)S(1)}, bf16[64,768]{1,0:T(8,128)(2,1)S(1)}, u32[]{:S(2)}, u32[]{:S(2)}) collective-permute-start(bf16[64,768]{1,0:T(8,128)(2,1)S(1)} %slice.32), channel_id=1, source_target_pairs={{32,0},{64,32},{96,64},{128,96},{160,128},{192,160},{224,192},{0,2... | collective-permute-start | bytes 294920 | tf_op jit(solution)/shard_map/ppermute | solution.py:33
  177.6 4.7 %collective-permute-done.28 = bf16[64,768]{1,0:T(8,128)(2,1)S(1)} collective-permute-done((bf16[64,768]{1,0:T(8,128)(2,1)S(1)}, bf16[64,768]{1,0:T(8,128)(2,1)S(1)}, u32[]{:S(2)}, u32[]{:S(2)}) %collective-permute-start.28) | collective-permute-done | bytes 98336 | tf_op jit(solution)/shard_map/ppermute | solution.py:29
  182.3 5.1 %collective-permute-start.30 = (bf16[1024,768]{1,0:T(8,128)(2,1)S(1)}, bf16[1024,768]{1,0:T(8,128)(2,1)S(1)}, u32[]{:S(2)}, u32[]{:S(2)}) collective-permute-start(bf16[1024,768]{1,0:T(8,128)(2,1)S(1)} %constant_dynamic-update-slice_fusion.4.blocks_ref), channel_id=1, source_target_pairs={{0,16},{16,0},{1,17},{17,1},{2,18},{18,2},{3,19},{19,3},{4,20},{20... | collective-permute-start | bytes 4718600 | tf_op jit(solution)/shard_map/ppermute | solution.py:25
  (135 shorter events, 55.9 us)
Async XLA Ops:
  0.6 7.7 %collective-permute-start.5 = (bf16[256,2048]{1,0:T(8,128)(2,1)}, bf16[256,2048]{1,0:T(8,128)(2,1)S(1)}, u32[]{:S(2)}, u32[]{:S(2)}) collective-permute-start(bf16[256,2048]{1,0:T(8,128)(2,1)} %bitcast.16), channel_id=1, source_target_pairs={{0,16},{16,0},{1,17},{17,1},{2,18},{18,2},{3,19},{19,3},{4,20},{20... | collective-permute-start | bytes 3145736 | tf_op jit(solution)/shard_map/ppermute | solution.py:25
  9.2 8.2 %collective-permute-start.11 = (bf16[128,768]{1,0:T(8,128)(2,1)S(1)}, bf16[128,768]{1,0:T(8,128)(2,1)S(1)}, u32[]{:S(2)}, u32[]{:S(2)}) collective-permute-start(bf16[128,768]{1,0:T(8,128)(2,1)S(1)} %get-tuple-element.195), channel_id=1, source_target_pairs={{32,0},{64,32},{96,64},{128,96},{160,128},{192,160},{224,192},{0,2... | collective-permute-start | bytes 589832 | tf_op jit(solution)/shard_map/ppermute | solution.py:33
  13.1 7.8 %collective-permute-start.7 = (bf16[128,768]{1,0:T(8,128)(2,1)S(1)}, bf16[128,768]{1,0:T(8,128)(2,1)S(1)}, u32[]{:S(2)}, u32[]{:S(2)}) collective-permute-start(bf16[128,768]{1,0:T(8,128)(2,1)S(1)} %get-tuple-element.191), channel_id=1, source_target_pairs={{0,32},{32,64},{64,96},{96,128},{128,160},{160,192},{192,224},{224... | collective-permute-start | bytes 589832 | tf_op jit(solution)/shard_map/ppermute | solution.py:29
  17.4 11.0 %collective-permute-start.12 = (bf16[256,768]{1,0:T(8,128)(2,1)S(1)}, bf16[256,768]{1,0:T(8,128)(2,1)S(1)}, u32[]{:S(2)}, u32[]{:S(2)}) collective-permute-start(bf16[256,768]{1,0:T(8,128)(2,1)S(1)} %pad_maximum_fusion.1), channel_id=1, source_target_pairs={{32,0},{64,32},{96,64},{128,96},{160,128},{192,160},{224,192},{0,2... | collective-permute-start | bytes 1179656 | tf_op jit(solution)/shard_map/ppermute | solution.py:33
  21.0 11.1 %collective-permute-start.8 = (bf16[256,768]{1,0:T(8,128)(2,1)S(1)}, bf16[256,768]{1,0:T(8,128)(2,1)S(1)}, u32[]{:S(2)}, u32[]{:S(2)}) collective-permute-start(bf16[256,768]{1,0:T(8,128)(2,1)S(1)} %pad_maximum_fusion), channel_id=1, source_target_pairs={{0,32},{32,64},{64,96},{96,128},{128,160},{160,192},{192,224},{224... | collective-permute-start | bytes 1179656 | tf_op jit(solution)/shard_map/ppermute | solution.py:29
  28.6 10.1 %collective-permute-start.13 = (bf16[256,768]{1,0:T(8,128)(2,1)S(1)}, bf16[256,768]{1,0:T(8,128)(2,1)S(1)}, u32[]{:S(2)}, u32[]{:S(2)}) collective-permute-start(bf16[256,768]{1,0:T(8,128)(2,1)S(1)} %add_convert_fusion.1), channel_id=1, source_target_pairs={{32,0},{64,32},{96,64},{128,96},{160,128},{192,160},{224,192},{0,2... | collective-permute-start | bytes 1179656 | tf_op jit(solution)/shard_map/ppermute | solution.py:33
  32.2 10.1 %collective-permute-start.9 = (bf16[256,768]{1,0:T(8,128)(2,1)S(1)}, bf16[256,768]{1,0:T(8,128)(2,1)S(1)}, u32[]{:S(2)}, u32[]{:S(2)}) collective-permute-start(bf16[256,768]{1,0:T(8,128)(2,1)S(1)} %add_convert_fusion.3), channel_id=1, source_target_pairs={{0,32},{32,64},{64,96},{96,128},{128,160},{160,192},{192,224},{224... | collective-permute-start | bytes 1179656 | tf_op jit(solution)/shard_map/ppermute | solution.py:29
  38.8 9.2 %collective-permute-start.14 = (bf16[256,768]{1,0:T(8,128)(2,1)S(1)}, bf16[256,768]{1,0:T(8,128)(2,1)S(1)}, u32[]{:S(2)}, u32[]{:S(2)}) collective-permute-start(bf16[256,768]{1,0:T(8,128)(2,1)S(1)} %add_convert_fusion), channel_id=1, source_target_pairs={{32,0},{64,32},{96,64},{128,96},{160,128},{192,160},{224,192},{0,2... | collective-permute-start | bytes 1179656 | tf_op jit(solution)/shard_map/ppermute | solution.py:33
  42.4 8.9 %collective-permute-start.10 = (bf16[256,768]{1,0:T(8,128)(2,1)S(1)}, bf16[256,768]{1,0:T(8,128)(2,1)S(1)}, u32[]{:S(2)}, u32[]{:S(2)}) collective-permute-start(bf16[256,768]{1,0:T(8,128)(2,1)S(1)} %add_convert_fusion.2), channel_id=1, source_target_pairs={{0,32},{32,64},{64,96},{96,128},{128,160},{160,192},{192,224},{224... | collective-permute-start | bytes 1179656 | tf_op jit(solution)/shard_map/ppermute | solution.py:29
  51.5 6.1 %collective-permute-start.17 = (bf16[128,768]{1,0:T(8,128)(2,1)S(1)}, bf16[128,768]{1,0:T(8,128)(2,1)S(1)}, u32[]{:S(2)}, u32[]{:S(2)}) collective-permute-start(bf16[128,768]{1,0:T(8,128)(2,1)S(1)} %slice.41.refs_0_), channel_id=1, source_target_pairs={{0,2},{1,3},{2,0},{3,1},{4,6},{5,7},{6,4},{7,5},{8,10},{9,11},{10,... | collective-permute-start | bytes 589832 | tf_op jit(solution)/shard_map/ppermute | solution.py:37
  54.5 5.9 %collective-permute-start.16 = (bf16[128,768]{1,0:T(8,128)(2,1)S(1)}, bf16[128,768]{1,0:T(8,128)(2,1)S(1)}, u32[]{:S(2)}, u32[]{:S(2)}) collective-permute-start(bf16[128,768]{1,0:T(8,128)(2,1)S(1)} %slice.41.refs_0_), channel_id=1, source_target_pairs={{0,3},{1,0},{2,1},{3,2},{4,7},{5,4},{6,5},{7,6},{8,11},{9,8},{10,9... | collective-permute-start | bytes 589832 | tf_op jit(solution)/shard_map/ppermute | solution.py:37
  55.3 7.8 %collective-permute-start.15 = (bf16[128,768]{1,0:T(8,128)(2,1)S(1)}, bf16[128,768]{1,0:T(8,128)(2,1)S(1)}, u32[]{:S(2)}, u32[]{:S(2)}) collective-permute-start(bf16[128,768]{1,0:T(8,128)(2,1)S(1)} %slice.41.refs_0_), channel_id=1, source_target_pairs={{0,1},{1,2},{2,3},{3,0},{4,5},{5,6},{6,7},{7,4},{8,9},{9,10},{10,1... | collective-permute-start | bytes 589832 | tf_op jit(solution)/shard_map/ppermute | solution.py:37
  64.1 6.1 %collective-permute-start.18 = (bf16[128,768]{1,0:T(8,128)(2,1)S(1)}, bf16[128,768]{1,0:T(8,128)(2,1)S(1)}, u32[]{:S(2)}, u32[]{:S(2)}) collective-permute-start(bf16[128,768]{1,0:T(8,128)(2,1)S(1)} %get-tuple-element.197), channel_id=1, source_target_pairs={{0,8},{4,12},{8,0},{12,4},{1,9},{5,13},{9,1},{13,5},{2,10},{6,14},... | collective-permute-start | bytes 589832 | tf_op jit(solution)/shard_map/ppermute | solution.py:37
  67.0 7.8 %collective-permute-start.19 = (bf16[128,768]{1,0:T(8,128)(2,1)S(1)}, bf16[128,768]{1,0:T(8,128)(2,1)S(1)}, u32[]{:S(2)}, u32[]{:S(2)}) collective-permute-start(bf16[128,768]{1,0:T(8,128)(2,1)S(1)} %get-tuple-element.198), channel_id=1, source_target_pairs={{0,4},{4,8},{8,12},{12,0},{1,5},{5,9},{9,13},{13,1},{2,6},{6,10},{... | collective-permute-start | bytes 589832 | tf_op jit(solution)/shard_map/ppermute | solution.py:37
  67.3 7.5 %collective-permute-start.20 = (bf16[128,768]{1,0:T(8,128)(2,1)S(1)}, bf16[128,768]{1,0:T(8,128)(2,1)S(1)}, u32[]{:S(2)}, u32[]{:S(2)}) collective-permute-start(bf16[128,768]{1,0:T(8,128)(2,1)S(1)} %get-tuple-element.199), channel_id=1, source_target_pairs={{0,12},{4,0},{8,4},{12,8},{1,13},{5,1},{9,5},{13,9},{2,14},{6,2},{... | collective-permute-start | bytes 589832 | tf_op jit(solution)/shard_map/ppermute | solution.py:37
  75.1 5.8 %collective-permute-start = (bf16[128,768]{1,0:T(8,128)(2,1)S(1)}, bf16[128,768]{1,0:T(8,128)(2,1)S(1)}, u32[]{:S(2)}, u32[]{:S(2)}) collective-permute-start(bf16[128,768]{1,0:T(8,128)(2,1)S(1)} %copy.19), channel_id=1, source_target_pairs={{0,32},{32,64},{64,96},{96,128},{128,160},{160,192},{192,224},{224... | collective-permute-start | bytes 589832 | tf_op jit(solution)/shard_map/while/body/eval_jaxpr/ppermute | solution.py:29
  81.0 5.9 %collective-permute-start = (bf16[128,768]{1,0:T(8,128)(2,1)S(1)}, bf16[128,768]{1,0:T(8,128)(2,1)S(1)}, u32[]{:S(2)}, u32[]{:S(2)}) collective-permute-start(bf16[128,768]{1,0:T(8,128)(2,1)S(1)} %copy.19), channel_id=1, source_target_pairs={{0,32},{32,64},{64,96},{96,128},{128,160},{160,192},{192,224},{224... | collective-permute-start | bytes 589832 | tf_op jit(solution)/shard_map/while/body/eval_jaxpr/ppermute | solution.py:29
  86.9 6.5 %collective-permute-start = (bf16[128,768]{1,0:T(8,128)(2,1)S(1)}, bf16[128,768]{1,0:T(8,128)(2,1)S(1)}, u32[]{:S(2)}, u32[]{:S(2)}) collective-permute-start(bf16[128,768]{1,0:T(8,128)(2,1)S(1)} %copy.19), channel_id=1, source_target_pairs={{0,32},{32,64},{64,96},{96,128},{128,160},{160,192},{192,224},{224... | collective-permute-start | bytes 589832 | tf_op jit(solution)/shard_map/while/body/eval_jaxpr/ppermute | solution.py:29
  93.4 7.9 %collective-permute-start = (bf16[128,768]{1,0:T(8,128)(2,1)S(1)}, bf16[128,768]{1,0:T(8,128)(2,1)S(1)}, u32[]{:S(2)}, u32[]{:S(2)}) collective-permute-start(bf16[128,768]{1,0:T(8,128)(2,1)S(1)} %copy.19), channel_id=1, source_target_pairs={{0,32},{32,64},{64,96},{96,128},{128,160},{160,192},{192,224},{224... | collective-permute-start | bytes 589832 | tf_op jit(solution)/shard_map/while/body/eval_jaxpr/ppermute | solution.py:29
  94.3 7.1 %collective-permute-start.1 = (bf16[128,768]{1,0:T(8,128)(2,1)S(1)}, bf16[128,768]{1,0:T(8,128)(2,1)S(1)}, u32[]{:S(2)}, u32[]{:S(2)}) collective-permute-start(bf16[128,768]{1,0:T(8,128)(2,1)S(1)} %copy.20), channel_id=1, source_target_pairs={{32,0},{64,32},{96,64},{128,96},{160,128},{192,160},{224,192},{0,2... | collective-permute-start | bytes 589832 | tf_op jit(solution)/shard_map/while/body/eval_jaxpr/ppermute | solution.py:33
  101.4 11.4 %collective-permute-start.21 = (bf16[1024,768]{1,0:T(8,128)(2,1)S(1)}, bf16[1024,768]{1,0:T(8,128)(2,1)S(1)}, u32[]{:S(2)}, u32[]{:S(2)}) collective-permute-start(bf16[1024,768]{1,0:T(8,128)(2,1)S(1)} %constant_dynamic-update-slice_fusion.8), channel_id=1, source_target_pairs={{0,16},{16,0},{1,17},{17,1},{2,18},{18,2},{3,19},{19,3},{4,20},{20... | collective-permute-start | bytes 4718600 | tf_op jit(solution)/shard_map/ppermute | solution.py:25
  128.5 7.6 %collective-permute-start.24 = (bf16[128,768]{1,0:T(8,128)(2,1)S(1)}, bf16[128,768]{1,0:T(8,128)(2,1)S(1)}, u32[]{:S(2)}, u32[]{:S(2)}) collective-permute-start(bf16[128,768]{1,0:T(8,128)(2,1)S(1)} %get-tuple-element.203.refs_0_), channel_id=1, source_target_pairs={{0,8},{4,12},{8,0},{12,4},{1,9},{5,13},{9,1},{13,5},{2,10},{6,14},... | collective-permute-start | bytes 589832 | tf_op jit(solution)/shard_map/ppermute | solution.py:37
  131.0 9.8 %collective-permute-start.23 = (bf16[128,768]{1,0:T(8,128)(2,1)S(1)}, bf16[128,768]{1,0:T(8,128)(2,1)S(1)}, u32[]{:S(2)}, u32[]{:S(2)}) collective-permute-start(bf16[128,768]{1,0:T(8,128)(2,1)S(1)} %get-tuple-element.203.refs_0_), channel_id=1, source_target_pairs={{0,12},{4,0},{8,4},{12,8},{1,13},{5,1},{9,5},{13,9},{2,14},{6,2},{... | collective-permute-start | bytes 589832 | tf_op jit(solution)/shard_map/ppermute | solution.py:37
  132.9 8.0 %collective-permute-start.22 = (bf16[128,768]{1,0:T(8,128)(2,1)S(1)}, bf16[128,768]{1,0:T(8,128)(2,1)S(1)}, u32[]{:S(2)}, u32[]{:S(2)}) collective-permute-start(bf16[128,768]{1,0:T(8,128)(2,1)S(1)} %get-tuple-element.203.refs_0_), channel_id=1, source_target_pairs={{0,4},{4,8},{8,12},{12,0},{1,5},{5,9},{9,13},{13,1},{2,6},{6,10},{... | collective-permute-start | bytes 589832 | tf_op jit(solution)/shard_map/ppermute | solution.py:37
  141.8 6.9 %collective-permute-start.25 = (bf16[128,768]{1,0:T(8,128)(2,1)S(1)}, bf16[128,768]{1,0:T(8,128)(2,1)S(1)}, u32[]{:S(2)}, u32[]{:S(2)}) collective-permute-start(bf16[128,768]{1,0:T(8,128)(2,1)S(1)} %get-tuple-element.205), channel_id=1, source_target_pairs={{0,2},{1,3},{2,0},{3,1},{4,6},{5,7},{6,4},{7,5},{8,10},{9,11},{10,... | collective-permute-start | bytes 589832 | tf_op jit(solution)/shard_map/ppermute | solution.py:37
  141.9 12.1 %collective-permute-start.26 = (bf16[128,768]{1,0:T(8,128)(2,1)S(1)}, bf16[128,768]{1,0:T(8,128)(2,1)S(1)}, u32[]{:S(2)}, u32[]{:S(2)}) collective-permute-start(bf16[128,768]{1,0:T(8,128)(2,1)S(1)} %get-tuple-element.206), channel_id=1, source_target_pairs={{0,1},{1,2},{2,3},{3,0},{4,5},{5,6},{6,7},{7,4},{8,9},{9,10},{10,1... | collective-permute-start | bytes 589832 | tf_op jit(solution)/shard_map/ppermute | solution.py:37
  142.0 12.0 %collective-permute-start.27 = (bf16[128,768]{1,0:T(8,128)(2,1)S(1)}, bf16[128,768]{1,0:T(8,128)(2,1)S(1)}, u32[]{:S(2)}, u32[]{:S(2)}) collective-permute-start(bf16[128,768]{1,0:T(8,128)(2,1)S(1)} %get-tuple-element.207), channel_id=1, source_target_pairs={{0,3},{1,0},{2,1},{3,2},{4,7},{5,4},{6,5},{7,6},{8,11},{9,8},{10,9... | collective-permute-start | bytes 589832 | tf_op jit(solution)/shard_map/ppermute | solution.py:37
  154.8 7.6 %collective-permute-start.2 = (bf16[128,768]{1,0:T(8,128)(2,1)S(1)}, bf16[128,768]{1,0:T(8,128)(2,1)S(1)}, u32[]{:S(2)}, u32[]{:S(2)}) collective-permute-start(bf16[128,768]{1,0:T(8,128)(2,1)S(1)} %copy.32), channel_id=1, source_target_pairs={{0,32},{32,64},{64,96},{96,128},{128,160},{160,192},{192,224},{224... | collective-permute-start | bytes 589832 | tf_op jit(solution)/shard_map/while/body/eval_jaxpr/ppermute | solution.py:29
  155.8 6.6 %collective-permute-start.3 = (bf16[128,768]{1,0:T(8,128)(2,1)S(1)}, bf16[128,768]{1,0:T(8,128)(2,1)S(1)}, u32[]{:S(2)}, u32[]{:S(2)}) collective-permute-start(bf16[128,768]{1,0:T(8,128)(2,1)S(1)} %copy.33), channel_id=1, source_target_pairs={{32,0},{64,32},{96,64},{128,96},{160,128},{192,160},{224,192},{0,2... | collective-permute-start | bytes 589832 | tf_op jit(solution)/shard_map/while/body/eval_jaxpr/ppermute | solution.py:33
  162.5 6.4 %collective-permute-start.2 = (bf16[128,768]{1,0:T(8,128)(2,1)S(1)}, bf16[128,768]{1,0:T(8,128)(2,1)S(1)}, u32[]{:S(2)}, u32[]{:S(2)}) collective-permute-start(bf16[128,768]{1,0:T(8,128)(2,1)S(1)} %copy.32), channel_id=1, source_target_pairs={{0,32},{32,64},{64,96},{96,128},{128,160},{160,192},{192,224},{224... | collective-permute-start | bytes 589832 | tf_op jit(solution)/shard_map/while/body/eval_jaxpr/ppermute | solution.py:29
  174.8 7.5 %collective-permute-start.29 = (bf16[64,768]{1,0:T(8,128)(2,1)S(1)}, bf16[64,768]{1,0:T(8,128)(2,1)S(1)}, u32[]{:S(2)}, u32[]{:S(2)}) collective-permute-start(bf16[64,768]{1,0:T(8,128)(2,1)S(1)} %slice.32), channel_id=1, source_target_pairs={{32,0},{64,32},{96,64},{128,96},{160,128},{192,160},{224,192},{0,2... | collective-permute-start | bytes 294920 | tf_op jit(solution)/shard_map/ppermute | solution.py:33
  182.3 8.2 %collective-permute-start.30 = (bf16[1024,768]{1,0:T(8,128)(2,1)S(1)}, bf16[1024,768]{1,0:T(8,128)(2,1)S(1)}, u32[]{:S(2)}, u32[]{:S(2)}) collective-permute-start(bf16[1024,768]{1,0:T(8,128)(2,1)S(1)} %constant_dynamic-update-slice_fusion.4.blocks_ref), channel_id=1, source_target_pairs={{0,16},{16,0},{1,17},{17,1},{2,18},{18,2},{3,19},{19,3},{4,20},{20... | collective-permute-start | bytes 4718600 | tf_op jit(solution)/shard_map/ppermute | solution.py:25
  (19 other events, 160.0 us)

commit v6 on v4

--- a/solution.py
+++ b/solution.py
@@ -390,7 +390,7 @@
     return mine.astype(F32) + up(below).astype(F32) + down(above).astype(F32)
 
 
-def ring(block):
+def ring(block, unroll=1):
     rows, width = block.shape
 
     def one(step, carry):
@@ -400,7 +400,7 @@
         return up(below), down(above), got
 
     got = jnp.zeros((NZ * rows, width), block.dtype)
-    far, _, got = lax.fori_loop(0, 4, one, (block, block, got))
+    far, _, got = lax.fori_loop(0, 4, one, (block, block, got), unroll=unroll)
     return lax.dynamic_update_slice(got, far, (0, 0))
 
 
@@ -437,7 +437,7 @@
     pieces = [kept] + [shift(sent[offset - 1], "y", offset) for offset in FAR_FIRST[1:]]
     replica = pick(here, copy_list, pieces)
 
-    own = ring(replica)
+    own = ring(replica, 2)
     full = place(1, here, swap(own), place(0, here, own))
     return (fresh_mom[None], update[None], full[None])
 

time: 191 us -> 190 us (level)
    ppermute x12, starting transfers between devices: 6.22 us -> 3.47 us  [up(): return lax.ppermute(value, 'z', [(i, (i + 1) % NZ) for i in range(NZ)])]
    ppermute x12, starting transfers between devices: 32.1 us -> 34.3 us  [down(): return lax.ppermute(value, 'z', [((i + 1) % NZ, i) for i in range(NZ)])]
where the time goes in v6:
time: 190 us
  waiting for transfers between devices  85.1 us (45%)
  starting transfers between devices  71.7 us (38%)
  Pallas kernels  25.7 us (14%)
  local copies, waits for them, and re-layouts  3.65 us (2%)
    ppermute x12, starting transfers between devices, down(): return lax.ppermute(value, 'z', [((i + 1) % NZ, i) for i in range(NZ)])  34.3 us
    ppermute x12, waiting for transfers between devices, up(): return lax.ppermute(value, 'z', [(i, (i + 1) % NZ) for i in range(NZ)])  31.3 us
    ppermute x12, waiting for transfers between devices, shift(): return lax.ppermute(value, axis, [(i, (i + offset) % 4) for i in range(4)])  29.6 us
    ppermute x12, waiting for transfers between devices, down(): return lax.ppermute(value, 'z', [((i + 1) % NZ, i) for i in range(NZ)])  21.3 us
    ppermute x12, starting transfers between devices, shift(): return lax.ppermute(value, axis, [(i, (i + offset) % 4) for i in range(4)])  17.2 us
    ppermute x5, starting transfers between devices, swap(): return lax.ppermute(value, 'core', [(0, 1), (1, 0)])  16.8 us
    pallas_call x1, Pallas kernels, newton_schulz(): pl.pallas_call(functools.partial(newton_kernel, 0.2 * math.sqrt(longest))...  15.7 us
  transfers between devices with their start and end apart: 41, of which 24 were waited for; matrix products, arithmetic and copies ran while one was open for 1% of the time, Pallas kernels for 3%

profile of v6, /device:TPU:1, one launch (start us, length us, event | category | flops | bytes accessed | tf_op | source)
XLA Modules:
  0.0 189.8 jit_solution(10446109108619938709)
XLA Ops:
  0.6 3.3 %collective-permute-start.7 = (bf16[256,2048]{1,0:T(8,128)(2,1)}, bf16[256,2048]{1,0:T(8,128)(2,1)S(1)}, u32[]{:S(2)}, u32[]{:S(2)}) collective-permute-start(bf16[256,2048]{1,0:T(8,128)(2,1)} %bitcast.16), channel_id=1, source_target_pairs={{0,16},{16,0},{1,17},{17,1},{2,18},{18,2},{3,19},{19,3},{4,20},{20... | collective-permute-start | bytes 3145736 | tf_op jit(solution)/shard_map/ppermute | solution.py:25
  9.2 3.9 %collective-permute-start.13 = (bf16[128,768]{1,0:T(8,128)(2,1)S(1)}, bf16[128,768]{1,0:T(8,128)(2,1)S(1)}, u32[]{:S(2)}, u32[]{:S(2)}) collective-permute-start(bf16[128,768]{1,0:T(8,128)(2,1)S(1)} %get-tuple-element.194), channel_id=1, source_target_pairs={{32,0},{64,32},{96,64},{128,96},{160,128},{192,160},{224,192},{0,2... | collective-permute-start | bytes 589832 | tf_op jit(solution)/shard_map/ppermute | solution.py:33
  17.4 3.5 %collective-permute-start.14 = (bf16[256,768]{1,0:T(8,128)(2,1)S(1)}, bf16[256,768]{1,0:T(8,128)(2,1)S(1)}, u32[]{:S(2)}, u32[]{:S(2)}) collective-permute-start(bf16[256,768]{1,0:T(8,128)(2,1)S(1)} %pad_maximum_fusion.1), channel_id=1, source_target_pairs={{32,0},{64,32},{96,64},{128,96},{160,128},{192,160},{224,192},{0,2... | collective-permute-start | bytes 1179656 | tf_op jit(solution)/shard_map/ppermute | solution.py:33
  21.1 7.4 %collective-permute-done.14 = bf16[256,768]{1,0:T(8,128)(2,1)S(1)} collective-permute-done((bf16[256,768]{1,0:T(8,128)(2,1)S(1)}, bf16[256,768]{1,0:T(8,128)(2,1)S(1)}, u32[]{:S(2)}, u32[]{:S(2)}) %collective-permute-start.14) | collective-permute-done | bytes 393248 | tf_op jit(solution)/shard_map/ppermute | solution.py:33
  28.6 3.5 %collective-permute-start.15 = (bf16[256,768]{1,0:T(8,128)(2,1)S(1)}, bf16[256,768]{1,0:T(8,128)(2,1)S(1)}, u32[]{:S(2)}, u32[]{:S(2)}) collective-permute-start(bf16[256,768]{1,0:T(8,128)(2,1)S(1)} %add_convert_fusion.1), channel_id=1, source_target_pairs={{32,0},{64,32},{96,64},{128,96},{160,128},{192,160},{224,192},{0,2... | collective-permute-start | bytes 1179656 | tf_op jit(solution)/shard_map/ppermute | solution.py:33
  32.3 6.4 %collective-permute-done.15 = bf16[256,768]{1,0:T(8,128)(2,1)S(1)} collective-permute-done((bf16[256,768]{1,0:T(8,128)(2,1)S(1)}, bf16[256,768]{1,0:T(8,128)(2,1)S(1)}, u32[]{:S(2)}, u32[]{:S(2)}) %collective-permute-start.15) | collective-permute-done | bytes 393248 | tf_op jit(solution)/shard_map/ppermute | solution.py:33
  38.8 3.5 %collective-permute-start.16 = (bf16[256,768]{1,0:T(8,128)(2,1)S(1)}, bf16[256,768]{1,0:T(8,128)(2,1)S(1)}, u32[]{:S(2)}, u32[]{:S(2)}) collective-permute-start(bf16[256,768]{1,0:T(8,128)(2,1)S(1)} %add_convert_fusion), channel_id=1, source_target_pairs={{32,0},{64,32},{96,64},{128,96},{160,128},{192,160},{224,192},{0,2... | collective-permute-start | bytes 1179656 | tf_op jit(solution)/shard_map/ppermute | solution.py:33
  42.5 5.5 %collective-permute-done.16 = bf16[256,768]{1,0:T(8,128)(2,1)S(1)} collective-permute-done((bf16[256,768]{1,0:T(8,128)(2,1)S(1)}, bf16[256,768]{1,0:T(8,128)(2,1)S(1)}, u32[]{:S(2)}, u32[]{:S(2)}) %collective-permute-start.16) | collective-permute-done | bytes 393248 | tf_op jit(solution)/shard_map/ppermute | solution.py:33
  48.0 3.3 %collective-permute-done.12 = bf16[256,768]{1,0:T(8,128)(2,1)S(1)} collective-permute-done((bf16[256,768]{1,0:T(8,128)(2,1)S(1)}, bf16[256,768]{1,0:T(8,128)(2,1)S(1)}, u32[]{:S(2)}, u32[]{:S(2)}) %collective-permute-start.12) | collective-permute-done | bytes 393248 | tf_op jit(solution)/shard_map/ppermute | solution.py:29
  51.5 3.0 %collective-permute-start.19 = (bf16[128,768]{1,0:T(8,128)(2,1)S(1)}, bf16[128,768]{1,0:T(8,128)(2,1)S(1)}, u32[]{:S(2)}, u32[]{:S(2)}) collective-permute-start(bf16[128,768]{1,0:T(8,128)(2,1)S(1)} %slice.33.refs_0_), channel_id=1, source_target_pairs={{0,2},{1,3},{2,0},{3,1},{4,6},{5,7},{6,4},{7,5},{8,10},{9,11},{10,... | collective-permute-start | bytes 589832 | tf_op jit(solution)/shard_map/ppermute | solution.py:37
  57.6 2.7 %collective-permute-done.18.refs_2_ = bf16[128,768]{1,0:T(8,128)(2,1)S(1)} collective-permute-done((bf16[128,768]{1,0:T(8,128)(2,1)S(1)}, bf16[128,768]{1,0:T(8,128)(2,1)S(1)}, u32[]{:S(2)}, u32[]{:S(2)}) %collective-permute-start.18) | collective-permute-done | bytes 196640 | tf_op jit(solution)/shard_map/ppermute | solution.py:37
  60.4 2.8 %collective-permute-done.17.refs_1_ = bf16[128,768]{1,0:T(8,128)(2,1)S(1)} collective-permute-done((bf16[128,768]{1,0:T(8,128)(2,1)S(1)}, bf16[128,768]{1,0:T(8,128)(2,1)S(1)}, u32[]{:S(2)}, u32[]{:S(2)}) %collective-permute-start.17) | collective-permute-done | bytes 196640 | tf_op jit(solution)/shard_map/ppermute | solution.py:37
  64.1 2.8 %collective-permute-start.20 = (bf16[128,768]{1,0:T(8,128)(2,1)S(1)}, bf16[128,768]{1,0:T(8,128)(2,1)S(1)}, u32[]{:S(2)}, u32[]{:S(2)}) collective-permute-start(bf16[128,768]{1,0:T(8,128)(2,1)S(1)} %get-tuple-element.196), channel_id=1, source_target_pairs={{0,8},{4,12},{8,0},{12,4},{1,9},{5,13},{9,1},{13,5},{2,10},{6,14},... | collective-permute-start | bytes 589832 | tf_op jit(solution)/shard_map/ppermute | solution.py:37
  70.2 4.6 %collective-permute-done.21 = bf16[128,768]{1,0:T(8,128)(2,1)S(1)} collective-permute-done((bf16[128,768]{1,0:T(8,128)(2,1)S(1)}, bf16[128,768]{1,0:T(8,128)(2,1)S(1)}, u32[]{:S(2)}, u32[]{:S(2)}) %collective-permute-start.21) | collective-permute-done | bytes 196640 | tf_op jit(solution)/shard_map/ppermute | solution.py:37
  75.1 26.3 %while.34 = (s32[]{:T(128)}, bf16[128,768]{1,0:T(8,128)(2,1)S(1)}, bf16[128,768]{1,0:T(8,128)(2,1)S(1)}, bf16[1024,768]{1,0:T(8,128)(2,1)S(1)}, s32[]{:T(128)}, ...) while((s32[]{:T(128)}, bf16[128,768]{1,0:T(8,128)(2,1)S(1)}, bf16[128,768]{1,0:T(8,128)(2,1)S(1)}, ...), condition=%wide.region_1.0_spmd, body=%wide.region_0.0_spmd.sunk | while | flops 12 | bytes 3146025 | solution.py:403
  78.0 2.9 %collective-permute-done = bf16[128,768]{1,0:T(8,128)(2,1)S(1)} collective-permute-done((bf16[128,768]{1,0:T(8,128)(2,1)S(1)}, bf16[128,768]{1,0:T(8,128)(2,1)S(1)}, u32[]{:S(2)}, u32[]{:S(2)}) %collective-permute-start) | collective-permute-done | bytes 196640 | tf_op jit(solution)/shard_map/while/body/eval_jaxpr/ppermute | solution.py:29
  81.1 2.8 %collective-permute-start.1 = (bf16[128,768]{1,0:T(8,128)(2,1)S(1)}, bf16[128,768]{1,0:T(8,128)(2,1)S(1)}, u32[]{:S(2)}, u32[]{:S(2)}) collective-permute-start(bf16[128,768]{1,0:T(8,128)(2,1)S(1)} %copy.22), channel_id=1, source_target_pairs={{32,0},{64,32},{96,64},{128,96},{160,128},{192,160},{224,192},{0,2... | collective-permute-start | bytes 589832 | tf_op jit(solution)/shard_map/while/body/eval_jaxpr/ppermute | solution.py:33
  84.0 2.9 %collective-permute-done = bf16[128,768]{1,0:T(8,128)(2,1)S(1)} collective-permute-done((bf16[128,768]{1,0:T(8,128)(2,1)S(1)}, bf16[128,768]{1,0:T(8,128)(2,1)S(1)}, u32[]{:S(2)}, u32[]{:S(2)}) %collective-permute-start) | collective-permute-done | bytes 196640 | tf_op jit(solution)/shard_map/while/body/eval_jaxpr/ppermute | solution.py:29
  89.9 3.5 %collective-permute-done = bf16[128,768]{1,0:T(8,128)(2,1)S(1)} collective-permute-done((bf16[128,768]{1,0:T(8,128)(2,1)S(1)}, bf16[128,768]{1,0:T(8,128)(2,1)S(1)}, u32[]{:S(2)}, u32[]{:S(2)}) %collective-permute-start) | collective-permute-done | bytes 196640 | tf_op jit(solution)/shard_map/while/body/eval_jaxpr/ppermute | solution.py:29
  96.7 4.6 %collective-permute-done = bf16[128,768]{1,0:T(8,128)(2,1)S(1)} collective-permute-done((bf16[128,768]{1,0:T(8,128)(2,1)S(1)}, bf16[128,768]{1,0:T(8,128)(2,1)S(1)}, u32[]{:S(2)}, u32[]{:S(2)}) %collective-permute-start) | collective-permute-done | bytes 196640 | tf_op jit(solution)/shard_map/while/body/eval_jaxpr/ppermute | solution.py:29
  101.4 8.4 %collective-permute-start.23 = (bf16[1024,768]{1,0:T(8,128)(2,1)S(1)}, bf16[1024,768]{1,0:T(8,128)(2,1)S(1)}, u32[]{:S(2)}, u32[]{:S(2)}) collective-permute-start(bf16[1024,768]{1,0:T(8,128)(2,1)S(1)} %constant_dynamic-update-slice_fusion.7), channel_id=1, source_target_pairs={{0,16},{16,0},{1,17},{17,1},{2,18},{18,2},{3,19},{19,3},{4,20},{20... | collective-permute-start | bytes 4718600 | tf_op jit(solution)/shard_map/ppermute | solution.py:25
  112.8 15.7 %newton_schulz.1 = (f32[128,768]{1,0:T(8,128)}, bf16[128,768]{1,0:T(8,128)(2,1)S(1)}) custom-call(f32[768,768]{1,0:T(8,128)S(1)} %fusion.3.gram_ref, bf16[1024,768]{1,0:T(8,128)(2,1)S(1)} %collective-permute-done.23.other_ref, f32[128,768]{1,0:T(8,128)S(1)} %get-tuple-element.226.mom_ref, bf16[128,768]{1,0:T(8,128)(2,1)S(1)} %bitcast.26), custom_call_target="tpu_custom_call" | custom-call | flops 12683575296 | bytes 4718592 | tf_op jit(solution)/shard_map/newton_schulz/pallas_call | solution.py:359
  132.9 3.3 %collective-permute-done.26.refs_3_ = bf16[128,768]{1,0:T(8,128)(2,1)S(1)} collective-permute-done((bf16[128,768]{1,0:T(8,128)(2,1)S(1)}, bf16[128,768]{1,0:T(8,128)(2,1)S(1)}, u32[]{:S(2)}, u32[]{:S(2)}) %collective-permute-start.26) | collective-permute-done | bytes 196640 | tf_op jit(solution)/shard_map/ppermute | solution.py:37
  136.1 4.7 %collective-permute-done.25.refs_2_ = bf16[128,768]{1,0:T(8,128)(2,1)S(1)} collective-permute-done((bf16[128,768]{1,0:T(8,128)(2,1)S(1)}, bf16[128,768]{1,0:T(8,128)(2,1)S(1)}, u32[]{:S(2)}, u32[]{:S(2)}) %collective-permute-start.25) | collective-permute-done | bytes 196640 | tf_op jit(solution)/shard_map/ppermute | solution.py:37
  144.7 4.0 %collective-permute-done.27.refs_1_ = bf16[128,768]{1,0:T(8,128)(2,1)S(1)} collective-permute-done((bf16[128,768]{1,0:T(8,128)(2,1)S(1)}, bf16[128,768]{1,0:T(8,128)(2,1)S(1)}, u32[]{:S(2)}, u32[]{:S(2)}) %collective-permute-start.27) | collective-permute-done | bytes 196640 | tf_op jit(solution)/shard_map/ppermute | solution.py:37
  148.7 5.3 %collective-permute-done.28.refs_2_ = bf16[128,768]{1,0:T(8,128)(2,1)S(1)} collective-permute-done((bf16[128,768]{1,0:T(8,128)(2,1)S(1)}, bf16[128,768]{1,0:T(8,128)(2,1)S(1)}, u32[]{:S(2)}, u32[]{:S(2)}) %collective-permute-start.28) | collective-permute-done | bytes 196640 | tf_op jit(solution)/shard_map/ppermute | solution.py:37
  154.8 25.5 %while.35 = (s32[]{:T(128)}, bf16[128,768]{1,0:T(8,128)(2,1)S(1)}, bf16[128,768]{1,0:T(8,128)(2,1)S(1)}, bf16[1024,768]{1,0:T(8,128)(2,1)S(1)}, s32[]{:T(128)}, ...) while((s32[]{:T(128)}, bf16[128,768]{1,0:T(8,128)(2,1)S(1)}, ...), condition=%wide.region_3.0_spmd, body=%wide.region_2.0_spmd.sunk | while | flops 24 | bytes 4719133 | solution.py:403
  158.0 4.5 %collective-permute-done.2 = bf16[128,768]{1,0:T(8,128)(2,1)S(1)} collective-permute-done((bf16[128,768]{1,0:T(8,128)(2,1)S(1)}, bf16[128,768]{1,0:T(8,128)(2,1)S(1)}, u32[]{:S(2)}, u32[]{:S(2)}) %collective-permute-start.2) | collective-permute-done | bytes 196640 | tf_op jit(solution)/shard_map/while/body/eval_jaxpr/ppermute | solution.py:29
  165.1 3.6 %collective-permute-done.3 = bf16[128,768]{1,0:T(8,128)(2,1)S(1)} collective-permute-done((bf16[128,768]{1,0:T(8,128)(2,1)S(1)}, bf16[128,768]{1,0:T(8,128)(2,1)S(1)}, u32[]{:S(2)}, u32[]{:S(2)}) %collective-permute-start.3) | collective-permute-done | bytes 196640 | tf_op jit(solution)/shard_map/while/body/eval_jaxpr/ppermute | solution.py:29
  171.5 3.0 %collective-permute-done.2 = bf16[128,768]{1,0:T(8,128)(2,1)S(1)} collective-permute-done((bf16[128,768]{1,0:T(8,128)(2,1)S(1)}, bf16[128,768]{1,0:T(8,128)(2,1)S(1)}, u32[]{:S(2)}, u32[]{:S(2)}) %collective-permute-start.2) | collective-permute-done | bytes 196640 | tf_op jit(solution)/shard_map/while/body/eval_jaxpr/ppermute | solution.py:29
  177.2 3.0 %collective-permute-done.3 = bf16[128,768]{1,0:T(8,128)(2,1)S(1)} collective-permute-done((bf16[128,768]{1,0:T(8,128)(2,1)S(1)}, bf16[128,768]{1,0:T(8,128)(2,1)S(1)}, u32[]{:S(2)}, u32[]{:S(2)}) %collective-permute-start.3) | collective-permute-done | bytes 196640 | tf_op jit(solution)/shard_map/while/body/eval_jaxpr/ppermute | solution.py:29
  180.2 4.6 %collective-permute-start.30 = (bf16[1024,768]{1,0:T(8,128)(2,1)S(1)}, bf16[1024,768]{1,0:T(8,128)(2,1)S(1)}, u32[]{:S(2)}, u32[]{:S(2)}) collective-permute-start(bf16[1024,768]{1,0:T(8,128)(2,1)S(1)} %constant_dynamic-update-slice_fusion.6.blocks_ref), channel_id=1, source_target_pairs={{0,16},{16,0},{1,17},{17,1},{2,18},{18,2},{3,19},{19,3},{4,20},{20... | collective-permute-start | bytes 4718600 | tf_op jit(solution)/shard_map/ppermute | solution.py:25
  (126 shorter events, 55.4 us)
Async XLA Ops:
  0.6 7.7 %collective-permute-start.7 = (bf16[256,2048]{1,0:T(8,128)(2,1)}, bf16[256,2048]{1,0:T(8,128)(2,1)S(1)}, u32[]{:S(2)}, u32[]{:S(2)}) collective-permute-start(bf16[256,2048]{1,0:T(8,128)(2,1)} %bitcast.16), channel_id=1, source_target_pairs={{0,16},{16,0},{1,17},{17,1},{2,18},{18,2},{3,19},{19,3},{4,20},{20... | collective-permute-start | bytes 3145736 | tf_op jit(solution)/shard_map/ppermute | solution.py:25
  9.2 8.2 %collective-permute-start.13 = (bf16[128,768]{1,0:T(8,128)(2,1)S(1)}, bf16[128,768]{1,0:T(8,128)(2,1)S(1)}, u32[]{:S(2)}, u32[]{:S(2)}) collective-permute-start(bf16[128,768]{1,0:T(8,128)(2,1)S(1)} %get-tuple-element.194), channel_id=1, source_target_pairs={{32,0},{64,32},{96,64},{128,96},{160,128},{192,160},{224,192},{0,2... | collective-permute-start | bytes 589832 | tf_op jit(solution)/shard_map/ppermute | solution.py:33
  13.1 7.8 %collective-permute-start.9 = (bf16[128,768]{1,0:T(8,128)(2,1)S(1)}, bf16[128,768]{1,0:T(8,128)(2,1)S(1)}, u32[]{:S(2)}, u32[]{:S(2)}) collective-permute-start(bf16[128,768]{1,0:T(8,128)(2,1)S(1)} %get-tuple-element.190), channel_id=1, source_target_pairs={{0,32},{32,64},{64,96},{96,128},{128,160},{160,192},{192,224},{224... | collective-permute-start | bytes 589832 | tf_op jit(solution)/shard_map/ppermute | solution.py:29
  17.4 11.0 %collective-permute-start.14 = (bf16[256,768]{1,0:T(8,128)(2,1)S(1)}, bf16[256,768]{1,0:T(8,128)(2,1)S(1)}, u32[]{:S(2)}, u32[]{:S(2)}) collective-permute-start(bf16[256,768]{1,0:T(8,128)(2,1)S(1)} %pad_maximum_fusion.1), channel_id=1, source_target_pairs={{32,0},{64,32},{96,64},{128,96},{160,128},{192,160},{224,192},{0,2... | collective-permute-start | bytes 1179656 | tf_op jit(solution)/shard_map/ppermute | solution.py:33
  21.0 11.1 %collective-permute-start.10 = (bf16[256,768]{1,0:T(8,128)(2,1)S(1)}, bf16[256,768]{1,0:T(8,128)(2,1)S(1)}, u32[]{:S(2)}, u32[]{:S(2)}) collective-permute-start(bf16[256,768]{1,0:T(8,128)(2,1)S(1)} %pad_maximum_fusion), channel_id=1, source_target_pairs={{0,32},{32,64},{64,96},{96,128},{128,160},{160,192},{192,224},{224... | collective-permute-start | bytes 1179656 | tf_op jit(solution)/shard_map/ppermute | solution.py:29
  28.6 10.1 %collective-permute-start.15 = (bf16[256,768]{1,0:T(8,128)(2,1)S(1)}, bf16[256,768]{1,0:T(8,128)(2,1)S(1)}, u32[]{:S(2)}, u32[]{:S(2)}) collective-permute-start(bf16[256,768]{1,0:T(8,128)(2,1)S(1)} %add_convert_fusion.1), channel_id=1, source_target_pairs={{32,0},{64,32},{96,64},{128,96},{160,128},{192,160},{224,192},{0,2... | collective-permute-start | bytes 1179656 | tf_op jit(solution)/shard_map/ppermute | solution.py:33
  32.2 10.1 %collective-permute-start.11 = (bf16[256,768]{1,0:T(8,128)(2,1)S(1)}, bf16[256,768]{1,0:T(8,128)(2,1)S(1)}, u32[]{:S(2)}, u32[]{:S(2)}) collective-permute-start(bf16[256,768]{1,0:T(8,128)(2,1)S(1)} %add_convert_fusion.3), channel_id=1, source_target_pairs={{0,32},{32,64},{64,96},{96,128},{128,160},{160,192},{192,224},{224... | collective-permute-start | bytes 1179656 | tf_op jit(solution)/shard_map/ppermute | solution.py:29
  38.8 9.2 %collective-permute-start.16 = (bf16[256,768]{1,0:T(8,128)(2,1)S(1)}, bf16[256,768]{1,0:T(8,128)(2,1)S(1)}, u32[]{:S(2)}, u32[]{:S(2)}) collective-permute-start(bf16[256,768]{1,0:T(8,128)(2,1)S(1)} %add_convert_fusion), channel_id=1, source_target_pairs={{32,0},{64,32},{96,64},{128,96},{160,128},{192,160},{224,192},{0,2... | collective-permute-start | bytes 1179656 | tf_op jit(solution)/shard_map/ppermute | solution.py:33
  42.4 8.9 %collective-permute-start.12 = (bf16[256,768]{1,0:T(8,128)(2,1)S(1)}, bf16[256,768]{1,0:T(8,128)(2,1)S(1)}, u32[]{:S(2)}, u32[]{:S(2)}) collective-permute-start(bf16[256,768]{1,0:T(8,128)(2,1)S(1)} %add_convert_fusion.2), channel_id=1, source_target_pairs={{0,32},{32,64},{64,96},{96,128},{128,160},{160,192},{192,224},{224... | collective-permute-start | bytes 1179656 | tf_op jit(solution)/shard_map/ppermute | solution.py:29
  51.5 6.1 %collective-permute-start.19 = (bf16[128,768]{1,0:T(8,128)(2,1)S(1)}, bf16[128,768]{1,0:T(8,128)(2,1)S(1)}, u32[]{:S(2)}, u32[]{:S(2)}) collective-permute-start(bf16[128,768]{1,0:T(8,128)(2,1)S(1)} %slice.33.refs_0_), channel_id=1, source_target_pairs={{0,2},{1,3},{2,0},{3,1},{4,6},{5,7},{6,4},{7,5},{8,10},{9,11},{10,... | collective-permute-start | bytes 589832 | tf_op jit(solution)/shard_map/ppermute | solution.py:37
  54.5 5.9 %collective-permute-start.18 = (bf16[128,768]{1,0:T(8,128)(2,1)S(1)}, bf16[128,768]{1,0:T(8,128)(2,1)S(1)}, u32[]{:S(2)}, u32[]{:S(2)}) collective-permute-start(bf16[128,768]{1,0:T(8,128)(2,1)S(1)} %slice.33.refs_0_), channel_id=1, source_target_pairs={{0,3},{1,0},{2,1},{3,2},{4,7},{5,4},{6,5},{7,6},{8,11},{9,8},{10,9... | collective-permute-start | bytes 589832 | tf_op jit(solution)/shard_map/ppermute | solution.py:37
  55.3 7.8 %collective-permute-start.17 = (bf16[128,768]{1,0:T(8,128)(2,1)S(1)}, bf16[128,768]{1,0:T(8,128)(2,1)S(1)}, u32[]{:S(2)}, u32[]{:S(2)}) collective-permute-start(bf16[128,768]{1,0:T(8,128)(2,1)S(1)} %slice.33.refs_0_), channel_id=1, source_target_pairs={{0,1},{1,2},{2,3},{3,0},{4,5},{5,6},{6,7},{7,4},{8,9},{9,10},{10,1... | collective-permute-start | bytes 589832 | tf_op jit(solution)/shard_map/ppermute | solution.py:37
  64.1 6.1 %collective-permute-start.20 = (bf16[128,768]{1,0:T(8,128)(2,1)S(1)}, bf16[128,768]{1,0:T(8,128)(2,1)S(1)}, u32[]{:S(2)}, u32[]{:S(2)}) collective-permute-start(bf16[128,768]{1,0:T(8,128)(2,1)S(1)} %get-tuple-element.196), channel_id=1, source_target_pairs={{0,8},{4,12},{8,0},{12,4},{1,9},{5,13},{9,1},{13,5},{2,10},{6,14},... | collective-permute-start | bytes 589832 | tf_op jit(solution)/shard_map/ppermute | solution.py:37
  67.0 7.8 %collective-permute-start.21 = (bf16[128,768]{1,0:T(8,128)(2,1)S(1)}, bf16[128,768]{1,0:T(8,128)(2,1)S(1)}, u32[]{:S(2)}, u32[]{:S(2)}) collective-permute-start(bf16[128,768]{1,0:T(8,128)(2,1)S(1)} %get-tuple-element.197), channel_id=1, source_target_pairs={{0,4},{4,8},{8,12},{12,0},{1,5},{5,9},{9,13},{13,1},{2,6},{6,10},{... | collective-permute-start | bytes 589832 | tf_op jit(solution)/shard_map/ppermute | solution.py:37
  67.3 7.5 %collective-permute-start.22 = (bf16[128,768]{1,0:T(8,128)(2,1)S(1)}, bf16[128,768]{1,0:T(8,128)(2,1)S(1)}, u32[]{:S(2)}, u32[]{:S(2)}) collective-permute-start(bf16[128,768]{1,0:T(8,128)(2,1)S(1)} %get-tuple-element.198), channel_id=1, source_target_pairs={{0,12},{4,0},{8,4},{12,8},{1,13},{5,1},{9,5},{13,9},{2,14},{6,2},{... | collective-permute-start | bytes 589832 | tf_op jit(solution)/shard_map/ppermute | solution.py:37
  75.1 5.8 %collective-permute-start = (bf16[128,768]{1,0:T(8,128)(2,1)S(1)}, bf16[128,768]{1,0:T(8,128)(2,1)S(1)}, u32[]{:S(2)}, u32[]{:S(2)}) collective-permute-start(bf16[128,768]{1,0:T(8,128)(2,1)S(1)} %copy.21), channel_id=1, source_target_pairs={{0,32},{32,64},{64,96},{96,128},{128,160},{160,192},{192,224},{224... | collective-permute-start | bytes 589832 | tf_op jit(solution)/shard_map/while/body/eval_jaxpr/ppermute | solution.py:29
  81.0 5.9 %collective-permute-start = (bf16[128,768]{1,0:T(8,128)(2,1)S(1)}, bf16[128,768]{1,0:T(8,128)(2,1)S(1)}, u32[]{:S(2)}, u32[]{:S(2)}) collective-permute-start(bf16[128,768]{1,0:T(8,128)(2,1)S(1)} %copy.21), channel_id=1, source_target_pairs={{0,32},{32,64},{64,96},{96,128},{128,160},{160,192},{192,224},{224... | collective-permute-start | bytes 589832 | tf_op jit(solution)/shard_map/while/body/eval_jaxpr/ppermute | solution.py:29
  86.9 6.5 %collective-permute-start = (bf16[128,768]{1,0:T(8,128)(2,1)S(1)}, bf16[128,768]{1,0:T(8,128)(2,1)S(1)}, u32[]{:S(2)}, u32[]{:S(2)}) collective-permute-start(bf16[128,768]{1,0:T(8,128)(2,1)S(1)} %copy.21), channel_id=1, source_target_pairs={{0,32},{32,64},{64,96},{96,128},{128,160},{160,192},{192,224},{224... | collective-permute-start | bytes 589832 | tf_op jit(solution)/shard_map/while/body/eval_jaxpr/ppermute | solution.py:29
  93.4 7.9 %collective-permute-start = (bf16[128,768]{1,0:T(8,128)(2,1)S(1)}, bf16[128,768]{1,0:T(8,128)(2,1)S(1)}, u32[]{:S(2)}, u32[]{:S(2)}) collective-permute-start(bf16[128,768]{1,0:T(8,128)(2,1)S(1)} %copy.21), channel_id=1, source_target_pairs={{0,32},{32,64},{64,96},{96,128},{128,160},{160,192},{192,224},{224... | collective-permute-start | bytes 589832 | tf_op jit(solution)/shard_map/while/body/eval_jaxpr/ppermute | solution.py:29
  94.3 7.1 %collective-permute-start.1 = (bf16[128,768]{1,0:T(8,128)(2,1)S(1)}, bf16[128,768]{1,0:T(8,128)(2,1)S(1)}, u32[]{:S(2)}, u32[]{:S(2)}) collective-permute-start(bf16[128,768]{1,0:T(8,128)(2,1)S(1)} %copy.22), channel_id=1, source_target_pairs={{32,0},{64,32},{96,64},{128,96},{160,128},{192,160},{224,192},{0,2... | collective-permute-start | bytes 589832 | tf_op jit(solution)/shard_map/while/body/eval_jaxpr/ppermute | solution.py:33
  101.4 11.4 %collective-permute-start.23 = (bf16[1024,768]{1,0:T(8,128)(2,1)S(1)}, bf16[1024,768]{1,0:T(8,128)(2,1)S(1)}, u32[]{:S(2)}, u32[]{:S(2)}) collective-permute-start(bf16[1024,768]{1,0:T(8,128)(2,1)S(1)} %constant_dynamic-update-slice_fusion.7), channel_id=1, source_target_pairs={{0,16},{16,0},{1,17},{17,1},{2,18},{18,2},{3,19},{19,3},{4,20},{20... | collective-permute-start | bytes 4718600 | tf_op jit(solution)/shard_map/ppermute | solution.py:25
  128.5 7.6 %collective-permute-start.26 = (bf16[128,768]{1,0:T(8,128)(2,1)S(1)}, bf16[128,768]{1,0:T(8,128)(2,1)S(1)}, u32[]{:S(2)}, u32[]{:S(2)}) collective-permute-start(bf16[128,768]{1,0:T(8,128)(2,1)S(1)} %get-tuple-element.202.refs_0_), channel_id=1, source_target_pairs={{0,8},{4,12},{8,0},{12,4},{1,9},{5,13},{9,1},{13,5},{2,10},{6,14},... | collective-permute-start | bytes 589832 | tf_op jit(solution)/shard_map/ppermute | solution.py:37
  131.0 9.8 %collective-permute-start.25 = (bf16[128,768]{1,0:T(8,128)(2,1)S(1)}, bf16[128,768]{1,0:T(8,128)(2,1)S(1)}, u32[]{:S(2)}, u32[]{:S(2)}) collective-permute-start(bf16[128,768]{1,0:T(8,128)(2,1)S(1)} %get-tuple-element.202.refs_0_), channel_id=1, source_target_pairs={{0,12},{4,0},{8,4},{12,8},{1,13},{5,1},{9,5},{13,9},{2,14},{6,2},{... | collective-permute-start | bytes 589832 | tf_op jit(solution)/shard_map/ppermute | solution.py:37
  132.9 8.0 %collective-permute-start.24 = (bf16[128,768]{1,0:T(8,128)(2,1)S(1)}, bf16[128,768]{1,0:T(8,128)(2,1)S(1)}, u32[]{:S(2)}, u32[]{:S(2)}) collective-permute-start(bf16[128,768]{1,0:T(8,128)(2,1)S(1)} %get-tuple-element.202.refs_0_), channel_id=1, source_target_pairs={{0,4},{4,8},{8,12},{12,0},{1,5},{5,9},{9,13},{13,1},{2,6},{6,10},{... | collective-permute-start | bytes 589832 | tf_op jit(solution)/shard_map/ppermute | solution.py:37
  141.8 6.9 %collective-permute-start.27 = (bf16[128,768]{1,0:T(8,128)(2,1)S(1)}, bf16[128,768]{1,0:T(8,128)(2,1)S(1)}, u32[]{:S(2)}, u32[]{:S(2)}) collective-permute-start(bf16[128,768]{1,0:T(8,128)(2,1)S(1)} %get-tuple-element.204), channel_id=1, source_target_pairs={{0,2},{1,3},{2,0},{3,1},{4,6},{5,7},{6,4},{7,5},{8,10},{9,11},{10,... | collective-permute-start | bytes 589832 | tf_op jit(solution)/shard_map/ppermute | solution.py:37
  141.9 12.1 %collective-permute-start.28 = (bf16[128,768]{1,0:T(8,128)(2,1)S(1)}, bf16[128,768]{1,0:T(8,128)(2,1)S(1)}, u32[]{:S(2)}, u32[]{:S(2)}) collective-permute-start(bf16[128,768]{1,0:T(8,128)(2,1)S(1)} %get-tuple-element.205), channel_id=1, source_target_pairs={{0,1},{1,2},{2,3},{3,0},{4,5},{5,6},{6,7},{7,4},{8,9},{9,10},{10,1... | collective-permute-start | bytes 589832 | tf_op jit(solution)/shard_map/ppermute | solution.py:37
  142.0 12.0 %collective-permute-start.29 = (bf16[128,768]{1,0:T(8,128)(2,1)S(1)}, bf16[128,768]{1,0:T(8,128)(2,1)S(1)}, u32[]{:S(2)}, u32[]{:S(2)}) collective-permute-start(bf16[128,768]{1,0:T(8,128)(2,1)S(1)} %get-tuple-element.206), channel_id=1, source_target_pairs={{0,3},{1,0},{2,1},{3,2},{4,7},{5,4},{6,5},{7,6},{8,11},{9,8},{10,9... | collective-permute-start | bytes 589832 | tf_op jit(solution)/shard_map/ppermute | solution.py:37
  154.8 7.6 %collective-permute-start.2 = (bf16[128,768]{1,0:T(8,128)(2,1)S(1)}, bf16[128,768]{1,0:T(8,128)(2,1)S(1)}, u32[]{:S(2)}, u32[]{:S(2)}) collective-permute-start(bf16[128,768]{1,0:T(8,128)(2,1)S(1)} %get-tuple-element.316), channel_id=1, source_target_pairs={{0,32},{32,64},{64,96},{96,128},{128,160},{160,192},{192,224},{224... | collective-permute-start | bytes 589832 | tf_op jit(solution)/shard_map/while/body/eval_jaxpr/ppermute | solution.py:29
  155.8 6.6 %collective-permute-start.4 = (bf16[128,768]{1,0:T(8,128)(2,1)S(1)}, bf16[128,768]{1,0:T(8,128)(2,1)S(1)}, u32[]{:S(2)}, u32[]{:S(2)}) collective-permute-start(bf16[128,768]{1,0:T(8,128)(2,1)S(1)} %get-tuple-element.317), channel_id=1, source_target_pairs={{32,0},{64,32},{96,64},{128,96},{160,128},{192,160},{224,192},{0,2... | collective-permute-start | bytes 589832 | tf_op jit(solution)/shard_map/while/body/eval_jaxpr/ppermute | solution.py:33
  162.4 6.3 %collective-permute-start.3 = (bf16[128,768]{1,0:T(8,128)(2,1)S(1)}, bf16[128,768]{1,0:T(8,128)(2,1)S(1)}, u32[]{:S(2)}, u32[]{:S(2)}) collective-permute-start(bf16[128,768]{1,0:T(8,128)(2,1)S(1)} %collective-permute-done.2), channel_id=1, source_target_pairs={{0,32},{32,64},{64,96},{96,128},{128,160},{160,192},{192,224},{224... | collective-permute-start | bytes 589832 | tf_op jit(solution)/shard_map/while/body/eval_jaxpr/ppermute | solution.py:29
  162.4 6.3 %collective-permute-start.5 = (bf16[128,768]{1,0:T(8,128)(2,1)S(1)}, bf16[128,768]{1,0:T(8,128)(2,1)S(1)}, u32[]{:S(2)}, u32[]{:S(2)}) collective-permute-start(bf16[128,768]{1,0:T(8,128)(2,1)S(1)} %collective-permute-done.4), channel_id=1, source_target_pairs={{32,0},{64,32},{96,64},{128,96},{160,128},{192,160},{224,192},{0,2... | collective-permute-start | bytes 589832 | tf_op jit(solution)/shard_map/while/body/eval_jaxpr/ppermute | solution.py:33
  180.2 7.6 %collective-permute-start.30 = (bf16[1024,768]{1,0:T(8,128)(2,1)S(1)}, bf16[1024,768]{1,0:T(8,128)(2,1)S(1)}, u32[]{:S(2)}, u32[]{:S(2)}) collective-permute-start(bf16[1024,768]{1,0:T(8,128)(2,1)S(1)} %constant_dynamic-update-slice_fusion.6.blocks_ref), channel_id=1, source_target_pairs={{0,16},{16,0},{1,17},{17,1},{2,18},{18,2},{3,19},{19,3},{4,20},{20... | collective-permute-start | bytes 4718600 | tf_op jit(solution)/shard_map/ppermute | solution.py:25
  (19 other events, 161.8 us)
